TPU v7x, 32 devices: a whole 2x2x4 slice. The times are simulated.
32 devices in a mesh: dp: 2 (over core), blk: 16 (over z, y, x).
Axes of the slice: x: 2, y: 2, z: 4, core: 2. Of those that a mesh axis runs over, the one named last changes fastest.
Arguments:
- features: bfloat16 [2, 8192, 128], P('dp', 'blk'), may hold values from -6 to 6
- tile_mask: int32 [2, 16], P('dp', 'blk'), may hold values 0 or 1
- w_first: bfloat16 [3456, 128], replicated, may hold values from -0.109375 to 0.109375
- w_second: bfloat16 [3456, 128], replicated, may hold values from -0.109375 to 0.109375
- cotangent: bfloat16 [2, 8192, 128], P('dp', 'blk'), may hold values from -6 to 6
Outputs:
- grad_first: float32 [3456, 128], replicated
- grad_second: float32 [3456, 128], replicated
- feature_grad: bfloat16 [2, 8192, 128], P('dp', 'blk')
All inputs are finite; a program needn't handle non-finite values. No bound on the sum of `tile_mask` on one device may be relied on, other than what follows from the above.
Results may differ from a plain program's by a relative error of at most 0.0039.
Values may be sent and summed in bfloat16 or wider, within the bound.
No kernel may reach another device: no remote copies, remote signals or barrier semaphores. Data moves between devices by JAX's collectives and lax.ppermute only.
A program may use at most 64 MiB of HBM per device.

v0:
```python
import jax
import jax.numpy as jnp
from jax import lax
from jax.sharding import PartitionSpec as P

TILE = 8


unscale = 1.0 / 512.0


def shifted(value, axis, steps):
    count = lax.axis_size(axis)
    leading, last = (max(0, -steps), min(count, count - steps))
    return lax.ppermute(value, axis, [(source, source + steps) for source in range(leading, last)])


def stack_depth(padded, depth_z):
    return jnp.concatenate(
        [padded[:, :, shift_z : shift_z + depth_z, :] for shift_z in range(3)], axis=-1
    )


def arrange(weight):
    width_in = weight.shape[0] // 27
    width_out = weight.shape[1]
    shaped = weight.reshape(width_in, 3, 3, 3, width_out).transpose(1, 2, 3, 0, 4)
    return shaped.reshape(3, 3, 3 * width_in, width_out)


def arrange_flipped(weight):
    width_in = weight.shape[0] // 27
    width_out = weight.shape[1]
    shaped = weight.reshape(width_in, 3, 3, 3, width_out)[:, ::-1, ::-1, ::-1, :].transpose(
        1, 2, 3, 4, 0
    )
    return shaped.reshape(3, 3, 3 * width_out, width_in)


def convolve(padded, kernel):
    size_x = padded.shape[0] - 2
    size_y = padded.shape[1] - 2
    size_z = padded.shape[2] - 2
    stacked = stack_depth(padded, size_z)
    summed = jnp.zeros((size_x * size_y * size_z, kernel.shape[-1]), jnp.float32)
    for step_x in range(3):
        for step_y in range(3):
            slab_rows = stacked[step_x : step_x + size_x, step_y : step_y + size_y].reshape(
                -1, stacked.shape[-1]
            )
            summed = summed + jnp.dot(
                slab_rows, kernel[step_x, step_y], preferred_element_type=jnp.float32
            )
    return summed


def correlate(padded, grads):
    size_x = padded.shape[0] - 2
    size_y = padded.shape[1] - 2
    size_z = padded.shape[2] - 2
    width_in = padded.shape[3]
    width_out = grads.shape[1]
    stacked = stack_depth(padded, size_z)
    blocks = []
    for step_x in range(3):
        for step_y in range(3):
            slab_rows = stacked[step_x : step_x + size_x, step_y : step_y + size_y].reshape(
                -1, stacked.shape[-1]
            )
            blocks.append(
                lax.dot_general(
                    slab_rows, grads, (((0,), (0,)), ((), ())), preferred_element_type=jnp.float32
                )
            )
    joined = jnp.stack(blocks).reshape(3, 3, 3, width_in, width_out).transpose(3, 0, 1, 2, 4)
    return joined.reshape(27 * width_in, width_out)


def sectioned_rims(values, place, extent):
    grown = values
    for axis_pos, stride in ((0, 16), (1, 4), (2, 1)):
        length = grown.shape[axis_pos]
        sides = []
        for toward in (-1, 1):
            if toward == 1:
                border = lax.slice_in_dim(grown, 0, 1, axis=axis_pos)
            else:
                border = lax.slice_in_dim(grown, length - 1, length, axis=axis_pos)
            arrived = shifted(border, "blk", -toward * stride)
            inside = (place[axis_pos] + toward >= 0) & (place[axis_pos] + toward < extent[axis_pos])
            sides.append(jnp.where(inside, arrived, jnp.zeros_like(arrived)))
        grown = jnp.concatenate([sides[0], grown, sides[1]], axis=axis_pos)
    return grown


def surround(values, place, extent):
    return sectioned_rims(values, place, extent)


def reduce_rows(term):
    return lax.psum(term, ("dp", "blk"))


def on_device(features, tile_mask, w_first, w_second, cotangent):
    width = features.shape[2]
    size_x = tile_mask.shape[1] * TILE
    region = (size_x, TILE, TILE, width)
    device_index = lax.axis_index("blk")
    place = (device_index // 16, device_index // 4 % 4, device_index % 4)
    extent = (lax.axis_size("blk") // 16, 4, 4)
    keep_rows = jnp.repeat(tile_mask[0], TILE * TILE * TILE).astype(jnp.bfloat16)[:, None]
    keep_float = keep_rows.astype(jnp.float32)
    inputs = features[0] * keep_rows
    grads_out = cotangent[0] * keep_rows
    pad_in = surround(inputs.reshape(region), place, extent)
    pre_act = convolve(pad_in, arrange(w_first))
    hidden = (jax.nn.silu(pre_act) * keep_float).astype(jnp.bfloat16)
    pad_hidden = surround(hidden.reshape(region), place, extent)
    pad_grads = surround(grads_out.reshape(region), place, extent)
    grad_second = reduce_rows(correlate(pad_hidden, grads_out) * unscale)
    back = convolve(pad_grads, arrange_flipped(w_second))
    sigma = jax.nn.sigmoid(pre_act)
    pre_grad = (back * sigma * (1.0 + pre_act * (1.0 - sigma)) * keep_float).astype(jnp.bfloat16)
    pad_pre = surround(pre_grad.reshape(region), place, extent)
    grad_first = reduce_rows(correlate(pad_in, pre_grad) * unscale)
    summed = grads_out.astype(jnp.float32) + convolve(pad_pre, arrange_flipped(w_first))
    result = (summed * keep_float).astype(jnp.bfloat16)
    return (grad_first, grad_second, result[None])


def solution(mesh):
    in_specs = (P("dp", "blk", None), P("dp", "blk"), P(), P(), P("dp", "blk", None))
    out_specs = (P(), P(), P("dp", "blk", None))
    return jax.shard_map(
        on_device, mesh=mesh, in_specs=in_specs, out_specs=out_specs, check_vma=False
    )
```

profile of v0, /device:TPU:0, one launch (start us, length us, event | category | flops | bytes accessed | tf_op | source)
XLA Modules:
  0.0 267.7 jit_solution(8728321422964012320)
XLA Ops:
  7.9 1.0 broadcast_multiply_fusion.2
  8.9 0.6 slice_bitcast_fusion.59
  9.5 0.6 collective-permute-start.6
  10.1 0.6 slice_bitcast_fusion.61
  10.7 0.6 collective-permute-start
  11.4 0.7 collective-permute-start.1
  12.0 1.3 collective-permute-start.7
  13.3 2.6 reshape.246
  15.9 2.6 rev.7
  18.5 1.1 copy.11
  19.6 1.0 copy.14
  20.8 0.4 reshape.236
  21.3 2.6 rev.6
  23.9 1.0 copy.10
  25.0 4.9 %collective-permute-start.8 = (bf16[10,1,8,128]{3,2,1,0:T(8,128)(2,1)S(1)}, bf16[10,1,8,128]{3,2,1,0:T(8,128)(2,1)S(1)}, u32[]{:S(2)}, u32[]{:S(2)}) collective-permute-start(bf16[10,1,8,128]{3,2,1,0:T(8,128)(2,1)S(1)} %get-tuple-element.53), channel_id=1, source_target_pairs={{0,4},{1,5},{2,6},{3,7},{4,8},{5,9},{6,10},{7,11},{8,12},{9,13},{1... | collective-permute-start | bytes 61448 | tf_op jit(solution)/shard_map/ppermute | solution.py:15
  30.0 1.3 collective-permute-start.9
  31.3 4.5 %collective-permute-start.2 = (bf16[10,1,8,128]{3,2,1,0:T(8,128)(2,1)S(1)}, bf16[10,1,8,128]{3,2,1,0:T(8,128)(2,1)S(1)}, u32[]{:S(2)}, u32[]{:S(2)}) collective-permute-start(bf16[10,1,8,128]{3,2,1,0:T(8,128)(2,1)S(1)} %get-tuple-element.55), channel_id=1, source_target_pairs={{0,4},{1,5},{2,6},{3,7},{4,8},{5,9},{6,10},{7,11},{8,12},{9,13},{1... | collective-permute-start | bytes 61448 | tf_op jit(solution)/shard_map/ppermute | solution.py:15
  35.9 1.3 collective-permute-start.3
  37.3 3.4 %collective-permute-start.10 = (bf16[10,10,1,128]{3,2,1,0:T(2,128)(2,1)S(1)}, bf16[10,10,1,128]{3,2,1,0:T(2,128)(2,1)S(1)}, u32[]{:S(2)}, u32[]{:S(2)}) collective-permute-start(bf16[10,10,1,128]{3,2,1,0:T(2,128)(2,1)S(1)} %get-tuple-element.45), channel_id=1, source_target_pairs={{0,1},{1,2},{2,3},{3,4},{4,5},{5,6},{6,7},{7,8},{8,9},{9,10},{10,1... | collective-permute-start | bytes 76808 | tf_op jit(solution)/shard_map/ppermute | solution.py:15
  40.7 0.8 collective-permute-done.3
  41.6 3.4 %collective-permute-start.4 = (bf16[10,10,1,128]{3,2,1,0:T(2,128)(2,1)S(1)}, bf16[10,10,1,128]{3,2,1,0:T(2,128)(2,1)S(1)}, u32[]{:S(2)}, u32[]{:S(2)}) collective-permute-start(bf16[10,10,1,128]{3,2,1,0:T(2,128)(2,1)S(1)} %get-tuple-element.47), channel_id=1, source_target_pairs={{0,1},{1,2},{2,3},{3,4},{4,5},{5,6},{6,7},{7,8},{8,9},{9,10},{10,1... | collective-permute-start | bytes 76808 | tf_op jit(solution)/shard_map/ppermute | solution.py:15
  45.0 1.3 collective-permute-start.5
  46.3 1.3 collective-permute-start.11
  47.7 5.3 %collective-permute-done.11 = bf16[10,10,1,128]{3,2,1,0:T(2,128)(2,1)S(1)} collective-permute-done((bf16[10,10,1,128]{3,2,1,0:T(2,128)(2,1)S(1)}, bf16[10,10,1,128]{3,2,1,0:T(2,128)(2,1)S(1)}, u32[]{:S(2)}, u32[]{:S(2)}) %collective-permute-start.11) | collective-permute-done | bytes 25632 | tf_op jit(solution)/shard_map/ppermute | solution.py:15
  54.0 0.4 fusion.48
  56.6 0.6 copy-done
  60.0 0.6 slice_bitcast_fusion.55
  60.9 1.3 collective-permute-start.18
  62.2 0.6 collective-permute-start.19
  62.8 0.6 slice_bitcast_fusion.57
  63.4 0.6 collective-permute-start.12
  64.1 0.7 collective-permute-start.13
  64.7 0.3 fusion.21
  65.7 0.3 fusion.18
  66.0 0.3 fusion.17
  67.5 1.2 copy.18
  68.7 2.2 mul.105
  70.9 6.1 %collective-permute-start.20 = (bf16[10,1,8,128]{3,2,1,0:T(8,128)(2,1)S(1)}, bf16[10,1,8,128]{3,2,1,0:T(8,128)(2,1)S(1)}, u32[]{:S(2)}, u32[]{:S(2)}) collective-permute-start(bf16[10,1,8,128]{3,2,1,0:T(8,128)(2,1)S(1)} %get-tuple-element.49), channel_id=1, source_target_pairs={{0,4},{1,5},{2,6},{3,7},{4,8},{5,9},{6,10},{7,11},{8,12},{9,13},{1... | collective-permute-start | bytes 61448 | tf_op jit(solution)/shard_map/ppermute | solution.py:15
  77.1 0.7 pad_maximum_fusion.65
  77.8 3.5 %collective-permute-start.14 = (bf16[10,1,8,128]{3,2,1,0:T(8,128)(2,1)S(1)}, bf16[10,1,8,128]{3,2,1,0:T(8,128)(2,1)S(1)}, u32[]{:S(2)}, u32[]{:S(2)}) collective-permute-start(bf16[10,1,8,128]{3,2,1,0:T(8,128)(2,1)S(1)} %get-tuple-element.51), channel_id=1, source_target_pairs={{0,4},{1,5},{2,6},{3,7},{4,8},{5,9},{6,10},{7,11},{8,12},{9,13},{1... | collective-permute-start | bytes 61448 | tf_op jit(solution)/shard_map/ppermute | solution.py:15
  81.3 1.3 collective-permute-start.15
  82.6 1.5 collective-permute-start.21
  84.1 4.8 %collective-permute-done.21 = bf16[10,1,8,128]{3,2,1,0:T(8,128)(2,1)S(1)} collective-permute-done((bf16[10,1,8,128]{3,2,1,0:T(8,128)(2,1)S(1)}, bf16[10,1,8,128]{3,2,1,0:T(8,128)(2,1)S(1)}, u32[]{:S(2)}, u32[]{:S(2)}) %collective-permute-start.21) | collective-permute-done | bytes 20512 | tf_op jit(solution)/shard_map/ppermute | solution.py:15
  89.0 2.5 collective-permute-start.22
  91.5 1.3 collective-permute-start.23
  92.8 1.1 pad_maximum_fusion.49
  93.9 4.5 %collective-permute-start.16 = (bf16[10,10,1,128]{3,2,1,0:T(2,128)(2,1)S(1)}, bf16[10,10,1,128]{3,2,1,0:T(2,128)(2,1)S(1)}, u32[]{:S(2)}, u32[]{:S(2)}) collective-permute-start(bf16[10,10,1,128]{3,2,1,0:T(2,128)(2,1)S(1)} %get-tuple-element.43), channel_id=1, source_target_pairs={{0,1},{1,2},{2,3},{3,4},{4,5},{5,6},{6,7},{7,8},{8,9},{9,10},{10,1... | collective-permute-start | bytes 76808 | tf_op jit(solution)/shard_map/ppermute | solution.py:15
  98.5 1.3 collective-permute-start.17
  100.2 1.9 fusion.46
  102.1 2.7 %collective-permute-done.17 = bf16[10,10,1,128]{3,2,1,0:T(2,128)(2,1)S(1)} collective-permute-done((bf16[10,10,1,128]{3,2,1,0:T(2,128)(2,1)S(1)}, bf16[10,10,1,128]{3,2,1,0:T(2,128)(2,1)S(1)}, u32[]{:S(2)}, u32[]{:S(2)}) %collective-permute-start.17) | collective-permute-done | bytes 25632 | tf_op jit(solution)/shard_map/ppermute | solution.py:15
  105.2 0.4 fusion.47
  105.9 0.3 fusion.12
  106.8 0.3 fusion.9
  107.5 0.3 fusion.7
  108.6 1.2 copy.17
  109.8 2.2 mul.112
  112.0 1.3 fusion.43
  113.3 0.9 copy-done.9
  115.1 0.4 copy-done.6
  116.4 0.4 copy-done.3
  117.1 0.9 fusion.25
  118.0 138.7 %all-reduce.3.cloned.1.call-done = (f32[3456,128]{1,0:T(8,128)}, f32[3456,128]{1,0:T(8,128)}) async-done(((f32[3456,128]{1,0:T(8,128)}, f32[3456,128]{1,0:T(8,128)}), (f32[3456,128]{1,0:T(8,128)}, f32[3456,128]{1,0:T(8,128)})) %all-reduce.3.cloned.1.call-update) | async-done | bytes 3538960 | tf_op jit(solution)/shard_map/psum | solution.py:101
  256.7 2.9 %copy.38 = f32[3456,128]{1,0:T(8,128)} copy(f32[3456,128]{1,0:T(8,128)} %get-tuple-element.69) | data formatting | bytes 3538944
  259.6 1.2 copy.39
  (118 shorter events, 13.2 us)
Async XLA Ops:
  7.2 249.6 %all-reduce.3.cloned.1.call-start = ((), (), s32[]{:S(2)}) async-start(), calls=%async_computation | async-start | bytes 7077888 | tf_op jit(solution)/shard_map/psum | solution.py:101
  9.5 15.5 %collective-permute-start.6 = (bf16[1,8,8,128]{3,2,1,0:T(8,128)(2,1)}, bf16[1,8,8,128]{3,2,1,0:T(8,128)(2,1)S(1)}, u32[]{:S(2)}, u32[]{:S(2)}) collective-permute-start(bf16[1,8,8,128]{3,2,1,0:T(8,128)(2,1)} %get-tuple-element.61), channel_id=1, source_target_pairs={} | collective-permute-start | bytes 49160 | tf_op jit(solution)/shard_map/ppermute | solution.py:15
  10.7 20.5 %collective-permute-start = (bf16[1,8,8,128]{3,2,1,0:T(8,128)(2,1)}, bf16[1,8,8,128]{3,2,1,0:T(8,128)(2,1)S(1)}, u32[]{:S(2)}, u32[]{:S(2)}) collective-permute-start(bf16[1,8,8,128]{3,2,1,0:T(8,128)(2,1)} %get-tuple-element.63), channel_id=1, source_target_pairs={} | collective-permute-start | bytes 49160 | tf_op jit(solution)/shard_map/ppermute | solution.py:15
  11.4 19.9 %collective-permute-start.1 = (bf16[1,8,8,128]{3,2,1,0:T(8,128)(2,1)}, bf16[1,8,8,128]{3,2,1,0:T(8,128)(2,1)S(1)}, u32[]{:S(2)}, u32[]{:S(2)}) collective-permute-start(bf16[1,8,8,128]{3,2,1,0:T(8,128)(2,1)} %get-tuple-element.64), channel_id=1, source_target_pairs={} | collective-permute-start | bytes 49160 | tf_op jit(solution)/shard_map/ppermute | solution.py:15
  12.0 12.9 %collective-permute-start.7 = (bf16[1,8,8,128]{3,2,1,0:T(8,128)(2,1)}, bf16[1,8,8,128]{3,2,1,0:T(8,128)(2,1)}, u32[]{:S(2)}, u32[]{:S(2)}) collective-permute-start(bf16[1,8,8,128]{3,2,1,0:T(8,128)(2,1)} %get-tuple-element.62), channel_id=1, source_target_pairs={} | collective-permute-start | bytes 49160 | tf_op jit(solution)/shard_map/ppermute | solution.py:15
  19.6 1.2 copy-start.12
  25.0 12.2 %collective-permute-start.8 = (bf16[10,1,8,128]{3,2,1,0:T(8,128)(2,1)S(1)}, bf16[10,1,8,128]{3,2,1,0:T(8,128)(2,1)S(1)}, u32[]{:S(2)}, u32[]{:S(2)}) collective-permute-start(bf16[10,1,8,128]{3,2,1,0:T(8,128)(2,1)S(1)} %get-tuple-element.53), channel_id=1, source_target_pairs={{0,4},{1,5},{2,6},{3,7},{4,8},{5,9},{6,10},{7,11},{8,12},{9,13},{1... | collective-permute-start | bytes 61448 | tf_op jit(solution)/shard_map/ppermute | solution.py:15
  30.0 7.3 %collective-permute-start.9 = (bf16[10,1,8,128]{3,2,1,0:T(8,128)(2,1)S(1)}, bf16[10,1,8,128]{3,2,1,0:T(8,128)(2,1)S(1)}, u32[]{:S(2)}, u32[]{:S(2)}) collective-permute-start(bf16[10,1,8,128]{3,2,1,0:T(8,128)(2,1)S(1)} %get-tuple-element.54), channel_id=1, source_target_pairs={{4,0},{5,1},{6,2},{7,3},{8,4},{9,5},{10,6},{11,7},{12,8},{13,9},{1... | collective-permute-start | bytes 61448 | tf_op jit(solution)/shard_map/ppermute | solution.py:15
  31.3 9.4 %collective-permute-start.2 = (bf16[10,1,8,128]{3,2,1,0:T(8,128)(2,1)S(1)}, bf16[10,1,8,128]{3,2,1,0:T(8,128)(2,1)S(1)}, u32[]{:S(2)}, u32[]{:S(2)}) collective-permute-start(bf16[10,1,8,128]{3,2,1,0:T(8,128)(2,1)S(1)} %get-tuple-element.55), channel_id=1, source_target_pairs={{0,4},{1,5},{2,6},{3,7},{4,8},{5,9},{6,10},{7,11},{8,12},{9,13},{1... | collective-permute-start | bytes 61448 | tf_op jit(solution)/shard_map/ppermute | solution.py:15
  35.9 5.7 %collective-permute-start.3 = (bf16[10,1,8,128]{3,2,1,0:T(8,128)(2,1)S(1)}, bf16[10,1,8,128]{3,2,1,0:T(8,128)(2,1)S(1)}, u32[]{:S(2)}, u32[]{:S(2)}) collective-permute-start(bf16[10,1,8,128]{3,2,1,0:T(8,128)(2,1)S(1)} %get-tuple-element.56), channel_id=1, source_target_pairs={{4,0},{5,1},{6,2},{7,3},{8,4},{9,5},{10,6},{11,7},{12,8},{13,9},{1... | collective-permute-start | bytes 61448 | tf_op jit(solution)/shard_map/ppermute | solution.py:15
  37.3 10.3 %collective-permute-start.10 = (bf16[10,10,1,128]{3,2,1,0:T(2,128)(2,1)S(1)}, bf16[10,10,1,128]{3,2,1,0:T(2,128)(2,1)S(1)}, u32[]{:S(2)}, u32[]{:S(2)}) collective-permute-start(bf16[10,10,1,128]{3,2,1,0:T(2,128)(2,1)S(1)} %get-tuple-element.45), channel_id=1, source_target_pairs={{0,1},{1,2},{2,3},{3,4},{4,5},{5,6},{6,7},{7,8},{8,9},{9,10},{10,1... | collective-permute-start | bytes 76808 | tf_op jit(solution)/shard_map/ppermute | solution.py:15
  41.6 12.0 %collective-permute-start.4 = (bf16[10,10,1,128]{3,2,1,0:T(2,128)(2,1)S(1)}, bf16[10,10,1,128]{3,2,1,0:T(2,128)(2,1)S(1)}, u32[]{:S(2)}, u32[]{:S(2)}) collective-permute-start(bf16[10,10,1,128]{3,2,1,0:T(2,128)(2,1)S(1)} %get-tuple-element.47), channel_id=1, source_target_pairs={{0,1},{1,2},{2,3},{3,4},{4,5},{5,6},{6,7},{7,8},{8,9},{9,10},{10,1... | collective-permute-start | bytes 76808 | tf_op jit(solution)/shard_map/ppermute | solution.py:15
  45.0 8.7 %collective-permute-start.5 = (bf16[10,10,1,128]{3,2,1,0:T(2,128)(2,1)S(1)}, bf16[10,10,1,128]{3,2,1,0:T(2,128)(2,1)S(1)}, u32[]{:S(2)}, u32[]{:S(2)}) collective-permute-start(bf16[10,10,1,128]{3,2,1,0:T(2,128)(2,1)S(1)} %get-tuple-element.48), channel_id=1, source_target_pairs={{1,0},{2,1},{3,2},{4,3},{5,4},{6,5},{7,6},{8,7},{9,8},{10,9},{11,1... | collective-permute-start | bytes 76808 | tf_op jit(solution)/shard_map/ppermute | solution.py:15
  46.3 6.6 %collective-permute-start.11 = (bf16[10,10,1,128]{3,2,1,0:T(2,128)(2,1)S(1)}, bf16[10,10,1,128]{3,2,1,0:T(2,128)(2,1)S(1)}, u32[]{:S(2)}, u32[]{:S(2)}) collective-permute-start(bf16[10,10,1,128]{3,2,1,0:T(2,128)(2,1)S(1)} %get-tuple-element.46), channel_id=1, source_target_pairs={{1,0},{2,1},{3,2},{4,3},{5,4},{6,5},{7,6},{8,7},{9,8},{10,9},{11,1... | collective-permute-start | bytes 76808 | tf_op jit(solution)/shard_map/ppermute | solution.py:15
  56.0 1.2 copy-start
  59.7 7.3 %copy-start.10 = (bf16[512,128]{1,0:T(8,128)(2,1)}, bf16[512,128]{1,0:T(8,128)(2,1)S(1)}, u32[]{:S(2)}) copy-start(bf16[512,128]{1,0:T(8,128)(2,1)S(1)} %get-tuple-element.65) | copy-start | bytes 393220
  60.9 10.0 %collective-permute-start.18 = (bf16[1,8,8,128]{3,2,1,0:T(8,128)(2,1)}, bf16[1,8,8,128]{3,2,1,0:T(8,128)(2,1)}, u32[]{:S(2)}, u32[]{:S(2)}) collective-permute-start(bf16[1,8,8,128]{3,2,1,0:T(8,128)(2,1)} %get-tuple-element.57), channel_id=1, source_target_pairs={} | collective-permute-start | bytes 49160 | tf_op jit(solution)/shard_map/ppermute | solution.py:15
  62.2 8.7 %collective-permute-start.19 = (bf16[1,8,8,128]{3,2,1,0:T(8,128)(2,1)}, bf16[1,8,8,128]{3,2,1,0:T(8,128)(2,1)S(1)}, u32[]{:S(2)}, u32[]{:S(2)}) collective-permute-start(bf16[1,8,8,128]{3,2,1,0:T(8,128)(2,1)} %get-tuple-element.58), channel_id=1, source_target_pairs={} | collective-permute-start | bytes 49160 | tf_op jit(solution)/shard_map/ppermute | solution.py:15
  63.4 13.6 %collective-permute-start.12 = (bf16[1,8,8,128]{3,2,1,0:T(8,128)(2,1)}, bf16[1,8,8,128]{3,2,1,0:T(8,128)(2,1)S(1)}, u32[]{:S(2)}, u32[]{:S(2)}) collective-permute-start(bf16[1,8,8,128]{3,2,1,0:T(8,128)(2,1)} %get-tuple-element.59), channel_id=1, source_target_pairs={} | collective-permute-start | bytes 49160 | tf_op jit(solution)/shard_map/ppermute | solution.py:15
  64.1 13.0 %collective-permute-start.13 = (bf16[1,8,8,128]{3,2,1,0:T(8,128)(2,1)}, bf16[1,8,8,128]{3,2,1,0:T(8,128)(2,1)S(1)}, u32[]{:S(2)}, u32[]{:S(2)}) collective-permute-start(bf16[1,8,8,128]{3,2,1,0:T(8,128)(2,1)} %get-tuple-element.60), channel_id=1, source_target_pairs={} | collective-permute-start | bytes 49160 | tf_op jit(solution)/shard_map/ppermute | solution.py:15
  70.9 13.2 %collective-permute-start.20 = (bf16[10,1,8,128]{3,2,1,0:T(8,128)(2,1)S(1)}, bf16[10,1,8,128]{3,2,1,0:T(8,128)(2,1)S(1)}, u32[]{:S(2)}, u32[]{:S(2)}) collective-permute-start(bf16[10,1,8,128]{3,2,1,0:T(8,128)(2,1)S(1)} %get-tuple-element.49), channel_id=1, source_target_pairs={{0,4},{1,5},{2,6},{3,7},{4,8},{5,9},{6,10},{7,11},{8,12},{9,13},{1... | collective-permute-start | bytes 61448 | tf_op jit(solution)/shard_map/ppermute | solution.py:15
  77.8 15.0 %collective-permute-start.14 = (bf16[10,1,8,128]{3,2,1,0:T(8,128)(2,1)S(1)}, bf16[10,1,8,128]{3,2,1,0:T(8,128)(2,1)S(1)}, u32[]{:S(2)}, u32[]{:S(2)}) collective-permute-start(bf16[10,1,8,128]{3,2,1,0:T(8,128)(2,1)S(1)} %get-tuple-element.51), channel_id=1, source_target_pairs={{0,4},{1,5},{2,6},{3,7},{4,8},{5,9},{6,10},{7,11},{8,12},{9,13},{1... | collective-permute-start | bytes 61448 | tf_op jit(solution)/shard_map/ppermute | solution.py:15
  81.3 11.5 %collective-permute-start.15 = (bf16[10,1,8,128]{3,2,1,0:T(8,128)(2,1)S(1)}, bf16[10,1,8,128]{3,2,1,0:T(8,128)(2,1)S(1)}, u32[]{:S(2)}, u32[]{:S(2)}) collective-permute-start(bf16[10,1,8,128]{3,2,1,0:T(8,128)(2,1)S(1)} %get-tuple-element.52), channel_id=1, source_target_pairs={{4,0},{5,1},{6,2},{7,3},{8,4},{9,5},{10,6},{11,7},{12,8},{13,9},{1... | collective-permute-start | bytes 61448 | tf_op jit(solution)/shard_map/ppermute | solution.py:15
  82.6 6.3 %collective-permute-start.21 = (bf16[10,1,8,128]{3,2,1,0:T(8,128)(2,1)S(1)}, bf16[10,1,8,128]{3,2,1,0:T(8,128)(2,1)S(1)}, u32[]{:S(2)}, u32[]{:S(2)}) collective-permute-start(bf16[10,1,8,128]{3,2,1,0:T(8,128)(2,1)S(1)} %get-tuple-element.50), channel_id=1, source_target_pairs={{4,0},{5,1},{6,2},{7,3},{8,4},{9,5},{10,6},{11,7},{12,8},{13,9},{1... | collective-permute-start | bytes 61448 | tf_op jit(solution)/shard_map/ppermute | solution.py:15
  89.0 10.8 %collective-permute-start.22 = (bf16[10,10,1,128]{3,2,1,0:T(2,128)(2,1)S(1)}, bf16[10,10,1,128]{3,2,1,0:T(2,128)(2,1)S(1)}, u32[]{:S(2)}, u32[]{:S(2)}) collective-permute-start(bf16[10,10,1,128]{3,2,1,0:T(2,128)(2,1)S(1)} %get-tuple-element.41), channel_id=1, source_target_pairs={{0,1},{1,2},{2,3},{3,4},{4,5},{5,6},{6,7},{7,8},{8,9},{9,10},{10,1... | collective-permute-start | bytes 76808 | tf_op jit(solution)/shard_map/ppermute | solution.py:15
  91.5 8.4 %collective-permute-start.23 = (bf16[10,10,1,128]{3,2,1,0:T(2,128)(2,1)S(1)}, bf16[10,10,1,128]{3,2,1,0:T(2,128)(2,1)S(1)}, u32[]{:S(2)}, u32[]{:S(2)}) collective-permute-start(bf16[10,10,1,128]{3,2,1,0:T(2,128)(2,1)S(1)} %get-tuple-element.42), channel_id=1, source_target_pairs={{1,0},{2,1},{3,2},{4,3},{5,4},{6,5},{7,6},{8,7},{9,8},{10,9},{11,1... | collective-permute-start | bytes 76808 | tf_op jit(solution)/shard_map/ppermute | solution.py:15
  93.9 8.1 %collective-permute-start.16 = (bf16[10,10,1,128]{3,2,1,0:T(2,128)(2,1)S(1)}, bf16[10,10,1,128]{3,2,1,0:T(2,128)(2,1)S(1)}, u32[]{:S(2)}, u32[]{:S(2)}) collective-permute-start(bf16[10,10,1,128]{3,2,1,0:T(2,128)(2,1)S(1)} %get-tuple-element.43), channel_id=1, source_target_pairs={{0,1},{1,2},{2,3},{3,4},{4,5},{5,6},{6,7},{7,8},{8,9},{9,10},{10,1... | collective-permute-start | bytes 76808 | tf_op jit(solution)/shard_map/ppermute | solution.py:15
  98.5 6.4 %collective-permute-start.17 = (bf16[10,10,1,128]{3,2,1,0:T(2,128)(2,1)S(1)}, bf16[10,10,1,128]{3,2,1,0:T(2,128)(2,1)S(1)}, u32[]{:S(2)}, u32[]{:S(2)}) collective-permute-start(bf16[10,10,1,128]{3,2,1,0:T(2,128)(2,1)S(1)} %get-tuple-element.44), channel_id=1, source_target_pairs={{1,0},{2,1},{3,2},{4,3},{5,4},{6,5},{7,6},{8,7},{9,8},{10,9},{11,1... | collective-permute-start | bytes 76808 | tf_op jit(solution)/shard_map/ppermute | solution.py:15
  100.2 4.7 %copy-start.11 = (bf16[512,128]{1,0:T(8,128)(2,1)S(1)}, bf16[512,128]{1,0:T(8,128)(2,1)}, u32[]{:S(2)}) copy-start(bf16[512,128]{1,0:T(8,128)(2,1)} %copy-done.10) | copy-start | bytes 393220
  113.2 1.0 copy-start.9
  113.3 1.2 copy-start.8
  113.3 1.5 copy-start.7
  114.5 1.0 copy-start.6
  114.8 1.0 copy-start.5
  115.1 1.1 copy-start.4
  115.8 1.0 copy-start.3
  116.1 1.0 copy-start.2
  256.7 2.9 %copy-start.1 = (f32[3456,128]{1,0:T(8,128)S(1)}, f32[3456,128]{1,0:T(8,128)}, u32[]{:S(2)}) copy-start(f32[3456,128]{1,0:T(8,128)} %get-tuple-element.70) | copy-start | bytes 5308420
Sparse Core Ops, SparseCore 0:
  113.4 143.2 all-reduce.2
where the time goes:
time: 269 us; the launch traced here: 268 us
  waiting for transfers between devices  152 us (57%)
  starting transfers between devices  49.8 us (19%)
  local copies, waits for them, and re-layouts  30.4 us (11%)
  between operations  15.8 us (6%)
  matrix products  14.4 us (5%)
  other arithmetic  4.92 us (2%)
    psum x1, waiting for transfers between devices, reduce_rows(): return lax.psum(term, ('dp', 'blk'))  139 us
    ppermute x24, starting transfers between devices, shifted(): lax.ppermute(value, axis, [(source, source + steps) for source in range(l...  49.8 us
    ppermute x24, waiting for transfers between devices, shifted(): lax.ppermute(value, axis, [(source, source + steps) for source in range(l...  13.7 us
    dot_general x27, matrix products, convolve(): jnp.dot(slab_rows, kernel[step_x, step_y], preferred_element_type=jnp.flo...  8.8 us
    unnamed x28, local copies, waits for them, and re-layouts  6.81 us
    dot_general x18, matrix products, correlate(): lax.dot_general(slab_rows, grads, (((0,), (0,)), ((), ())), preferred_ele...  5.62 us
  transfers between devices with their start and end apart: 25, of which 5 were waited for; matrix products, arithmetic and copies ran while one was open for 10% of the time, Pallas kernels for 0%

commit v1 on v0

v1 whole, which is shorter than its diff:
```python
import functools

import jax
import jax.numpy as jnp
from jax import lax
from jax.experimental import pallas as pl
from jax.experimental.pallas import tpu as pltpu
from jax.sharding import PartitionSpec as P

TILE = 8
FACE = TILE * TILE
RIM = TILE + 2
GROWN = TILE + 4
IN_PITCH = 160
PITCH = 128
OUT_PITCH = 96
TAPS = 27
INNER = 4
BF = jnp.bfloat16
F32 = jnp.float32
unscale = 1.0 / 512.0
LIMIT = 48 * 2**20

VM = pl.BlockSpec(memory_space=pltpu.VMEM)
SM = pl.BlockSpec(memory_space=pltpu.SMEM)
AWAY = pl.BlockSpec(memory_space=pl.ANY)


def call(body, outs, ins, scratch=(), smem=(), away=(), flops=0):
    specs = [SM if i in smem else AWAY if i in away else VM for i in range(len(ins))]
    moved = sum(a.size * a.dtype.itemsize for a in list(ins) + list(outs))
    return pl.pallas_call(
        body,
        out_shape=list(outs),
        in_specs=specs,
        out_specs=[VM] * len(outs),
        scratch_shapes=list(scratch),
        compiler_params=pltpu.CompilerParams(vmem_limit_bytes=LIMIT),
        cost_estimate=pl.CostEstimate(flops=flops, bytes_accessed=moved, transcendentals=0),
    )(*ins)


def shape(dims, kind):
    return jax.ShapeDtypeStruct(dims, kind)


def parity(stride):
    return lax.axis_index("blk") // stride % 2


def pack_rows(planes, tile_of, mask_rows, mask, feat, cot, inp, grads, marks, even, odd, raw, sem):
    copies = [
        pltpu.make_async_copy(src, raw.at[at], sem.at[at]) for at, src in enumerate((feat, cot))
    ]
    for copy in copies:
        copy.start()
    row = lax.broadcasted_iota(jnp.int32, (mask_rows, 128), 0)
    filled = jnp.zeros((mask_rows, 128), F32)
    kept_of = [mask[0, tile_of(e)].astype(F32) for e in range(planes)]
    for e in range(planes):
        filled = jnp.where(row == e, kept_of[e], filled)
    filled = filled.astype(BF)
    marks[...] = filled
    even[4 * planes * TILE :, :] = filled
    odd[4 * planes * TILE :, :] = filled
    for copy in copies:
        copy.wait()
    side = parity(4)
    for at, dst in enumerate((inp, grads)):
        for e in range(planes):
            kept = (raw[at, e * FACE : (e + 1) * FACE, :].astype(F32) * kept_of[e]).astype(BF)
            dst[e * FACE : (e + 1) * FACE, :] = kept

    def faces(lo, hi):
        for at, src in enumerate((inp, grads)):
            for e in range(planes):
                to = slice((at * planes + e) * 2 * TILE, (at * planes + e + 1) * 2 * TILE)
                lo[to, :] = src[e * FACE : e * FACE + 2 * TILE, :]
                hi[to, :] = src[(e + 1) * FACE - 2 * TILE : (e + 1) * FACE, :]

    @pl.when(side == 0)
    def _():
        faces(odd, even)

    @pl.when(side == 1)
    def _():
        faces(even, odd)


def pack_depth(
    planes, mask_rows, inp, grads, marks, y_even, y_odd, even, odd, tall_in, tall_g, marks3, grown
):
    strip = planes * GROWN
    line = GROWN * TILE
    tail = 4 * planes * TILE

    def middle(from_lo, from_hi):
        for at, (src, dst) in enumerate(((inp, tall_in), (grads, tall_g))):
            for e in range(planes):
                base = (at * planes + e) * 2 * TILE
                top = e * line
                dst[top : top + 2 * TILE, :] = from_lo[base : base + 2 * TILE, :]
                dst[top + 2 * TILE : top + 2 * TILE + FACE, :] = src[e * FACE : (e + 1) * FACE, :]
                dst[top + 2 * TILE + FACE : top + line, :] = from_hi[base : base + 2 * TILE, :]
        for at, rows in enumerate((from_lo[tail:, :], marks[...], from_hi[tail:, :])):
            marks3[at * mask_rows : (at + 1) * mask_rows, :] = rows

    @pl.when(parity(4) == 0)
    def _():
        middle(y_odd, y_even)

    @pl.when(parity(4) == 1)
    def _():
        middle(y_even, y_odd)

    for ref in (even, odd):
        ref[4 * strip :, :] = marks3[...]
    side = parity(1)
    for at, src in enumerate((tall_in, tall_g)):
        grown[...] = src[...].astype(F32)

        def faces(lo, hi, at=at):
            for k in range(2):
                to = slice((at * 2 + k) * strip, (at * 2 + k + 1) * strip)
                lo[to, :] = grown[pl.ds(k, strip, stride=TILE), :].astype(BF)
                hi[to, :] = grown[pl.ds(TILE - 2 + k, strip, stride=TILE), :].astype(BF)

        @pl.when(side == 0)
        def _():
            faces(odd, even)

        @pl.when(side == 1)
        def _():
            faces(even, odd)


def lay_weights(first, second, first_rows, first_wide, second_wide, raw, wide, sem):
    copies = [
        pltpu.make_async_copy(src, raw.at[at], sem.at[at])
        for at, src in enumerate((first, second))
    ]
    for copy in copies:
        copy.start()
    for at, (rows, columns) in enumerate(((first_rows, first_wide), (None, second_wide))):
        copies[at].wait()
        wide[...] = raw[at].astype(F32)
        for tap in range(TAPS):
            block = wide[pl.ds(tap, 128, stride=TAPS), :].astype(BF)
            if rows is not None:
                rows[tap * 128 : (tap + 1) * 128, :] = block
            columns[:, tap * 128 : (tap + 1) * 128] = block


def dot(a, b):
    return lax.dot_general(a, b, (((1,), (0,)), ((), ())), preferred_element_type=F32)


def dot_t(a, b):
    return lax.dot_general(a, b, (((1,), (1,)), ((), ())), preferred_element_type=F32)


def spread(planes, first_plane, at, tall, z_even, z_odd, grid):
    grid[...] = jnp.zeros_like(grid)
    strip = planes * GROWN
    for e in range(planes):
        top = (first_plane + e) * IN_PITCH + 2
        for y in range(0, GROWN, 2):
            pair = tall[(e * GROWN + y) * TILE : (e * GROWN + y + 2) * TILE, :].astype(F32)
            grid[top + y * GROWN : top + y * GROWN + TILE, :] = pair[:TILE]
            grid[top + (y + 1) * GROWN : top + (y + 1) * GROWN + TILE, :] = pair[TILE:]
    swapped = parity(1) == 0
    for k in range(2):
        rows = slice((at * 2 + k) * strip, (at * 2 + k + 1) * strip)
        one, two = z_even[rows, :].astype(F32), z_odd[rows, :].astype(F32)
        left, right = jnp.where(swapped, two, one), jnp.where(swapped, one, two)
        for e in range(planes):
            top = (first_plane + e) * IN_PITCH
            grid[pl.ds(top + k, GROWN, stride=GROWN), :] = left[e * GROWN : (e + 1) * GROWN]
            grid[pl.ds(top + 2 + TILE + k, GROWN, stride=GROWN), :] = right[
                e * GROWN : (e + 1) * GROWN
            ]


def stack(n_planes, grid, stacked, flipped):
    for p in range(n_planes):
        for b in range(3):
            for c in range(3):
                step = (2 - b) * GROWN + 2 - c if flipped else b * GROWN + c
                at = (3 * b + c) * 128
                stacked[p * PITCH : (p + 1) * PITCH, at : at + 128] = grid[
                    p * IN_PITCH + step : p * IN_PITCH + step + PITCH, :
                ].astype(BF)


def own_lines(grid, at):
    return jnp.concatenate([grid[at : at + TILE, :], grid[at + GROWN : at + GROWN + TILE, :]], 0)


def stack_own(n_planes, pitch, skip, grid, stacked):
    for p in range(n_planes):
        for y in range(0, TILE, 2):
            to = p * FACE + y * TILE
            for b in range(3):
                for c in range(3):
                    at = p * pitch + (y + skip + 2 - b) * GROWN + skip + 2 - c
                    stacked[to : to + 2 * TILE, (3 * b + c) * 128 : (3 * b + c + 1) * 128] = (
                        own_lines(grid, at).astype(BF)
                    )


def emit(core, at, value, kept, sent):
    half = value.shape[0] // 2
    columns = slice(at, at + value.shape[1])

    @pl.when(core == 0)
    def _():
        kept[:, columns] = value[:half]
        sent[:, columns] = value[half:].astype(BF)

    @pl.when(core == 1)
    def _():
        kept[:, columns] = value[half:]
        sent[:, columns] = value[:half].astype(BF)


def marked(planes, mask_rows, marks3, z_even, z_odd):
    tail = 4 * planes * GROWN
    swapped = parity(1) == 0

    def mark(by, bz, e):
        at = by * mask_rows + e
        if bz == 1:
            return marks3[at : at + 1, :].astype(F32)
        one = z_even[tail + at : tail + at + 1, :].astype(F32)
        two = z_odd[tail + at : tail + at + 1, :].astype(F32)
        return jnp.where(swapped, two, one) if bz == 0 else jnp.where(swapped, one, two)

    return mark


def spans(rows, ends):
    row = lax.broadcasted_iota(jnp.int32, (rows, 128), 0)
    line = row // GROWN
    depth = row - line * GROWN
    return [(line >= lo) & (line <= hi) for lo, hi in ends], [
        (depth >= lo) & (depth <= hi) for lo, hi in ends
    ]


def pad_terms(*refs):
    used = TAPS * 128
    for ref in refs:
        if ref.shape[1] > used:
            ref[:, used:] = jnp.zeros((ref.shape[0], ref.shape[1] - used), ref.dtype)


def forward(
    planes, deep, mask_rows,
    tall_in, tall_g, marks3, z_even, z_odd, w1_rows,
    kept, sent, act, grid_g,
    grid_in, st_in, st_own, hidden,
):
    core = lax.axis_index("dp")
    size_x = planes - 4 * deep
    n_in = size_x + 2 + 2 * deep
    n_out = size_x + 2 * deep
    third = 9 * 128
    spread(planes, 1 - deep, 0, tall_in, z_even, z_odd, grid_in)
    stack(n_in, grid_in, st_in, False)
    rows = n_out * PITCH
    total = dot(st_in[0:rows, :], w1_rows[0:third, :])
    for a in (1, 2):
        total = total + dot(
            st_in[a * PITCH : a * PITCH + rows, :], w1_rows[a * third : (a + 1) * third, :]
        )
    act[...] = total
    spread(planes, 1 - deep, 1, tall_g, z_even, z_odd, grid_g)
    stack_own(n_in, IN_PITCH, 1, grid_g, st_own)
    for p in range(size_x):
        at = mask_rows + p + 2 * deep
        keep = marks3[at : at + 1, :].astype(F32)
        for y in range(0, TILE, 2):
            pre = own_lines(act, (p + deep) * PITCH + (y + 1) * GROWN + 1)
            to = p * FACE + y * TILE
            hidden[to : to + 2 * TILE, :] = pre * jax.nn.sigmoid(pre) * keep
    hid_t = hidden[...].T.astype(BF)
    rows = size_x * FACE
    for a in range(3):
        at = (deep + 2 - a) * FACE
        part = dot(hid_t, st_own[at : at + rows, :]) * unscale
        emit(core, a * third, part, kept, sent)
    pad_terms(kept, sent)


def backward(
    planes, deep, mask_rows, tile_of,
    grid_g, act, inp, marks3, z_even, z_odd, w2_wide,
    kept, sent, st_own,
    st_g, pg,
):
    core = lax.axis_index("dp")
    size_x = planes - 4 * deep
    n_in = size_x + 2 + 2 * deep
    n_out = size_x + 2 * deep
    third = 9 * 128
    mark = marked(planes, mask_rows, marks3, z_even, z_odd)
    in_line, in_depth = spans(PITCH, ((0, 0), (1, TILE), (RIM - 1, RIM - 1)))
    stack(n_in, grid_g, st_g, True)
    rows = n_out * PITCH
    back = jnp.zeros((rows, 128), F32)
    for a in range(3):
        at = (2 - a) * PITCH
        back = back + dot_t(st_g[at : at + rows, :], w2_wide[:, a * third : (a + 1) * third])
    if not deep:
        for at in (0, (size_x + 1) * PITCH):
            pg[at : at + PITCH, :] = jnp.zeros((PITCH, 128), F32)
    tile, keep = None, None
    for p in range(n_out):
        if tile_of(p + deep) != tile:
            tile, keep = tile_of(p + deep), jnp.zeros((PITCH, 128), F32)
            for by in range(3):
                for bz in range(3):
                    keep = jnp.where(in_line[by] & in_depth[bz], mark(by, bz, p + deep), keep)
        pre = act[p * PITCH : (p + 1) * PITCH, :]
        sigma = jax.nn.sigmoid(pre)
        grad = back[p * PITCH : (p + 1) * PITCH] * sigma * (1.0 + pre * (1.0 - sigma))
        at = (p + 1 - deep) * PITCH
        pg[at : at + PITCH, :] = (grad * keep).astype(BF).astype(F32)
    stack_own(size_x + 2, PITCH, 0, pg, st_own)
    rows = size_x * FACE
    top = 2 * deep * FACE
    in_t = inp[top : top + rows, :].astype(F32).T.astype(BF)
    for a in range(3):
        at = (2 - a) * FACE
        part = dot(in_t, st_own[at : at + rows, :]) * unscale
        emit(core, a * third, part, kept, sent)
    pad_terms(kept, sent)


def last(planes, deep, mask_rows, st_own, grads, marks3, w1_wide, result):
    size_x = planes - 4 * deep
    third = 9 * 128
    rows = size_x * FACE
    total = jnp.zeros((rows, 128), F32)
    for a in range(3):
        at = (2 - a) * FACE
        total = total + dot_t(st_own[at : at + rows, :], w1_wide[:, a * third : (a + 1) * third])
    for p in range(size_x):
        e = p + 2 * deep
        m = marks3[mask_rows + e : mask_rows + e + 1, :].astype(F32)
        own = slice(p * FACE, (p + 1) * FACE)
        summed = (grads[e * FACE : (e + 1) * FACE, :].astype(F32) + total[own]) * m
        result[own, :] = summed.astype(BF)


def swap(value, axis, bits):
    count = lax.axis_size(axis)
    return lax.ppermute(value, axis, [(source, source ^ bits) for source in range(count)])


def split_rows(parts, kept, got, own, *sent):
    me = lax.axis_index("blk") % INNER
    rows = own.shape[0]
    for k in range(parts):
        at = pl.ds(pl.multiple_of((me ^ k) * rows, rows), rows)
        value = kept[at, :] + got[at, :].astype(F32)
        if k == 0:
            own[...] = value
        else:
            sent[k - 1][...] = value.astype(BF)


def split_columns(parts, *refs):
    kept, got, own, sent = refs[0], refs[1:INNER], refs[INNER], refs[INNER + 1 :]
    me = lax.axis_index("blk") // INNER
    columns = own.shape[1]
    for k in range(parts):
        at = pl.ds(pl.multiple_of((me ^ k) * columns, 128), columns)
        value = kept[:, at]
        for ref in got:
            value = value + ref[:, at].astype(F32)
        if k == 0:
            own[...] = value
        else:
            sent[k - 1][...] = value.astype(BF)


def add_pair(one, two, out):
    out[...] = (one[...].astype(F32) + two[...].astype(F32)).astype(BF)


def add_all(parts, *refs):
    value = refs[0][...]
    for ref in refs[1:parts]:
        value = value + ref[...].astype(F32)
    refs[parts][...] = value.astype(BF)


def join_columns(parts, *refs):
    me = lax.axis_index("blk") // INNER
    out = refs[parts]
    columns = refs[0].shape[1]
    for k in range(parts):
        out[:, pl.ds(pl.multiple_of((me ^ k) * columns, 128), columns)] = refs[k][...]


def join_rows(parts, *refs):
    me = lax.axis_index("blk") % INNER
    out = refs[parts]
    rows = refs[0].shape[0]
    for k in range(parts):
        out[pl.ds(pl.multiple_of((me ^ k) * rows, rows), rows), :] = refs[k][...]


def finish(own, other, out):
    core = lax.axis_index("dp")
    half = own.shape[0]

    def write(low, high):
        for at, ref in ((0, low), (half, high)):
            for tap in range(TAPS):
                out[pl.ds(at * TAPS + tap, half, stride=TAPS), :] = ref[
                    :, tap * 128 : (tap + 1) * 128
                ].astype(F32)

    @pl.when(core == 0)
    def _():
        write(own, other)

    @pl.when(core == 1)
    def _():
        write(other, own)


def after(value, *others):
    return lax.optimization_barrier((value, *others))[0]


def near(values):
    return [swap(v, "blk", k + 1) for k, v in enumerate(values)]


def far(values):
    return [swap(v, "blk", INNER * (k + 1)) for k, v in enumerate(values)]


def split_stage(kept, got):
    half, columns = kept.shape
    rows = half // INNER
    return call(
        functools.partial(split_rows, INNER),
        [shape((rows, columns), F32)] + [shape((rows, columns), BF)] * (INNER - 1),
        [kept, got],
    )


def sum_stage(own, gots):
    parts = len(gots) + 1
    return call(functools.partial(add_all, parts), [shape(own.shape, BF)], [own] + gots)[0]


def pair_stage(value, got):
    return call(add_pair, [shape(value.shape, BF)], [value, got])[0]


def back_stage(wide, gots):
    rows, columns = wide.shape
    return call(
        functools.partial(join_rows, INNER), [shape((rows * INNER, columns), BF)], [wide] + gots
    )[0]


def wide_sum(own, gots):
    outer = lax.axis_size("blk") // INNER
    rows, columns = own.shape
    part = columns // outer
    own, *send = call(
        functools.partial(split_columns, outer),
        [shape((rows, part), F32)] + [shape((rows, part), BF)] * (outer - 1),
        [own] + gots,
    )
    done = sum_stage(own, far(send))
    return call(
        functools.partial(join_columns, outer),
        [shape((rows, columns), BF)],
        [done] + far([done] * (outer - 1)),
    )[0]


def finished(mine, other):
    return call(finish, [shape((2 * mine.shape[0] * TAPS, 128), F32)], [mine, other])[0]


def reduce_rest(own, send):
    outer = lax.axis_size("blk") // INNER
    gots = near(send)
    if outer > 4:
        value = wide_sum(own, gots)
    else:
        value = sum_stage(own, gots)
        step = 1
        while step < outer:
            value = pair_stage(value, swap(value, "blk", INNER * step))
            step *= 2
    mine = back_stage(value, near([value] * (INNER - 1)))
    return finished(mine, swap(mine, "dp", 1))


def on_device(features, tile_mask, w_first, w_second, cotangent):
    width = features.shape[2]
    tiles = tile_mask.shape[1]
    size_x = tiles * TILE
    count = lax.axis_size("blk")
    deep = 1 if count // 16 > 1 else 0
    planes = size_x + 4 * deep
    feat, cot, mask = features[0], cotangent[0], tile_mask

    def along(value, stride, extent, toward):
        pairs = [
            (s, s + toward * stride)
            for s in range(count)
            if 0 <= s // stride % extent + toward < extent
        ]
        return lax.ppermute(value, "blk", pairs)

    if deep:
        wide_mask = jnp.broadcast_to(
            jnp.repeat(tile_mask[0], TILE)[:, None], (size_x, width)
        ).astype(BF)
        keep = jnp.repeat(wide_mask, FACE, axis=0)
        feat, cot = feat * keep, cot * keep
        slab = 2 * FACE
        up = jnp.concatenate([feat[-slab:], cot[-slab:], wide_mask[-16:]], 0)
        down = jnp.concatenate([feat[:slab], cot[:slab], wide_mask[:16]], 0)
        before = along(up, 16, count // 16, 1)
        behind = along(down, 16, count // 16, -1)
        feat = jnp.concatenate([before[:slab], feat, behind[:slab]], 0)
        cot = jnp.concatenate([before[slab : 2 * slab], cot, behind[slab : 2 * slab]], 0)
        ends = [v[2 * slab : 2 * slab + 1, :1].astype(jnp.int32) for v in (before, behind)]
        mask = jnp.concatenate([ends[0], tile_mask, ends[1]], 1)

    def tile_of(e):
        if not deep:
            return e // TILE
        return (e + TILE - 2) // TILE

    def beside(one, two, stride, extent):
        pairs = ([], [])
        for s in range(count):
            place = s // stride % extent
            if place + 1 < extent:
                pairs[place % 2].extend([(s, s + stride), (s + stride, s)])
        return lax.ppermute(one, "blk", pairs[0]), lax.ppermute(two, "blk", pairs[1])

    mask_rows = -(-planes // 16) * 16
    side = 4 * planes * TILE + mask_rows
    cells = planes * FACE
    inp, grads, marks, even, odd = call(
        functools.partial(pack_rows, planes, tile_of, mask_rows),
        [shape((cells, width), BF)] * 2
        + [shape((mask_rows, width), BF)]
        + [shape((side, width), BF)] * 2,
        [mask, feat, cot],
        scratch=[pltpu.VMEM((2, cells, width), BF), pltpu.SemaphoreType.DMA((2,))],
        smem=(0,),
        away=(1, 2),
    )
    y_even, y_odd = beside(even, odd, 4, 4)
    w1_rows, w1_wide, w2_wide = call(
        lay_weights,
        [shape((TAPS * width, width), BF)] + [shape((width, TAPS * width), BF)] * 2,
        [w_first, w_second],
        scratch=[
            pltpu.VMEM((2, TAPS * width, width), BF),
            pltpu.VMEM((TAPS * width, width), F32),
            pltpu.SemaphoreType.DMA((2,)),
        ],
        away=(0, 1),
    )
    edge = 4 * planes * GROWN + 3 * mask_rows
    even, odd, tall_in, tall_g, marks3 = call(
        functools.partial(pack_depth, planes, mask_rows),
        [shape((edge, width), BF)] * 2
        + [shape((planes * GROWN * TILE, width), BF)] * 2
        + [shape((3 * mask_rows, width), BF)],
        [inp, grads, marks, y_even, y_odd],
        scratch=[pltpu.VMEM((planes * GROWN * TILE, width), F32)],
    )
    z_even, z_odd = beside(even, odd, 1, 4)
    outer = count // INNER
    columns = TAPS * width if outer <= 4 else -(-TAPS // outer) * outer * width
    n_in = size_x + 2 + 2 * deep
    n_out = size_x + 2 * deep
    half = width // 2
    work = 2 * size_x * FACE * TAPS * width * width
    terms = [shape((half, columns), F32), shape((half, columns), BF)]
    kept_a, sent_a, act, grid_g = call(
        functools.partial(forward, planes, deep, mask_rows),
        terms + [shape((n_out * PITCH, width), F32), shape((n_in * IN_PITCH, width), F32)],
        [tall_in, tall_g, marks3, z_even, z_odd, w1_rows],
        scratch=[
            pltpu.VMEM((n_in * IN_PITCH, width), F32),
            pltpu.VMEM((n_in * PITCH, 9 * width), BF),
            pltpu.VMEM((n_in * FACE, 9 * width), BF),
            pltpu.VMEM((size_x * FACE, width), F32),
        ],
        flops=2 * work,
    )
    own_a, *send_a = split_stage(kept_a, swap(sent_a, "dp", 1))
    act = after(act, own_a)
    kept_b, sent_b, st_own = call(
        functools.partial(backward, planes, deep, mask_rows, tile_of),
        terms + [shape(((size_x + 2) * FACE, 9 * width), BF)],
        [grid_g, act, inp, marks3, z_even, z_odd, w2_wide],
        scratch=[
            pltpu.VMEM((n_in * PITCH, 9 * width), BF),
            pltpu.VMEM(((size_x + 2) * PITCH, width), F32),
        ],
        flops=2 * work,
    )
    own_b, *send_b = split_stage(kept_b, swap(sent_b, "dp", 1))
    st_own = after(st_own, own_b)
    (result,) = call(
        functools.partial(last, planes, deep, mask_rows),
        [shape((size_x * FACE, width), BF)],
        [st_own, grads, marks3, w1_wide],
        flops=work,
    )
    grad_second = reduce_rest(own_a, send_a)
    grad_first = reduce_rest(own_b, send_b)
    return (grad_first, grad_second, result[None])


def solution(mesh):
    in_specs = (P("dp", "blk", None), P("dp", "blk"), P(), P(), P("dp", "blk", None))
    out_specs = (P(), P(), P("dp", "blk", None))
    return jax.shard_map(
        on_device, mesh=mesh, in_specs=in_specs, out_specs=out_specs, check_vma=False
    )
```

time: 269 us -> 73.5 us (0.27)
  waiting for transfers between devices: 152 us -> 14.2 us
  local copies, waits for them, and re-layouts: 30.4 us -> 4.13 us
  Pallas kernels: 0 us -> 14.8 us
  matrix products: 14.4 us -> 0 us
  between operations: 15.8 us -> 1.45 us
  starting transfers between devices: 49.8 us -> 38.6 us
  other arithmetic: 4.92 us -> 0 us
    psum x1 -> x0, waiting for transfers between devices: 139 us -> none  [reduce_rows(): return lax.psum(term, ('dp', 'blk'))]
    pallas_call x0 -> x18, Pallas kernels: none -> 14.8 us  [call(): pl.pallas_call(body, out_shape=list(outs), in_specs=specs, out_specs=[VM]...]
    dot_general x45 -> x0, matrix products: 14.4 us -> none  [the longest x27 8.8 us: convolve(): jnp.dot(slab_rows, kernel[step_x, step_y], preferred_element_type=jnp.flo...]
    ppermute x24, starting transfers between devices: 49.8 us -> 38.6 us  [the longest x20 32.2 us: swap(): lax.ppermute(value, axis, [(source, source ^ bits) for source in range(co...]
    mul x4 -> x0, local copies, waits for them, and re-layouts: 6.81 us -> none  [the longest x2 3.4 us: on_device(): grad_second = reduce_rows(correlate(pad_hidden, grads_out) * unscale)]
    slice x8 -> x0, local copies, waits for them, and re-layouts: 5.33 us -> none  [the longest x3 2.53 us: convolve(): stacked[step_x:step_x + size_x, step_y:step_y + size_y]]
    rev x2 -> x0, local copies, waits for them, and re-layouts: 5.18 us -> none  [arrange_flipped(): weight.reshape(width_in, 3, 3, 3, width_out)[:, ::-1, ::-1, ::-1, :]]
    transpose x3 -> x0, local copies, waits for them, and re-layouts: 3.18 us -> none  [the longest x2 2.06 us: arrange_flipped(): weight.reshape(width_in, 3, 3, 3, width_out)[:, ::-1, ::-1, ::-1, :]]
  transfers between devices with their start and end apart: 25 -> 24, of which waited for: 5 -> 10; matrix products, arithmetic and copies ran while one was open for 10% -> 0% of each run, Pallas kernels for 0% -> 6%
where the time goes in v1:
time: 73.5 us; the launch traced here: 73.2 us
  starting transfers between devices  38.6 us (53%)
  Pallas kernels  14.8 us (20%)
  waiting for transfers between devices  14.2 us (19%)
  local copies, waits for them, and re-layouts  4.13 us (6%)
  between operations  1.45 us (2%)
    ppermute x20, starting transfers between devices, swap(): lax.ppermute(value, axis, [(source, source ^ bits) for source in range(co...  32.2 us
    pallas_call x18, Pallas kernels, call(): pl.pallas_call(body, out_shape=list(outs), in_specs=specs, out_specs=[VM]...  14.8 us
    ppermute x20, waiting for transfers between devices, swap(): lax.ppermute(value, axis, [(source, source ^ bits) for source in range(co...  12.6 us
    ppermute x2, starting transfers between devices, beside(): lax.ppermute(one, 'blk', pairs[0])  5.09 us
    unnamed x8, local copies, waits for them, and re-layouts  4.13 us
    ppermute x2, waiting for transfers between devices, beside(): lax.ppermute(one, 'blk', pairs[0])  1.63 us
  transfers between devices with their start and end apart: 24, of which 10 were waited for; matrix products, arithmetic and copies ran while one was open for 0% of the time, Pallas kernels for 6%

profile of v1, /device:TPU:0, one launch (start us, length us, event | category | flops | bytes accessed | tf_op | source)
XLA Modules:
  0.0 73.2 jit_solution(18402806407041202498)
XLA Ops:
  1.3 0.9 %copy-done.2 = bf16[1,512,128]{2,1,0:T(8,128)(2,1)S(1)} copy-done((bf16[1,512,128]{2,1,0:T(8,128)(2,1)S(1)}, bf16[1,512,128]{2,1,0:T(8,128)(2,1)}, u32[]{:S(2)}) %copy-start.2) | copy-done | bytes 131096
  2.2 0.9 %copy-done.3 = bf16[1,512,128]{2,1,0:T(8,128)(2,1)S(1)} copy-done((bf16[1,512,128]{2,1,0:T(8,128)(2,1)S(1)}, bf16[1,512,128]{2,1,0:T(8,128)(2,1)}, u32[]{:S(2)}) %copy-start.3) | copy-done | bytes 131096
  3.1 0.4 shard_map.76
  3.5 3.1 %collective-permute-start = (bf16[272,128]{1,0:T(8,128)(2,1)S(1)}, bf16[272,128]{1,0:T(8,128)(2,1)S(1)}, u32[]{:S(2)}, u32[]{:S(2)}) collective-permute-start(bf16[272,128]{1,0:T(8,128)(2,1)S(1)} %get-tuple-element.36), channel_id=1, source_target_pairs={{0,4},{4,0},{1,5},{5,1},{2,6},{6,2},{3,7},{7,3},{8,12},{12,8},{9,1... | collective-permute-start | bytes 208904 | tf_op jit(solution)/shard_map/ppermute | solution.py:553
  6.6 0.7 collective-permute-start.1
  7.2 1.6 %collective-permute-done.y_even = bf16[272,128]{1,0:T(8,128)(2,1)S(1)} collective-permute-done((bf16[272,128]{1,0:T(8,128)(2,1)S(1)}, bf16[272,128]{1,0:T(8,128)(2,1)S(1)}, u32[]{:S(2)}, u32[]{:S(2)}) %collective-permute-start) | collective-permute-done | bytes 69664 | tf_op jit(solution)/shard_map/ppermute | solution.py:553
  8.9 0.0 collective-permute-done.1.y_odd
  8.9 0.2 shard_map.77
  9.0 2.0 %collective-permute-start.2 = (bf16[432,128]{1,0:T(8,128)(2,1)S(1)}, bf16[432,128]{1,0:T(8,128)(2,1)S(1)}, u32[]{:S(2)}, u32[]{:S(2)}) collective-permute-start(bf16[432,128]{1,0:T(8,128)(2,1)S(1)} %get-tuple-element.41), channel_id=1, source_target_pairs={{0,1},{1,0},{2,3},{3,2},{4,5},{5,4},{6,7},{7,6},{8,9},{9,8},{10,11... | collective-permute-start | bytes 331784 | tf_op jit(solution)/shard_map/ppermute | solution.py:553
  11.0 0.7 collective-permute-start.3
  11.7 0.0 copy-start
  11.7 1.2 %copy-done = bf16[3456,128]{1,0:T(8,128)(2,1)S(1)} copy-done((bf16[3456,128]{1,0:T(8,128)(2,1)S(1)}, bf16[3456,128]{1,0:T(8,128)(2,1)}, u32[]{:S(2)}) %copy-start) | copy-done | bytes 884760
  12.9 1.2 %copy-done.1 = bf16[3456,128]{1,0:T(8,128)(2,1)S(1)} copy-done((bf16[3456,128]{1,0:T(8,128)(2,1)S(1)}, bf16[3456,128]{1,0:T(8,128)(2,1)}, u32[]{:S(2)}) %copy-start.1) | copy-done | bytes 884760
  14.0 0.9 %shard_map.78 = (bf16[3456,128]{1,0:T(8,128)(2,1)S(1)}, bf16[128,3456]{1,0:T(8,128)(2,1)S(1)}, bf16[128,3456]{1,0:T(8,128)(2,1)S(1)}) custom-call(bf16[3456,128]{1,0:T(8,128)(2,1)S(1)} %copy-done, bf16[3456,128]{1,0:T(8,128)(2,1)S(1)} %copy-done.1), custom_call_target="tpu_custom_call" | custom-call | bytes 4423680 | tf_op jit(solution)/shard_map/pallas_call | solution.py:32
  15.0 0.0 collective-permute-done.2.z_even
  15.0 0.0 collective-permute-done.3.z_odd
  15.0 4.2 %shard_map.79 = (f32[64,3456]{1,0:T(8,128)S(1)}, bf16[64,3456]{1,0:T(8,128)(2,1)S(1)}, f32[1024,128]{1,0:T(8,128)S(1)}, f32[1600,128]{1,0:T(8,128)S(1)}) custom-call(bf16[768,128]{1,0:T(8,128)(2,1)S(1)} %get-tuple-element.38.tall_in, bf16[768,128]{1,0:T(8,128)(2,1)S(1)} %get-tuple-element.39.tall_g, bf16[48,128]{1,0:T(8,128)(2,1)S(1)} %get-tuple-element.40.marks3, ...), custom_call_target="tpu_custom_call" | custom-call | flops 905969664 | bytes 4182016 | tf_op jit(solution)/shard_map/pallas_call | solution.py:32
  19.2 0.1 collective-permute-start.4
  19.3 1.8 %collective-permute-done.4.got = bf16[64,3456]{1,0:T(8,128)(2,1)S(1)} collective-permute-done((bf16[64,3456]{1,0:T(8,128)(2,1)S(1)}, bf16[64,3456]{1,0:T(8,128)(2,1)S(1)}, u32[]{:S(2)}, u32[]{:S(2)}) %collective-permute-start.4) | collective-permute-done | bytes 442400 | tf_op jit(solution)/shard_map/ppermute | solution.py:358
  21.1 0.1 shard_map.80
  21.2 4.2 %shard_map.81 = (f32[64,3456]{1,0:T(8,128)S(1)}, bf16[64,3456]{1,0:T(8,128)(2,1)S(1)}, bf16[640,1152]{1,0:T(8,128)(2,1)S(1)}) custom-call(f32[1600,128]{1,0:T(8,128)S(1)} %get-tuple-element.44.grid_g, f32[1024,128]{1,0:T(8,128)S(1)} %get-tuple-element.49.act, bf16[512,128]{1,0:T(8,128)(2,1)S(1)} %get-tuple-element.33.inp, ...), custom_call_target="tpu_custom_call" | custom-call | flops 905969664 | bytes 5394432 | tf_op jit(solution)/shard_map/pallas_call | solution.py:32
  25.4 0.2 collective-permute-start.5
  25.6 4.2 %collective-permute-start.15 = (bf16[16,3456]{1,0:T(8,128)(2,1)S(1)}, bf16[16,3456]{1,0:T(8,128)(2,1)S(1)}, u32[]{:S(2)}, u32[]{:S(2)}) collective-permute-start(bf16[16,3456]{1,0:T(8,128)(2,1)S(1)} %get-tuple-element.57), channel_id=1, source_target_pairs={{0,1},{1,0},{2,3},{3,2},{4,5},{5,4},{6,7},{7,6},{8,9},{9,8},{10,11... | collective-permute-start | bytes 331784 | tf_op jit(solution)/shard_map/ppermute | solution.py:358
  29.8 0.9 %collective-permute-start.16 = (bf16[16,3456]{1,0:T(8,128)(2,1)S(1)}, bf16[16,3456]{1,0:T(8,128)(2,1)S(1)}, u32[]{:S(2)}, u32[]{:S(2)}) collective-permute-start(bf16[16,3456]{1,0:T(8,128)(2,1)S(1)} %get-tuple-element.58), channel_id=1, source_target_pairs={{0,2},{1,3},{2,0},{3,1},{4,6},{5,7},{6,4},{7,5},{8,10},{9,11},{10,... | collective-permute-start | bytes 331784 | tf_op jit(solution)/shard_map/ppermute | solution.py:358
  30.7 1.5 %collective-permute-start.17 = (bf16[16,3456]{1,0:T(8,128)(2,1)S(1)}, bf16[16,3456]{1,0:T(8,128)(2,1)S(1)}, u32[]{:S(2)}, u32[]{:S(2)}) collective-permute-start(bf16[16,3456]{1,0:T(8,128)(2,1)S(1)} %get-tuple-element.59), channel_id=1, source_target_pairs={{0,3},{1,2},{2,1},{3,0},{4,7},{5,6},{6,5},{7,4},{8,11},{9,10},{10,... | collective-permute-start | bytes 331784 | tf_op jit(solution)/shard_map/ppermute | solution.py:358
  32.2 0.0 collective-permute-done.5.got
  32.2 0.1 shard_map.82
  32.3 1.2 %collective-permute-start.6 = (bf16[16,3456]{1,0:T(8,128)(2,1)S(1)}, bf16[16,3456]{1,0:T(8,128)(2,1)S(1)}, u32[]{:S(2)}, u32[]{:S(2)}) collective-permute-start(bf16[16,3456]{1,0:T(8,128)(2,1)S(1)} %get-tuple-element.54), channel_id=1, source_target_pairs={{0,1},{1,0},{2,3},{3,2},{4,5},{5,4},{6,7},{7,6},{8,9},{9,8},{10,11... | collective-permute-start | bytes 331784 | tf_op jit(solution)/shard_map/ppermute | solution.py:358
  33.5 0.9 %collective-permute-start.7 = (bf16[16,3456]{1,0:T(8,128)(2,1)S(1)}, bf16[16,3456]{1,0:T(8,128)(2,1)S(1)}, u32[]{:S(2)}, u32[]{:S(2)}) collective-permute-start(bf16[16,3456]{1,0:T(8,128)(2,1)S(1)} %get-tuple-element.55), channel_id=1, source_target_pairs={{0,2},{1,3},{2,0},{3,1},{4,6},{5,7},{6,4},{7,5},{8,10},{9,11},{10,... | collective-permute-start | bytes 331784 | tf_op jit(solution)/shard_map/ppermute | solution.py:358
  34.4 0.0 collective-permute-done.15.refs_1_
  34.4 1.4 %collective-permute-start.8 = (bf16[16,3456]{1,0:T(8,128)(2,1)S(1)}, bf16[16,3456]{1,0:T(8,128)(2,1)S(1)}, u32[]{:S(2)}, u32[]{:S(2)}) collective-permute-start(bf16[16,3456]{1,0:T(8,128)(2,1)S(1)} %get-tuple-element.56), channel_id=1, source_target_pairs={{0,3},{1,2},{2,1},{3,0},{4,7},{5,6},{6,5},{7,4},{8,11},{9,10},{10,... | collective-permute-start | bytes 331784 | tf_op jit(solution)/shard_map/ppermute | solution.py:358
  35.8 0.4 collective-permute-done.16.refs_2_
  36.2 2.2 %collective-permute-done.17.refs_3_ = bf16[16,3456]{1,0:T(8,128)(2,1)S(1)} collective-permute-done((bf16[16,3456]{1,0:T(8,128)(2,1)S(1)}, bf16[16,3456]{1,0:T(8,128)(2,1)S(1)}, u32[]{:S(2)}, u32[]{:S(2)}) %collective-permute-start.17) | collective-permute-done | bytes 110624 | tf_op jit(solution)/shard_map/ppermute | solution.py:358
  38.4 0.1 shard_map.88.one
  38.5 4.7 %collective-permute-start.18 = (bf16[16,3456]{1,0:T(8,128)(2,1)S(1)}, bf16[16,3456]{1,0:T(8,128)(2,1)S(1)}, u32[]{:S(2)}, u32[]{:S(2)}) collective-permute-start(bf16[16,3456]{1,0:T(8,128)(2,1)S(1)} %shard_map.88.one), channel_id=1, source_target_pairs={{0,4},{1,5},{2,6},{3,7},{4,0},{5,1},{6,2},{7,3},{8,12},{9,13},{10,... | collective-permute-start | bytes 331784 | tf_op jit(solution)/shard_map/ppermute | solution.py:358
  43.1 0.0 collective-permute-done.6.refs_1_
  43.1 0.0 collective-permute-done.7.refs_2_
  43.1 0.0 collective-permute-done.8.refs_3_
  43.1 0.1 shard_map.83.one
  43.2 4.1 %collective-permute-start.9 = (bf16[16,3456]{1,0:T(8,128)(2,1)S(1)}, bf16[16,3456]{1,0:T(8,128)(2,1)S(1)}, u32[]{:S(2)}, u32[]{:S(2)}) collective-permute-start(bf16[16,3456]{1,0:T(8,128)(2,1)S(1)} %shard_map.83.one), channel_id=1, source_target_pairs={{0,4},{1,5},{2,6},{3,7},{4,0},{5,1},{6,2},{7,3},{8,12},{9,13},{10,... | collective-permute-start | bytes 331784 | tf_op jit(solution)/shard_map/ppermute | solution.py:358
  47.3 0.0 collective-permute-done.18.two
  47.4 2.1 %collective-permute-start.19 = (bf16[16,3456]{1,0:T(8,128)(2,1)S(1)}, bf16[16,3456]{1,0:T(8,128)(2,1)S(1)}, u32[]{:S(2)}, u32[]{:S(2)}) collective-permute-start(bf16[16,3456]{1,0:T(8,128)(2,1)S(1)} %shard_map.89.one), channel_id=1, source_target_pairs={{0,8},{1,9},{2,10},{3,11},{4,12},{5,13},{6,14},{7,15},{8,0},{9,1},... | collective-permute-start | bytes 331784 | tf_op jit(solution)/shard_map/ppermute | solution.py:358
  49.4 1.2 %collective-permute-done.9.two = bf16[16,3456]{1,0:T(8,128)(2,1)S(1)} collective-permute-done((bf16[16,3456]{1,0:T(8,128)(2,1)S(1)}, bf16[16,3456]{1,0:T(8,128)(2,1)S(1)}, u32[]{:S(2)}, u32[]{:S(2)}) %collective-permute-start.9) | collective-permute-done | bytes 110624 | tf_op jit(solution)/shard_map/ppermute | solution.py:358
  50.6 4.2 %collective-permute-start.10 = (bf16[16,3456]{1,0:T(8,128)(2,1)S(1)}, bf16[16,3456]{1,0:T(8,128)(2,1)S(1)}, u32[]{:S(2)}, u32[]{:S(2)}) collective-permute-start(bf16[16,3456]{1,0:T(8,128)(2,1)S(1)} %shard_map.84.one), channel_id=1, source_target_pairs={{0,8},{1,9},{2,10},{3,11},{4,12},{5,13},{6,14},{7,15},{8,0},{9,1},... | collective-permute-start | bytes 331784 | tf_op jit(solution)/shard_map/ppermute | solution.py:358
  54.9 2.1 %collective-permute-done.19.two = bf16[16,3456]{1,0:T(8,128)(2,1)S(1)} collective-permute-done((bf16[16,3456]{1,0:T(8,128)(2,1)S(1)}, bf16[16,3456]{1,0:T(8,128)(2,1)S(1)}, u32[]{:S(2)}, u32[]{:S(2)}) %collective-permute-start.19) | collective-permute-done | bytes 110624 | tf_op jit(solution)/shard_map/ppermute | solution.py:358
  57.0 1.6 %collective-permute-start.22 = (bf16[16,3456]{1,0:T(8,128)(2,1)S(1)}, bf16[16,3456]{1,0:T(8,128)(2,1)S(1)}, u32[]{:S(2)}, u32[]{:S(2)}) collective-permute-start(bf16[16,3456]{1,0:T(8,128)(2,1)S(1)} %shard_map.90.refs_0_), channel_id=1, source_target_pairs={{0,3},{1,2},{2,1},{3,0},{4,7},{5,6},{6,5},{7,4},{8,11},{9,10},{10,... | collective-permute-start | bytes 331784 | tf_op jit(solution)/shard_map/ppermute | solution.py:358
  58.6 0.0 collective-permute-start.21
  58.6 1.9 %collective-permute-start.20 = (bf16[16,3456]{1,0:T(8,128)(2,1)S(1)}, bf16[16,3456]{1,0:T(8,128)(2,1)S(1)}, u32[]{:S(2)}, u32[]{:S(2)}) collective-permute-start(bf16[16,3456]{1,0:T(8,128)(2,1)S(1)} %shard_map.90.refs_0_), channel_id=1, source_target_pairs={{0,1},{1,0},{2,3},{3,2},{4,5},{5,4},{6,7},{7,6},{8,9},{9,8},{10,11... | collective-permute-start | bytes 331784 | tf_op jit(solution)/shard_map/ppermute | solution.py:358
  60.6 0.0 collective-permute-done.10.two
  60.6 1.6 %collective-permute-start.13 = (bf16[16,3456]{1,0:T(8,128)(2,1)S(1)}, bf16[16,3456]{1,0:T(8,128)(2,1)S(1)}, u32[]{:S(2)}, u32[]{:S(2)}) collective-permute-start(bf16[16,3456]{1,0:T(8,128)(2,1)S(1)} %shard_map.85.refs_0_), channel_id=1, source_target_pairs={{0,3},{1,2},{2,1},{3,0},{4,7},{5,6},{6,5},{7,4},{8,11},{9,10},{10,... | collective-permute-start | bytes 331784 | tf_op jit(solution)/shard_map/ppermute | solution.py:358
  62.2 0.0 collective-permute-start.12
  62.2 0.6 collective-permute-done.22.refs_3_
  62.8 1.4 %collective-permute-start.11 = (bf16[16,3456]{1,0:T(8,128)(2,1)S(1)}, bf16[16,3456]{1,0:T(8,128)(2,1)S(1)}, u32[]{:S(2)}, u32[]{:S(2)}) collective-permute-start(bf16[16,3456]{1,0:T(8,128)(2,1)S(1)} %shard_map.85.refs_0_), channel_id=1, source_target_pairs={{0,1},{1,0},{2,3},{3,2},{4,5},{5,4},{6,7},{7,6},{8,9},{9,8},{10,11... | collective-permute-start | bytes 331784 | tf_op jit(solution)/shard_map/ppermute | solution.py:358
  64.2 2.1 %collective-permute-done.21.refs_2_ = bf16[16,3456]{1,0:T(8,128)(2,1)S(1)} collective-permute-done((bf16[16,3456]{1,0:T(8,128)(2,1)S(1)}, bf16[16,3456]{1,0:T(8,128)(2,1)S(1)}, u32[]{:S(2)}, u32[]{:S(2)}) %collective-permute-start.21) | collective-permute-done | bytes 110624 | tf_op jit(solution)/shard_map/ppermute | solution.py:358
  66.3 0.0 collective-permute-done.20.refs_1_
  66.3 0.1 collective-permute-start.23
  66.4 1.3 %collective-permute-done.13.refs_3_ = bf16[16,3456]{1,0:T(8,128)(2,1)S(1)} collective-permute-done((bf16[16,3456]{1,0:T(8,128)(2,1)S(1)}, bf16[16,3456]{1,0:T(8,128)(2,1)S(1)}, u32[]{:S(2)}, u32[]{:S(2)}) %collective-permute-start.13) | collective-permute-done | bytes 110624 | tf_op jit(solution)/shard_map/ppermute | solution.py:358
  67.7 0.9 %collective-permute-done.12.refs_2_ = bf16[16,3456]{1,0:T(8,128)(2,1)S(1)} collective-permute-done((bf16[16,3456]{1,0:T(8,128)(2,1)S(1)}, bf16[16,3456]{1,0:T(8,128)(2,1)S(1)}, u32[]{:S(2)}, u32[]{:S(2)}) %collective-permute-start.12) | collective-permute-done | bytes 110624 | tf_op jit(solution)/shard_map/ppermute | solution.py:358
  68.7 0.0 collective-permute-done.11.refs_1_
  68.7 0.1 collective-permute-start.14
  68.8 1.7 %shard_map.93 = bf16[512,128]{1,0:T(8,128)(2,1)} custom-call(bf16[640,1152]{1,0:T(8,128)(2,1)S(1)} %get-tuple-element.61.st_own, bf16[512,128]{1,0:T(8,128)(2,1)S(1)} %get-tuple-element.34.grads, bf16[48,128]{1,0:T(8,128)(2,1)S(1)} %get-tuple-element.40.marks3, bf16[128,3456]{1,0:T(8,128)(2,1)S(1)} %get-tuple-element.62.w1_wide), custom_call_target="tpu_custom_call" | custom-call | flops 452984832 | bytes 2633728 | tf_op jit(solution)/shard_map/pallas_call | solution.py:32
  70.5 0.0 collective-permute-done.23.other
  70.5 1.3 %shard_map.92 = f32[3456,128]{1,0:T(8,128)} custom-call(bf16[64,3456]{1,0:T(8,128)(2,1)S(1)} %shard_map.91.own, bf16[64,3456]{1,0:T(8,128)(2,1)S(1)} %collective-permute-done.23.other), custom_call_target="tpu_custom_call" | custom-call | bytes 2654208 | tf_op jit(solution)/shard_map/pallas_call | solution.py:32
  71.9 1.3 %shard_map.87 = f32[3456,128]{1,0:T(8,128)} custom-call(bf16[64,3456]{1,0:T(8,128)(2,1)S(1)} %shard_map.86.own, bf16[64,3456]{1,0:T(8,128)(2,1)S(1)} %collective-permute-done.14.other), custom_call_target="tpu_custom_call" | custom-call | bytes 2654208 | tf_op jit(solution)/shard_map/pallas_call | solution.py:32
  (10 shorter events, 0.2 us)
Async XLA Ops:
  1.3 0.9 %copy-start.2 = (bf16[1,512,128]{2,1,0:T(8,128)(2,1)S(1)}, bf16[1,512,128]{2,1,0:T(8,128)(2,1)}, u32[]{:S(2)}) copy-start(bf16[1,512,128]{2,1,0:T(8,128)(2,1)} %param.5) | copy-start | bytes 393220
  2.2 0.9 %copy-start.3 = (bf16[1,512,128]{2,1,0:T(8,128)(2,1)S(1)}, bf16[1,512,128]{2,1,0:T(8,128)(2,1)}, u32[]{:S(2)}) copy-start(bf16[1,512,128]{2,1,0:T(8,128)(2,1)} %param.9) | copy-start | bytes 393220
  3.5 5.4 %collective-permute-start = (bf16[272,128]{1,0:T(8,128)(2,1)S(1)}, bf16[272,128]{1,0:T(8,128)(2,1)S(1)}, u32[]{:S(2)}, u32[]{:S(2)}) collective-permute-start(bf16[272,128]{1,0:T(8,128)(2,1)S(1)} %get-tuple-element.36), channel_id=1, source_target_pairs={{0,4},{4,0},{1,5},{5,1},{2,6},{6,2},{3,7},{7,3},{8,12},{12,8},{9,1... | collective-permute-start | bytes 208904 | tf_op jit(solution)/shard_map/ppermute | solution.py:553
  6.6 2.3 %collective-permute-start.1 = (bf16[272,128]{1,0:T(8,128)(2,1)S(1)}, bf16[272,128]{1,0:T(8,128)(2,1)S(1)}, u32[]{:S(2)}, u32[]{:S(2)}) collective-permute-start(bf16[272,128]{1,0:T(8,128)(2,1)S(1)} %get-tuple-element.37), channel_id=1, source_target_pairs={{4,8},{8,4},{5,9},{9,5},{6,10},{10,6},{7,11},{11,7},{20,24},{24,20... | collective-permute-start | bytes 208904 | tf_op jit(solution)/shard_map/ppermute | solution.py:553
  9.0 5.9 %collective-permute-start.2 = (bf16[432,128]{1,0:T(8,128)(2,1)S(1)}, bf16[432,128]{1,0:T(8,128)(2,1)S(1)}, u32[]{:S(2)}, u32[]{:S(2)}) collective-permute-start(bf16[432,128]{1,0:T(8,128)(2,1)S(1)} %get-tuple-element.41), channel_id=1, source_target_pairs={{0,1},{1,0},{2,3},{3,2},{4,5},{5,4},{6,7},{7,6},{8,9},{9,8},{10,11... | collective-permute-start | bytes 331784 | tf_op jit(solution)/shard_map/ppermute | solution.py:553
  11.0 4.0 %collective-permute-start.3 = (bf16[432,128]{1,0:T(8,128)(2,1)S(1)}, bf16[432,128]{1,0:T(8,128)(2,1)S(1)}, u32[]{:S(2)}, u32[]{:S(2)}) collective-permute-start(bf16[432,128]{1,0:T(8,128)(2,1)S(1)} %get-tuple-element.42), channel_id=1, source_target_pairs={{1,2},{2,1},{5,6},{6,5},{9,10},{10,9},{13,14},{14,13},{17,18},{18,... | collective-permute-start | bytes 331784 | tf_op jit(solution)/shard_map/ppermute | solution.py:553
  11.7 1.2 %copy-start = (bf16[3456,128]{1,0:T(8,128)(2,1)S(1)}, bf16[3456,128]{1,0:T(8,128)(2,1)}, u32[]{:S(2)}) copy-start(bf16[3456,128]{1,0:T(8,128)(2,1)} %first.1) | copy-start | bytes 2654212
  12.9 1.2 %copy-start.1 = (bf16[3456,128]{1,0:T(8,128)(2,1)S(1)}, bf16[3456,128]{1,0:T(8,128)(2,1)}, u32[]{:S(2)}) copy-start(bf16[3456,128]{1,0:T(8,128)(2,1)} %second.1) | copy-start | bytes 2654212
  19.2 1.9 %collective-permute-start.4 = (bf16[64,3456]{1,0:T(8,128)(2,1)S(1)}, bf16[64,3456]{1,0:T(8,128)(2,1)S(1)}, u32[]{:S(2)}, u32[]{:S(2)}) collective-permute-start(bf16[64,3456]{1,0:T(8,128)(2,1)S(1)} %get-tuple-element.47), channel_id=1, source_target_pairs={{0,16},{16,0},{1,17},{17,1},{2,18},{18,2},{3,19},{19,3},{4,20},{20... | collective-permute-start | bytes 1327112 | tf_op jit(solution)/shard_map/ppermute | solution.py:358
  25.4 6.8 %collective-permute-start.5 = (bf16[64,3456]{1,0:T(8,128)(2,1)S(1)}, bf16[64,3456]{1,0:T(8,128)(2,1)S(1)}, u32[]{:S(2)}, u32[]{:S(2)}) collective-permute-start(bf16[64,3456]{1,0:T(8,128)(2,1)S(1)} %get-tuple-element.52), channel_id=1, source_target_pairs={{0,16},{16,0},{1,17},{17,1},{2,18},{18,2},{3,19},{19,3},{4,20},{20... | collective-permute-start | bytes 1327112 | tf_op jit(solution)/shard_map/ppermute | solution.py:358
  25.6 8.8 %collective-permute-start.15 = (bf16[16,3456]{1,0:T(8,128)(2,1)S(1)}, bf16[16,3456]{1,0:T(8,128)(2,1)S(1)}, u32[]{:S(2)}, u32[]{:S(2)}) collective-permute-start(bf16[16,3456]{1,0:T(8,128)(2,1)S(1)} %get-tuple-element.57), channel_id=1, source_target_pairs={{0,1},{1,0},{2,3},{3,2},{4,5},{5,4},{6,7},{7,6},{8,9},{9,8},{10,11... | collective-permute-start | bytes 331784 | tf_op jit(solution)/shard_map/ppermute | solution.py:358
  29.8 6.4 %collective-permute-start.16 = (bf16[16,3456]{1,0:T(8,128)(2,1)S(1)}, bf16[16,3456]{1,0:T(8,128)(2,1)S(1)}, u32[]{:S(2)}, u32[]{:S(2)}) collective-permute-start(bf16[16,3456]{1,0:T(8,128)(2,1)S(1)} %get-tuple-element.58), channel_id=1, source_target_pairs={{0,2},{1,3},{2,0},{3,1},{4,6},{5,7},{6,4},{7,5},{8,10},{9,11},{10,... | collective-permute-start | bytes 331784 | tf_op jit(solution)/shard_map/ppermute | solution.py:358
  30.7 7.7 %collective-permute-start.17 = (bf16[16,3456]{1,0:T(8,128)(2,1)S(1)}, bf16[16,3456]{1,0:T(8,128)(2,1)S(1)}, u32[]{:S(2)}, u32[]{:S(2)}) collective-permute-start(bf16[16,3456]{1,0:T(8,128)(2,1)S(1)} %get-tuple-element.59), channel_id=1, source_target_pairs={{0,3},{1,2},{2,1},{3,0},{4,7},{5,6},{6,5},{7,4},{8,11},{9,10},{10,... | collective-permute-start | bytes 331784 | tf_op jit(solution)/shard_map/ppermute | solution.py:358
  32.3 10.9 %collective-permute-start.6 = (bf16[16,3456]{1,0:T(8,128)(2,1)S(1)}, bf16[16,3456]{1,0:T(8,128)(2,1)S(1)}, u32[]{:S(2)}, u32[]{:S(2)}) collective-permute-start(bf16[16,3456]{1,0:T(8,128)(2,1)S(1)} %get-tuple-element.54), channel_id=1, source_target_pairs={{0,1},{1,0},{2,3},{3,2},{4,5},{5,4},{6,7},{7,6},{8,9},{9,8},{10,11... | collective-permute-start | bytes 331784 | tf_op jit(solution)/shard_map/ppermute | solution.py:358
  33.5 9.7 %collective-permute-start.7 = (bf16[16,3456]{1,0:T(8,128)(2,1)S(1)}, bf16[16,3456]{1,0:T(8,128)(2,1)S(1)}, u32[]{:S(2)}, u32[]{:S(2)}) collective-permute-start(bf16[16,3456]{1,0:T(8,128)(2,1)S(1)} %get-tuple-element.55), channel_id=1, source_target_pairs={{0,2},{1,3},{2,0},{3,1},{4,6},{5,7},{6,4},{7,5},{8,10},{9,11},{10,... | collective-permute-start | bytes 331784 | tf_op jit(solution)/shard_map/ppermute | solution.py:358
  34.4 8.7 %collective-permute-start.8 = (bf16[16,3456]{1,0:T(8,128)(2,1)S(1)}, bf16[16,3456]{1,0:T(8,128)(2,1)S(1)}, u32[]{:S(2)}, u32[]{:S(2)}) collective-permute-start(bf16[16,3456]{1,0:T(8,128)(2,1)S(1)} %get-tuple-element.56), channel_id=1, source_target_pairs={{0,3},{1,2},{2,1},{3,0},{4,7},{5,6},{6,5},{7,4},{8,11},{9,10},{10,... | collective-permute-start | bytes 331784 | tf_op jit(solution)/shard_map/ppermute | solution.py:358
  38.5 8.8 %collective-permute-start.18 = (bf16[16,3456]{1,0:T(8,128)(2,1)S(1)}, bf16[16,3456]{1,0:T(8,128)(2,1)S(1)}, u32[]{:S(2)}, u32[]{:S(2)}) collective-permute-start(bf16[16,3456]{1,0:T(8,128)(2,1)S(1)} %shard_map.88.one), channel_id=1, source_target_pairs={{0,4},{1,5},{2,6},{3,7},{4,0},{5,1},{6,2},{7,3},{8,12},{9,13},{10,... | collective-permute-start | bytes 331784 | tf_op jit(solution)/shard_map/ppermute | solution.py:358
  43.2 7.4 %collective-permute-start.9 = (bf16[16,3456]{1,0:T(8,128)(2,1)S(1)}, bf16[16,3456]{1,0:T(8,128)(2,1)S(1)}, u32[]{:S(2)}, u32[]{:S(2)}) collective-permute-start(bf16[16,3456]{1,0:T(8,128)(2,1)S(1)} %shard_map.83.one), channel_id=1, source_target_pairs={{0,4},{1,5},{2,6},{3,7},{4,0},{5,1},{6,2},{7,3},{8,12},{9,13},{10,... | collective-permute-start | bytes 331784 | tf_op jit(solution)/shard_map/ppermute | solution.py:358
  47.4 9.6 %collective-permute-start.19 = (bf16[16,3456]{1,0:T(8,128)(2,1)S(1)}, bf16[16,3456]{1,0:T(8,128)(2,1)S(1)}, u32[]{:S(2)}, u32[]{:S(2)}) collective-permute-start(bf16[16,3456]{1,0:T(8,128)(2,1)S(1)} %shard_map.89.one), channel_id=1, source_target_pairs={{0,8},{1,9},{2,10},{3,11},{4,12},{5,13},{6,14},{7,15},{8,0},{9,1},... | collective-permute-start | bytes 331784 | tf_op jit(solution)/shard_map/ppermute | solution.py:358
  50.6 10.0 %collective-permute-start.10 = (bf16[16,3456]{1,0:T(8,128)(2,1)S(1)}, bf16[16,3456]{1,0:T(8,128)(2,1)S(1)}, u32[]{:S(2)}, u32[]{:S(2)}) collective-permute-start(bf16[16,3456]{1,0:T(8,128)(2,1)S(1)} %shard_map.84.one), channel_id=1, source_target_pairs={{0,8},{1,9},{2,10},{3,11},{4,12},{5,13},{6,14},{7,15},{8,0},{9,1},... | collective-permute-start | bytes 331784 | tf_op jit(solution)/shard_map/ppermute | solution.py:358
  57.0 5.8 %collective-permute-start.22 = (bf16[16,3456]{1,0:T(8,128)(2,1)S(1)}, bf16[16,3456]{1,0:T(8,128)(2,1)S(1)}, u32[]{:S(2)}, u32[]{:S(2)}) collective-permute-start(bf16[16,3456]{1,0:T(8,128)(2,1)S(1)} %shard_map.90.refs_0_), channel_id=1, source_target_pairs={{0,3},{1,2},{2,1},{3,0},{4,7},{5,6},{6,5},{7,4},{8,11},{9,10},{10,... | collective-permute-start | bytes 331784 | tf_op jit(solution)/shard_map/ppermute | solution.py:358
  58.6 7.6 %collective-permute-start.21 = (bf16[16,3456]{1,0:T(8,128)(2,1)S(1)}, bf16[16,3456]{1,0:T(8,128)(2,1)S(1)}, u32[]{:S(2)}, u32[]{:S(2)}) collective-permute-start(bf16[16,3456]{1,0:T(8,128)(2,1)S(1)} %shard_map.90.refs_0_), channel_id=1, source_target_pairs={{0,2},{1,3},{2,0},{3,1},{4,6},{5,7},{6,4},{7,5},{8,10},{9,11},{10,... | collective-permute-start | bytes 331784 | tf_op jit(solution)/shard_map/ppermute | solution.py:358
  58.6 7.6 %collective-permute-start.20 = (bf16[16,3456]{1,0:T(8,128)(2,1)S(1)}, bf16[16,3456]{1,0:T(8,128)(2,1)S(1)}, u32[]{:S(2)}, u32[]{:S(2)}) collective-permute-start(bf16[16,3456]{1,0:T(8,128)(2,1)S(1)} %shard_map.90.refs_0_), channel_id=1, source_target_pairs={{0,1},{1,0},{2,3},{3,2},{4,5},{5,4},{6,7},{7,6},{8,9},{9,8},{10,11... | collective-permute-start | bytes 331784 | tf_op jit(solution)/shard_map/ppermute | solution.py:358
  60.6 7.1 %collective-permute-start.13 = (bf16[16,3456]{1,0:T(8,128)(2,1)S(1)}, bf16[16,3456]{1,0:T(8,128)(2,1)S(1)}, u32[]{:S(2)}, u32[]{:S(2)}) collective-permute-start(bf16[16,3456]{1,0:T(8,128)(2,1)S(1)} %shard_map.85.refs_0_), channel_id=1, source_target_pairs={{0,3},{1,2},{2,1},{3,0},{4,7},{5,6},{6,5},{7,4},{8,11},{9,10},{10,... | collective-permute-start | bytes 331784 | tf_op jit(solution)/shard_map/ppermute | solution.py:358
  62.2 6.4 %collective-permute-start.12 = (bf16[16,3456]{1,0:T(8,128)(2,1)S(1)}, bf16[16,3456]{1,0:T(8,128)(2,1)S(1)}, u32[]{:S(2)}, u32[]{:S(2)}) collective-permute-start(bf16[16,3456]{1,0:T(8,128)(2,1)S(1)} %shard_map.85.refs_0_), channel_id=1, source_target_pairs={{0,2},{1,3},{2,0},{3,1},{4,6},{5,7},{6,4},{7,5},{8,10},{9,11},{10,... | collective-permute-start | bytes 331784 | tf_op jit(solution)/shard_map/ppermute | solution.py:358
  62.8 5.9 %collective-permute-start.11 = (bf16[16,3456]{1,0:T(8,128)(2,1)S(1)}, bf16[16,3456]{1,0:T(8,128)(2,1)S(1)}, u32[]{:S(2)}, u32[]{:S(2)}) collective-permute-start(bf16[16,3456]{1,0:T(8,128)(2,1)S(1)} %shard_map.85.refs_0_), channel_id=1, source_target_pairs={{0,1},{1,0},{2,3},{3,2},{4,5},{5,4},{6,7},{7,6},{8,9},{9,8},{10,11... | collective-permute-start | bytes 331784 | tf_op jit(solution)/shard_map/ppermute | solution.py:358
  66.3 4.2 %collective-permute-start.23 = (bf16[64,3456]{1,0:T(8,128)(2,1)S(1)}, bf16[64,3456]{1,0:T(8,128)(2,1)S(1)}, u32[]{:S(2)}, u32[]{:S(2)}) collective-permute-start(bf16[64,3456]{1,0:T(8,128)(2,1)S(1)} %shard_map.91.own), channel_id=1, source_target_pairs={{0,16},{16,0},{1,17},{17,1},{2,18},{18,2},{3,19},{19,3},{4,20},{20... | collective-permute-start | bytes 1327112 | tf_op jit(solution)/shard_map/ppermute | solution.py:358
  68.7 3.2 %collective-permute-start.14 = (bf16[64,3456]{1,0:T(8,128)(2,1)S(1)}, bf16[64,3456]{1,0:T(8,128)(2,1)S(1)}, u32[]{:S(2)}, u32[]{:S(2)}) collective-permute-start(bf16[64,3456]{1,0:T(8,128)(2,1)S(1)} %shard_map.86.own), channel_id=1, source_target_pairs={{0,16},{16,0},{1,17},{17,1},{2,18},{18,2},{3,19},{19,3},{4,20},{20... | collective-permute-start | bytes 1327112 | tf_op jit(solution)/shard_map/ppermute | solution.py:358

commit v2 on v1

v2 whole, which is shorter than its diff:
```python
import functools

import jax
import jax.numpy as jnp
from jax import lax
from jax.experimental import pallas as pl
from jax.experimental.pallas import tpu as pltpu
from jax.sharding import PartitionSpec as P

TILE = 8
FACE = TILE * TILE
RIM = TILE + 2
GROWN = TILE + 4
IN_PITCH = 160
PITCH = 128
INNER_PITCH = 80
OUTER_PITCH = 48
EDGE = 24
SPARE = 16
TAPS = 27
INNER = 4
BF = jnp.bfloat16
F32 = jnp.float32
unscale = 1.0 / 512.0
LIMIT = 24 * 2**20

VM = pl.BlockSpec(memory_space=pltpu.VMEM)
SM = pl.BlockSpec(memory_space=pltpu.SMEM)


def call(body, outs, ins, scratch=(), smem=(), flops=0):
    specs = [SM if i in smem else VM for i in range(len(ins))]
    moved = sum(a.size * a.dtype.itemsize for a in list(ins) + list(outs))
    return pl.pallas_call(
        body,
        out_shape=list(outs),
        in_specs=specs,
        out_specs=[VM] * len(outs),
        scratch_shapes=list(scratch),
        compiler_params=pltpu.CompilerParams(vmem_limit_bytes=LIMIT),
        cost_estimate=pl.CostEstimate(flops=flops, bytes_accessed=moved, transcendentals=0),
    )(*ins)


def shape(dims, kind):
    return jax.ShapeDtypeStruct(dims, kind)


def parity(stride):
    return lax.axis_index("blk") // stride % 2


def pack_depth(planes, tile_of, mask_rows, mask, feat, cot, inp, grads, marks, even, odd, wide):
    lines = planes * TILE
    row = lax.broadcasted_iota(jnp.int32, (mask_rows, 128), 0)
    filled = jnp.zeros((mask_rows, 128), F32)
    kept_of = [mask[0, tile_of(e)].astype(F32) for e in range(planes)]
    for e in range(planes):
        filled = jnp.where(row == e, kept_of[e], filled)
    filled = filled.astype(BF)
    marks[...] = filled
    even[4 * lines :, :] = filled
    odd[4 * lines :, :] = filled
    side = parity(1)
    for at, (src, dst) in enumerate(((feat, inp), (cot, grads))):
        for e in range(planes):
            rows = slice(e * FACE, (e + 1) * FACE)
            kept = src[rows, :].astype(F32) * kept_of[e]
            wide[rows, :] = kept
            dst[rows, :] = kept.astype(BF)

        def faces(lo, hi, at=at):
            for k in range(2):
                to = slice((at * 2 + k) * lines, (at * 2 + k + 1) * lines)
                lo[to, :] = wide[pl.ds(k, lines, stride=TILE), :].astype(BF)
                hi[to, :] = wide[pl.ds(TILE - 2 + k, lines, stride=TILE), :].astype(BF)

        @pl.when(side == 0)
        def _():
            faces(odd, even)

        @pl.when(side == 1)
        def _():
            faces(even, odd)


def pack_lines(
    planes, mask_rows, inp, grads, marks, z_even, z_odd, even, odd, deep_in, deep_g, marks3
):
    lines = planes * TILE
    plane = TILE * GROWN
    edge = 2 * GROWN
    swapped = parity(1) == 0

    def sides(rows):
        one, two = z_even[rows, :].astype(F32), z_odd[rows, :].astype(F32)
        return jnp.where(swapped, two, one), jnp.where(swapped, one, two)

    left, right = sides(slice(4 * lines, 4 * lines + mask_rows))
    for at, rows in enumerate((left, marks[...].astype(F32), right)):
        marks3[at * mask_rows : (at + 1) * mask_rows, :] = rows.astype(BF)
    for ref in (even, odd):
        ref[4 * planes * GROWN :, :] = marks3[...]
    side = parity(4)
    for at, (src, dst) in enumerate(((inp, deep_in), (grads, deep_g))):
        dst[lines * GROWN :, :] = jnp.zeros((SPARE, 128), F32)
        for pair in range(0, lines, 2):
            cells = src[pair * TILE : (pair + 2) * TILE, :].astype(F32)
            top = pair * GROWN + 2
            dst[top : top + TILE, :] = cells[:TILE]
            dst[top + GROWN : top + GROWN + TILE, :] = cells[TILE:]
        for k in range(2):
            left, right = sides(slice((at * 2 + k) * lines, (at * 2 + k + 1) * lines))
            dst[pl.ds(k, lines, stride=GROWN), :] = left
            dst[pl.ds(2 + TILE + k, lines, stride=GROWN), :] = right

        def faces(lo, hi, at=at, dst=dst):
            for e in range(0, planes, 2):
                to = slice((at * planes + e) * edge, (at * planes + e + 2) * edge)
                for ref, start in ((lo, 0), (hi, plane - edge)):
                    ref[to, :] = jnp.concatenate(
                        [
                            dst[p * plane + start : p * plane + start + edge, :]
                            for p in (e, e + 1)
                        ],
                        0,
                    ).astype(BF)

        @pl.when(side == 0)
        def _():
            faces(odd, even)

        @pl.when(side == 1)
        def _():
            faces(even, odd)


def lay_weights(src, *refs):
    *outs, wide = refs
    wide[...] = src[...].astype(F32)
    for tap in range(TAPS):
        a, bc = tap // 9, tap % 9
        block = wide[pl.ds(tap, 128, stride=TAPS), :].astype(BF)
        outs[0][a * 128 : (a + 1) * 128, bc * 128 : (bc + 1) * 128] = block
        for out in outs[1:]:
            out[bc * 128 : (bc + 1) * 128, a * 128 : (a + 1) * 128] = block


def dot(a, b):
    return lax.dot_general(a, b, (((1,), (0,)), ((), ())), preferred_element_type=F32)


def dot_t(a, b):
    return lax.dot_general(a, b, (((1,), (1,)), ((), ())), preferred_element_type=F32)


def spread(planes, first_plane, at, deep, y_even, y_odd, grid):
    plane = TILE * GROWN
    edge = 2 * GROWN
    swapped = parity(4) == 0
    used = edge + plane + edge
    for p in range(grid.shape[0] // IN_PITCH):
        top = p * IN_PITCH
        if first_plane <= p < first_plane + planes:
            grid[top + used : top + IN_PITCH, :] = jnp.zeros((IN_PITCH - used, 128), F32)
            e = p - first_plane
            grid[top + edge : top + edge + plane, :] = deep[e * plane : (e + 1) * plane, :]
        else:
            grid[top : top + IN_PITCH, :] = jnp.zeros((IN_PITCH, 128), F32)
    for e in range(0, planes, 2):
        rows = slice((at * planes + e) * edge, (at * planes + e + 2) * edge)
        one, two = y_even[rows, :].astype(F32), y_odd[rows, :].astype(F32)
        low, high = jnp.where(swapped, two, one), jnp.where(swapped, one, two)
        for k in range(2):
            top = (first_plane + e + k) * IN_PITCH
            grid[top : top + edge, :] = low[k * edge : (k + 1) * edge]
            grid[top + edge + plane : top + used, :] = high[k * edge : (k + 1) * edge]


def stack(planes, first, pitch, parts, grid, stacked, out_pitch, flipped):
    for j in range(planes):
        for b in range(3):
            for c in range(3):
                step = (2 - b) * GROWN + 2 - c if flipped else b * GROWN + c
                at = (3 * b + c) * 128
                cells = [
                    grid[(j + first) * pitch + lo + step : (j + first) * pitch + lo + step + n, :]
                    for lo, n in parts
                ]
                cells = cells[0] if len(cells) == 1 else jnp.concatenate(cells, 0)
                to = j * out_pitch
                stacked[to : to + out_pitch, at : at + 128] = cells.astype(BF)


def add_planes(planes, pitch, shift, pair, single, p):
    total = jnp.zeros((pitch, 128), F32)
    for a, (ref, at) in enumerate(((pair, 0), (pair, 128), (single, 0))):
        j = p - shift(a)
        if 0 <= j < planes:
            total = total + ref[j * pitch : (j + 1) * pitch, at : at + 128]
    return total


def own_lines(grid, at):
    return jnp.concatenate([grid[at : at + TILE, :], grid[at + GROWN : at + GROWN + TILE, :]], 0)


def stack_own(planes, first, pitch, skip, grid, stacked):
    for p in range(planes):
        for y in range(0, TILE, 2):
            to = p * FACE + y * TILE
            for b in range(3):
                for c in range(3):
                    at = (p + first) * pitch + (y + skip + 2 - b) * GROWN + skip + 2 - c
                    stacked[to : to + 2 * TILE, (3 * b + c) * 128 : (3 * b + c + 1) * 128] = (
                        own_lines(grid, at).astype(BF)
                    )


def emit(core, at, value, kept, sent):
    half = value.shape[0] // 2
    columns = slice(at, at + value.shape[1])

    @pl.when(core == 0)
    def _():
        kept[:, columns] = value[:half]
        sent[:, columns] = value[half:].astype(BF)

    @pl.when(core == 1)
    def _():
        kept[:, columns] = value[half:]
        sent[:, columns] = value[:half].astype(BF)


def marked(planes, mask_rows, marks3, y_even, y_odd):
    tail = 4 * planes * GROWN
    swapped = parity(4) == 0

    def mark(by, bz, e):
        at = bz * mask_rows + e
        if by == 1:
            return marks3[at : at + 1, :].astype(F32)
        one = y_even[tail + at : tail + at + 1, :].astype(F32)
        two = y_odd[tail + at : tail + at + 1, :].astype(F32)
        return jnp.where(swapped, two, one) if by == 0 else jnp.where(swapped, one, two)

    return mark


def spans(rows, ends):
    row = lax.broadcasted_iota(jnp.int32, (rows, 128), 0)
    line = row // GROWN
    depth = row - line * GROWN
    return [(line >= lo) & (line <= hi) for lo, hi in ends], [
        (depth >= lo) & (depth <= hi) for lo, hi in ends
    ]


def pad_terms(*refs):
    used = TAPS * 128
    for ref in refs:
        if ref.shape[1] > used:
            ref[:, used:] = jnp.zeros((ref.shape[0], ref.shape[1] - used), ref.dtype)


def ahead(
    planes, deep,
    deep_in, deep_g, inp, w1_tall, w2_wide,
    act, back, in_t,
    stacked, pair, single, padded,
):
    size_x = planes - 4 * deep
    n_out = size_x + 2 * deep
    parts = ((0, INNER_PITCH),)
    plane = TILE * GROWN
    stack(planes, 0, plane, parts, deep_in, stacked, INNER_PITCH, False)
    pair[...] = dot(stacked[...], w1_tall[:, 0:256])
    single[...] = dot(stacked[...], w1_tall[:, 256:384])
    for p in range(n_out):
        act[p * INNER_PITCH : (p + 1) * INNER_PITCH, :] = add_planes(
            planes, INNER_PITCH, lambda a: 1 - deep - a, pair, single, p
        )
    stack(planes, 0, plane, parts, deep_g, stacked, INNER_PITCH, True)
    pair[...] = dot_t(stacked[...], w2_wide[0:256, :])
    single[...] = dot_t(stacked[...], w2_wide[256:384, :])
    for p in range(n_out):
        back[p * INNER_PITCH : (p + 1) * INNER_PITCH, :] = add_planes(
            planes, INNER_PITCH, lambda a: a - 1 - deep, pair, single, p
        )
    padded[...] = jnp.zeros_like(padded)
    top = (1 + deep) * FACE
    rows = size_x * FACE
    padded[top : top + rows, :] = inp[2 * deep * FACE : 2 * deep * FACE + rows, :].astype(F32)
    in_t[...] = padded[...].T.astype(BF)


def whole_plane(inner, outer, p):
    ends = outer[p * OUTER_PITCH : (p + 1) * OUTER_PITCH]
    middle = inner[p * INNER_PITCH : p * INNER_PITCH + PITCH - 2 * EDGE - TILE, :]
    rest = jnp.zeros((TILE, 128), F32)
    return jnp.concatenate([ends[:EDGE], middle, ends[EDGE:], rest], 0)


OUTER_PARTS = ((0, EDGE), (PITCH - EDGE - TILE, EDGE))


def correlate(turned_rows, stacked, columns):
    left = jnp.concatenate([turned_rows[:, a * FACE : a * FACE + columns] for a in range(3)], 0)
    return dot(left, stacked) * unscale


def forward(
    planes, deep, mask_rows,
    deep_in, deep_g, marks3, y_even, y_odd, inner, w1_tall,
    kept, sent, act, grid_g,
    grid_in, outer, pair, single, st_own, hidden,
):
    core = lax.axis_index("dp")
    size_x = planes - 4 * deep
    n_out = size_x + 2 * deep
    first = 1 - deep
    third = 9 * 128
    spread(planes, first, 0, deep_in, y_even, y_odd, grid_in)
    stack(planes, first, IN_PITCH, OUTER_PARTS, grid_in, outer, OUTER_PITCH, False)
    pair[...] = dot(outer[...], w1_tall[:, 0:256])
    single[...] = dot(outer[...], w1_tall[:, 256:384])
    for p in range(n_out):
        ends = add_planes(planes, OUTER_PITCH, lambda a: 1 - deep - a, pair, single, p)
        act[p * PITCH : (p + 1) * PITCH, :] = whole_plane(
            inner.at[p * INNER_PITCH : (p + 1) * INNER_PITCH, :], ends, 0
        )
    spread(planes, first, 1, deep_g, y_even, y_odd, grid_g)
    stack_own(planes, first, IN_PITCH, 1, grid_g, st_own)
    hidden[...] = jnp.zeros_like(hidden)
    for p in range(size_x):
        at = mask_rows + p + 2 * deep
        keep = marks3[at : at + 1, :].astype(F32)
        for y in range(0, TILE, 2):
            pre = own_lines(act, (p + deep) * PITCH + (y + 1) * GROWN + 1)
            to = (p + 1 + 2 * deep) * FACE + y * TILE
            hidden[to : to + 2 * TILE, :] = pre * jax.nn.sigmoid(pre) * keep
    part = correlate(hidden[...].T.astype(BF), st_own[...], planes * FACE)
    for a in range(3):
        emit(core, a * third, part[a * 128 : (a + 1) * 128], kept, sent)
    pad_terms(kept, sent)


def backward(
    planes, deep, mask_rows, tile_of,
    grid_g, act, inner, in_t, marks3, y_even, y_odd, w2_wide,
    kept, sent, st_own,
    outer, pair, single, pg,
):
    core = lax.axis_index("dp")
    size_x = planes - 4 * deep
    n_out = size_x + 2 * deep
    third = 9 * 128
    mark = marked(planes, mask_rows, marks3, y_even, y_odd)
    in_line, in_depth = spans(PITCH, ((0, 0), (1, TILE), (RIM - 1, RIM - 1)))
    stack(planes, 1 - deep, IN_PITCH, OUTER_PARTS, grid_g, outer, OUTER_PITCH, True)
    pair[...] = dot_t(outer[...], w2_wide[0:256, :])
    single[...] = dot_t(outer[...], w2_wide[256:384, :])
    tile, keep = None, None
    for p in range(n_out):
        if tile_of(p + deep) != tile:
            tile, keep = tile_of(p + deep), jnp.zeros((PITCH, 128), F32)
            for by in range(3):
                for bz in range(3):
                    keep = jnp.where(in_line[by] & in_depth[bz], mark(by, bz, p + deep), keep)
        ends = add_planes(planes, OUTER_PITCH, lambda a: a - 1 - deep, pair, single, p)
        back = whole_plane(inner.at[p * INNER_PITCH : (p + 1) * INNER_PITCH, :], ends, 0)
        pre = act[p * PITCH : (p + 1) * PITCH, :]
        sigma = jax.nn.sigmoid(pre)
        grad = back * sigma * (1.0 + pre * (1.0 - sigma))
        pg[p * PITCH : (p + 1) * PITCH, :] = (grad * keep).astype(BF).astype(F32)
    stack_own(n_out, 0, PITCH, 0, pg, st_own)
    part = correlate(in_t, st_own[...], n_out * FACE)
    for a in range(3):
        emit(core, a * third, part[a * 128 : (a + 1) * 128], kept, sent)
    pad_terms(kept, sent)


def last(planes, deep, mask_rows, st_own, grads, marks3, w1_wide, result, pair, single):
    size_x = planes - 4 * deep
    n_out = size_x + 2 * deep
    pair[...] = dot_t(st_own[...], w1_wide[0:256, :])
    single[...] = dot_t(st_own[...], w1_wide[256:384, :])
    for p in range(size_x):
        e = p + 2 * deep
        m = marks3[mask_rows + e : mask_rows + e + 1, :].astype(F32)
        total = add_planes(n_out, FACE, lambda a: a - 1 - deep, pair, single, p)
        summed = (grads[e * FACE : (e + 1) * FACE, :].astype(F32) + total) * m
        result[p * FACE : (p + 1) * FACE, :] = summed.astype(BF)


def swap(value, axis, bits):
    count = lax.axis_size(axis)
    return lax.ppermute(value, axis, [(source, source ^ bits) for source in range(count)])


def cross(value, bits):
    count = lax.axis_size("blk")
    pairs = [
        (core * count + s, core * count + (s ^ bit))
        for core, bit in enumerate(bits)
        for s in range(count)
    ]
    return lax.ppermute(value, ("dp", "blk"), pairs)


def turned(k):
    return {0: 0, 1: 1 + lax.axis_index("dp"), 2: 2 - lax.axis_index("dp"), 3: 3}[k]


def split_rows(parts, kept, got, own, *sent):
    me = lax.axis_index("blk") % INNER
    rows = own.shape[0]
    for k in range(parts):
        at = pl.ds(pl.multiple_of((me ^ turned(k)) * rows, rows), rows)
        value = kept[at, :] + got[at, :].astype(F32)
        if k == 0:
            own[...] = value
        else:
            sent[k - 1][...] = value.astype(BF)


def split_columns(parts, *refs):
    kept, got, own, sent = refs[0], refs[1:INNER], refs[INNER], refs[INNER + 1 :]
    me = lax.axis_index("blk") // INNER
    columns = own.shape[1]
    for k in range(parts):
        at = pl.ds(pl.multiple_of((me ^ k) * columns, 128), columns)
        value = kept[:, at]
        for ref in got:
            value = value + ref[:, at].astype(F32)
        if k == 0:
            own[...] = value
        else:
            sent[k - 1][...] = value.astype(BF)


def add_pair(one, two, out):
    out[...] = (one[...].astype(F32) + two[...].astype(F32)).astype(BF)


def add_all(parts, *refs):
    value = refs[0][...]
    for ref in refs[1:parts]:
        value = value + ref[...].astype(F32)
    refs[parts][...] = value.astype(BF)


def join_columns(parts, *refs):
    me = lax.axis_index("blk") // INNER
    out = refs[parts]
    columns = refs[0].shape[1]
    for k in range(parts):
        out[:, pl.ds(pl.multiple_of((me ^ k) * columns, 128), columns)] = refs[k][...]


def join_rows(parts, *refs):
    me = lax.axis_index("blk") % INNER
    out = refs[parts]
    rows = refs[0].shape[0]
    for k in range(parts):
        out[pl.ds(pl.multiple_of((me ^ turned(k)) * rows, rows), rows), :] = refs[k][...]


def finish(own, other, out):
    core = lax.axis_index("dp")
    half = own.shape[0]

    def write(low, high):
        for at, ref in ((0, low), (half, high)):
            for tap in range(TAPS):
                out[pl.ds(at * TAPS + tap, half, stride=TAPS), :] = ref[
                    :, tap * 128 : (tap + 1) * 128
                ].astype(F32)

    @pl.when(core == 0)
    def _():
        write(own, other)

    @pl.when(core == 1)
    def _():
        write(other, own)


def after(value, *others):
    return lax.optimization_barrier((value, *others))[0]


def near(values):
    return [cross(v, bits) for v, bits in zip(values, ((1, 2), (2, 1), (3, 3)))]


def far(values):
    return [swap(v, "blk", INNER * (k + 1)) for k, v in enumerate(values)]


def split_stage(kept, got):
    half, columns = kept.shape
    rows = half // INNER
    return call(
        functools.partial(split_rows, INNER),
        [shape((rows, columns), F32)] + [shape((rows, columns), BF)] * (INNER - 1),
        [kept, got],
    )


def sum_stage(own, gots):
    parts = len(gots) + 1
    return call(functools.partial(add_all, parts), [shape(own.shape, BF)], [own] + gots)[0]


def pair_stage(value, got):
    return call(add_pair, [shape(value.shape, BF)], [value, got])[0]


def back_stage(wide, gots):
    rows, columns = wide.shape
    return call(
        functools.partial(join_rows, INNER), [shape((rows * INNER, columns), BF)], [wide] + gots
    )[0]


def wide_sum(own, gots):
    outer = lax.axis_size("blk") // INNER
    rows, columns = own.shape
    part = columns // outer
    own, *send = call(
        functools.partial(split_columns, outer),
        [shape((rows, part), F32)] + [shape((rows, part), BF)] * (outer - 1),
        [own] + gots,
    )
    done = sum_stage(own, far(send))
    return call(
        functools.partial(join_columns, outer),
        [shape((rows, columns), BF)],
        [done] + far([done] * (outer - 1)),
    )[0]


def finished(mine, other):
    return call(finish, [shape((2 * mine.shape[0] * TAPS, 128), F32)], [mine, other])[0]


def across(owns, gots, beside):
    outer = lax.axis_size("blk") // INNER
    if outer > 4:
        one, two = [wide_sum(own, got) for own, got in zip(owns, gots)]
        return one, two, beside(one)
    one = sum_stage(owns[0], gots[0])
    two = sum_stage(after(owns[1], one), gots[1])
    steps = [INNER << k for k in range(outer.bit_length() - 1)]
    other = None
    for bits in zip(steps, reversed(steps)):
        got_one, got_two = cross(one, bits), cross(two, bits)
        one = pair_stage(after(one, two), got_one)
        if other is None:
            other = beside(one)
            two = after(two, other)
        two = pair_stage(after(two, one), got_two)
    return one, two, other


def on_device(features, tile_mask, w_first, w_second, cotangent):
    width = features.shape[2]
    tiles = tile_mask.shape[1]
    size_x = tiles * TILE
    count = lax.axis_size("blk")
    deep = 1 if count // 16 > 1 else 0
    planes = size_x + 4 * deep
    feat, cot, mask = features[0], cotangent[0], tile_mask

    def along(value, stride, extent, toward):
        pairs = [
            (s, s + toward * stride)
            for s in range(count)
            if 0 <= s // stride % extent + toward < extent
        ]
        return lax.ppermute(value, "blk", pairs)

    if deep:
        wide_mask = jnp.broadcast_to(
            jnp.repeat(tile_mask[0], TILE)[:, None], (size_x, width)
        ).astype(BF)
        keep = jnp.repeat(wide_mask, FACE, axis=0)
        feat, cot = feat * keep, cot * keep
        slab = 2 * FACE
        up = jnp.concatenate([feat[-slab:], cot[-slab:], wide_mask[-16:]], 0)
        down = jnp.concatenate([feat[:slab], cot[:slab], wide_mask[:16]], 0)
        before = along(up, 16, count // 16, 1)
        behind = along(down, 16, count // 16, -1)
        feat = jnp.concatenate([before[:slab], feat, behind[:slab]], 0)
        cot = jnp.concatenate([before[slab : 2 * slab], cot, behind[slab : 2 * slab]], 0)
        ends = [v[2 * slab : 2 * slab + 1, :1].astype(jnp.int32) for v in (before, behind)]
        mask = jnp.concatenate([ends[0], tile_mask, ends[1]], 1)

    def tile_of(e):
        if not deep:
            return e // TILE
        return (e + TILE - 2) // TILE

    def beside(one, two, stride, extent):
        pairs = ([], [])
        for s in range(count):
            place = s // stride % extent
            if place + 1 < extent:
                pairs[place % 2].extend([(s, s + stride), (s + stride, s)])
        return lax.ppermute(one, "blk", pairs[0]), lax.ppermute(two, "blk", pairs[1])

    mask_rows = -(-planes // 16) * 16
    lines = planes * TILE
    cells = planes * FACE
    side = 4 * lines + mask_rows
    inp, grads, marks, even, odd = call(
        functools.partial(pack_depth, planes, tile_of, mask_rows),
        [shape((cells, width), BF)] * 2
        + [shape((mask_rows, width), BF)]
        + [shape((side, width), BF)] * 2,
        [mask, feat, cot],
        scratch=[pltpu.VMEM((cells, width), F32)],
        smem=(0,),
    )
    z_even, z_odd = beside(even, odd, 1, 4)
    broad = shape((3 * width, 9 * width), BF)
    upright = shape((9 * width, 3 * width), BF)

    def laid(weight, outs):
        return call(lay_weights, outs, [weight], scratch=[pltpu.VMEM((TAPS * width, width), F32)])

    (w2_wide,) = laid(w_second, [broad])
    w1_wide, w1_tall = laid(w_first, [broad, upright])
    inp = after(inp, w2_wide, w1_wide)
    edge = 4 * planes * GROWN + 3 * mask_rows
    even, odd, deep_in, deep_g, marks3 = call(
        functools.partial(pack_lines, planes, mask_rows),
        [shape((edge, width), BF)] * 2
        + [shape((lines * GROWN + SPARE, width), F32)] * 2
        + [shape((3 * mask_rows, width), BF)],
        [inp, grads, marks, z_even, z_odd],
    )
    y_even, y_odd = beside(even, odd, 4, 4)
    outer = count // INNER
    columns = TAPS * width if outer <= 4 else -(-TAPS // outer) * outer * width
    n_in = size_x + 2 + 2 * deep
    n_out = size_x + 2 * deep
    half = width // 2
    work = 2 * size_x * FACE * TAPS * width * width
    terms = [shape((half, columns), F32), shape((half, columns), BF)]

    def parts_of(rows):
        return [pltpu.VMEM((rows, 2 * width), F32), pltpu.VMEM((rows, width), F32)]

    inner_act, inner_back, in_t = call(
        functools.partial(ahead, planes, deep),
        [shape((n_out * INNER_PITCH, width), F32)] * 2
        + [shape((width, (n_out + 2) * FACE), BF)],
        [deep_in, deep_g, inp, w1_tall, w2_wide],
        scratch=[pltpu.VMEM((planes * INNER_PITCH, 9 * width), BF)]
        + parts_of(planes * INNER_PITCH)
        + [pltpu.VMEM(((n_out + 2) * FACE, width), F32)],
        flops=2 * work,
    )
    marks3 = after(marks3, in_t)
    kept_a, sent_a, act, grid_g = call(
        functools.partial(forward, planes, deep, mask_rows),
        terms + [shape((n_out * PITCH, width), F32), shape((n_in * IN_PITCH, width), F32)],
        [deep_in, deep_g, marks3, y_even, y_odd, inner_act, w1_tall],
        scratch=[
            pltpu.VMEM((n_in * IN_PITCH, width), F32),
            pltpu.VMEM((planes * OUTER_PITCH, 9 * width), BF),
        ]
        + parts_of(planes * OUTER_PITCH)
        + [
            pltpu.VMEM((planes * FACE, 9 * width), BF),
            pltpu.VMEM(((planes + 2) * FACE, width), F32),
        ],
        flops=2 * work,
    )
    own_a, *send_a = split_stage(kept_a, swap(sent_a, "dp", 1))
    kept_b, sent_b, st_own = call(
        functools.partial(backward, planes, deep, mask_rows, tile_of),
        terms + [shape((n_out * FACE, 9 * width), BF)],
        [grid_g, act, inner_back, in_t, marks3, y_even, y_odd, w2_wide],
        scratch=[pltpu.VMEM((planes * OUTER_PITCH, 9 * width), BF)]
        + parts_of(planes * OUTER_PITCH)
        + [pltpu.VMEM((n_out * PITCH, width), F32)],
        flops=2 * work,
    )
    own_b, *send_b = split_stage(kept_b, swap(sent_b, "dp", 1))
    gots_a = near(send_a)
    gots_b = near(send_b)
    own_a = after(own_a, own_b)

    def last_part(cue):
        return call(
            functools.partial(last, planes, deep, mask_rows),
            [shape((size_x * FACE, width), BF)],
            [after(st_own, cue), grads, marks3, w1_wide],
            scratch=parts_of(n_out * FACE),
            flops=work,
        )[0]

    value_a, value_b, result = across((own_a, own_b), (gots_a, gots_b), last_part)
    gots_a = near([value_a] * (INNER - 1))
    gots_b = near([value_b] * (INNER - 1))
    mine_a = back_stage(value_a, gots_a)
    mine_b = back_stage(value_b, gots_b)
    grad_second = finished(mine_a, swap(mine_a, "dp", 1))
    grad_first = finished(mine_b, swap(mine_b, "dp", 1))
    return (grad_first, grad_second, result[None])


def solution(mesh):
    in_specs = (P("dp", "blk", None), P("dp", "blk"), P(), P(), P("dp", "blk", None))
    out_specs = (P(), P(), P("dp", "blk", None))
    return jax.shard_map(
        on_device, mesh=mesh, in_specs=in_specs, out_specs=out_specs, check_vma=False
    )
```

time: 73.5 us -> 64.2 us (0.87)
  waiting for transfers between devices: 14.2 us -> 8.78 us
  Pallas kernels: 14.8 us -> 11.3 us
    ppermute x0 -> x16, starting transfers between devices: none -> 31.6 us  [cross(): return lax.ppermute(value, ('dp', 'blk'), pairs)]
    ppermute x20 -> x4, starting transfers between devices: 32.2 us -> 0.76 us  [swap(): lax.ppermute(value, axis, [(source, source ^ bits) for source in range(co...]
    ppermute x20 -> x4, waiting for transfers between devices: 12.6 us -> 0.44 us  [swap(): lax.ppermute(value, axis, [(source, source ^ bits) for source in range(co...]
    ppermute x0 -> x16, waiting for transfers between devices: none -> 7.87 us  [cross(): return lax.ppermute(value, ('dp', 'blk'), pairs)]
    pallas_call x18 -> x20, Pallas kernels: 14.8 us -> 11.3 us  [call(): pl.pallas_call(body, out_shape=list(outs), in_specs=specs, out_specs=[VM]...]
    ppermute x2, waiting for transfers between devices: 1.63 us -> 0.47 us  [beside(): lax.ppermute(one, 'blk', pairs[0])]
  transfers between devices with their start and end apart: 24 -> 24, of which waited for: 10 -> 8; matrix products, arithmetic and copies ran while one was open for 0% -> 0% of each run, Pallas kernels for 6% -> 12%
where the time goes in v2:
time: 64.2 us; the launch traced here: 63.9 us
  starting transfers between devices  38.3 us (60%)
  Pallas kernels  11.3 us (18%)
  waiting for transfers between devices  8.78 us (14%)
  local copies, waits for them, and re-layouts  4.13 us (6%)
  between operations  1.48 us (2%)
    ppermute x16, starting transfers between devices, cross(): return lax.ppermute(value, ('dp', 'blk'), pairs)  31.6 us
    pallas_call x20, Pallas kernels, call(): pl.pallas_call(body, out_shape=list(outs), in_specs=specs, out_specs=[VM]...  11.3 us
    ppermute x16, waiting for transfers between devices, cross(): return lax.ppermute(value, ('dp', 'blk'), pairs)  7.87 us
    ppermute x2, starting transfers between devices, beside(): lax.ppermute(one, 'blk', pairs[0])  4.64 us
    unnamed x8, local copies, waits for them, and re-layouts  4.13 us
    ppermute x2, starting transfers between devices, beside(): lax.ppermute(two, 'blk', pairs[1])  1.31 us
  transfers between devices with their start and end apart: 24, of which 8 were waited for; matrix products, arithmetic and copies ran while one was open for 0% of the time, Pallas kernels for 12%

profile of v2, /device:TPU:0, one launch (start us, length us, event | category | flops | bytes accessed | tf_op | source)
XLA Modules:
  0.0 63.9 jit_solution(12012973412737988779)
XLA Ops:
  1.3 0.9 %copy-done.2 = bf16[1,512,128]{2,1,0:T(8,128)(2,1)S(1)} copy-done((bf16[1,512,128]{2,1,0:T(8,128)(2,1)S(1)}, bf16[1,512,128]{2,1,0:T(8,128)(2,1)}, u32[]{:S(2)}) %copy-start.2) | copy-done | bytes 131096
  2.2 0.9 %copy-done.3 = bf16[1,512,128]{2,1,0:T(8,128)(2,1)S(1)} copy-done((bf16[1,512,128]{2,1,0:T(8,128)(2,1)S(1)}, bf16[1,512,128]{2,1,0:T(8,128)(2,1)}, u32[]{:S(2)}) %copy-start.3) | copy-done | bytes 131096
  3.1 0.1 shard_map.76
  3.2 3.0 %collective-permute-start = (bf16[272,128]{1,0:T(8,128)(2,1)S(1)}, bf16[272,128]{1,0:T(8,128)(2,1)S(1)}, u32[]{:S(2)}, u32[]{:S(2)}) collective-permute-start(bf16[272,128]{1,0:T(8,128)(2,1)S(1)} %get-tuple-element.48), channel_id=1, source_target_pairs={{0,1},{1,0},{2,3},{3,2},{4,5},{5,4},{6,7},{7,6},{8,9},{9,8},{10,11... | collective-permute-start | bytes 208904 | tf_op jit(solution)/shard_map/ppermute | solution.py:611
  6.2 0.7 %collective-permute-start.1 = (bf16[272,128]{1,0:T(8,128)(2,1)S(1)}, bf16[272,128]{1,0:T(8,128)(2,1)S(1)}, u32[]{:S(2)}, u32[]{:S(2)}) collective-permute-start(bf16[272,128]{1,0:T(8,128)(2,1)S(1)} %get-tuple-element.49), channel_id=1, source_target_pairs={{1,2},{2,1},{5,6},{6,5},{9,10},{10,9},{13,14},{14,13},{17,18},{18,... | collective-permute-start | bytes 208904 | tf_op jit(solution)/shard_map/ppermute | solution.py:611
  6.9 0.0 copy-start
  6.9 1.2 %copy-done = bf16[3456,128]{1,0:T(8,128)(2,1)S(1)} copy-done((bf16[3456,128]{1,0:T(8,128)(2,1)S(1)}, bf16[3456,128]{1,0:T(8,128)(2,1)}, u32[]{:S(2)}) %copy-start) | copy-done | bytes 884760
  8.0 0.3 shard_map.78
  8.4 0.0 copy-start.1
  8.4 1.2 %copy-done.1 = bf16[3456,128]{1,0:T(8,128)(2,1)S(1)} copy-done((bf16[3456,128]{1,0:T(8,128)(2,1)S(1)}, bf16[3456,128]{1,0:T(8,128)(2,1)}, u32[]{:S(2)}) %copy-start.1) | copy-done | bytes 884760
  9.6 0.3 shard_map.77.w2_wide
  9.8 0.0 collective-permute-done.1.z_odd
  9.8 0.1 shard_map.79
  9.9 1.6 %collective-permute-start.2 = (bf16[432,128]{1,0:T(8,128)(2,1)S(1)}, bf16[432,128]{1,0:T(8,128)(2,1)S(1)}, u32[]{:S(2)}, u32[]{:S(2)}) collective-permute-start(bf16[432,128]{1,0:T(8,128)(2,1)S(1)} %get-tuple-element.56), channel_id=1, source_target_pairs={{0,4},{4,0},{1,5},{5,1},{2,6},{6,2},{3,7},{7,3},{8,12},{12,8},{9,1... | collective-permute-start | bytes 331784 | tf_op jit(solution)/shard_map/ppermute | solution.py:611
  11.6 0.7 %collective-permute-start.3 = (bf16[432,128]{1,0:T(8,128)(2,1)S(1)}, bf16[432,128]{1,0:T(8,128)(2,1)S(1)}, u32[]{:S(2)}, u32[]{:S(2)}) collective-permute-start(bf16[432,128]{1,0:T(8,128)(2,1)S(1)} %get-tuple-element.57), channel_id=1, source_target_pairs={{4,8},{8,4},{5,9},{9,5},{6,10},{10,6},{7,11},{11,7},{20,24},{24,20... | collective-permute-start | bytes 331784 | tf_op jit(solution)/shard_map/ppermute | solution.py:611
  12.2 2.0 %shard_map.80 = (f32[640,128]{1,0:T(8,128)S(1)}, f32[640,128]{1,0:T(8,128)S(1)}, bf16[128,640]{1,0:T(8,128)(2,1)S(1)}) custom-call(f32[784,128]{1,0:T(8,128)S(1)} %get-tuple-element.50.deep_in, f32[784,128]{1,0:T(8,128)S(1)} %get-tuple-element.51.deep_g, bf16[512,128]{1,0:T(8,128)(2,1)S(1)} %get-tuple-element.45.inp, ...), custom_call_target="tpu_custom_call" | custom-call | flops 905969664 | bytes 3522560 | tf_op jit(solution)/shard_map/pallas_call | solution.py:34
  14.3 0.5 collective-permute-done.2.y_even
  14.8 0.0 collective-permute-done.3.y_odd
  14.8 2.0 %shard_map.81 = (f32[64,3456]{1,0:T(8,128)S(1)}, bf16[64,3456]{1,0:T(8,128)(2,1)S(1)}, f32[1024,128]{1,0:T(8,128)S(1)}, f32[1600,128]{1,0:T(8,128)S(1)}) custom-call(f32[784,128]{1,0:T(8,128)S(1)} %get-tuple-element.50.deep_in, f32[784,128]{1,0:T(8,128)S(1)} %get-tuple-element.51.deep_g, bf16[48,128]{1,0:T(8,128)(2,1)S(1)} %get-tuple-element.55.marks3, ...), custom_call_target="tpu_custom_call" | custom-call | flops 905969664 | bytes 4919296 | tf_op jit(solution)/shard_map/pallas_call | solution.py:34
  16.7 0.1 collective-permute-start.5
  16.8 1.8 %shard_map.82 = (f32[64,3456]{1,0:T(8,128)S(1)}, bf16[64,3456]{1,0:T(8,128)(2,1)S(1)}, bf16[512,1152]{1,0:T(8,128)(2,1)S(1)}) custom-call(f32[1600,128]{1,0:T(8,128)S(1)} %get-tuple-element.59.grid_g, f32[1024,128]{1,0:T(8,128)S(1)} %get-tuple-element.60.act, f32[640,128]{1,0:T(8,128)S(1)} %get-tuple-element.61.inner, ...), custom_call_target="tpu_custom_call" | custom-call | flops 905969664 | bytes 5459968 | tf_op jit(solution)/shard_map/pallas_call | solution.py:34
  18.6 0.6 collective-permute-start.4
  19.2 0.1 shard_map.84
  19.3 4.3 %collective-permute-start.6 = (bf16[16,3456]{1,0:T(8,128)(2,1)S(1)}, bf16[16,3456]{1,0:T(8,128)(2,1)S(1)}, u32[]{:S(2)}, u32[]{:S(2)}) collective-permute-start(bf16[16,3456]{1,0:T(8,128)(2,1)S(1)} %get-tuple-element.69), channel_id=1, source_target_pairs={{0,1},{1,0},{2,3},{3,2},{4,5},{5,4},{6,7},{7,6},{8,9},{9,8},{10,11... | collective-permute-start | bytes 331784 | tf_op jit(solution)/shard_map/ppermute | solution.py:408
  23.6 0.8 %collective-permute-start.7 = (bf16[16,3456]{1,0:T(8,128)(2,1)S(1)}, bf16[16,3456]{1,0:T(8,128)(2,1)S(1)}, u32[]{:S(2)}, u32[]{:S(2)}) collective-permute-start(bf16[16,3456]{1,0:T(8,128)(2,1)S(1)} %get-tuple-element.70), channel_id=1, source_target_pairs={{0,2},{1,3},{2,0},{3,1},{4,6},{5,7},{6,4},{7,5},{8,10},{9,11},{10,... | collective-permute-start | bytes 331784 | tf_op jit(solution)/shard_map/ppermute | solution.py:408
  24.4 1.4 %collective-permute-start.8 = (bf16[16,3456]{1,0:T(8,128)(2,1)S(1)}, bf16[16,3456]{1,0:T(8,128)(2,1)S(1)}, u32[]{:S(2)}, u32[]{:S(2)}) collective-permute-start(bf16[16,3456]{1,0:T(8,128)(2,1)S(1)} %get-tuple-element.71), channel_id=1, source_target_pairs={{0,3},{1,2},{2,1},{3,0},{4,7},{5,6},{6,5},{7,4},{8,11},{9,10},{10,... | collective-permute-start | bytes 331784 | tf_op jit(solution)/shard_map/ppermute | solution.py:408
  25.7 0.0 collective-permute-done.4.got
  25.7 0.1 shard_map.83
  25.8 2.1 %collective-permute-start.10 = (bf16[16,3456]{1,0:T(8,128)(2,1)S(1)}, bf16[16,3456]{1,0:T(8,128)(2,1)S(1)}, u32[]{:S(2)}, u32[]{:S(2)}) collective-permute-start(bf16[16,3456]{1,0:T(8,128)(2,1)S(1)} %get-tuple-element.74), channel_id=1, source_target_pairs={{0,2},{1,3},{2,0},{3,1},{4,6},{5,7},{6,4},{7,5},{8,10},{9,11},{10,... | collective-permute-start | bytes 331784 | tf_op jit(solution)/shard_map/ppermute | solution.py:408
  27.9 0.7 %collective-permute-start.11 = (bf16[16,3456]{1,0:T(8,128)(2,1)S(1)}, bf16[16,3456]{1,0:T(8,128)(2,1)S(1)}, u32[]{:S(2)}, u32[]{:S(2)}) collective-permute-start(bf16[16,3456]{1,0:T(8,128)(2,1)S(1)} %get-tuple-element.75), channel_id=1, source_target_pairs={{0,3},{1,2},{2,1},{3,0},{4,7},{5,6},{6,5},{7,4},{8,11},{9,10},{10,... | collective-permute-start | bytes 331784 | tf_op jit(solution)/shard_map/ppermute | solution.py:408
  28.7 0.0 collective-permute-done.6.refs_1_
  28.7 0.8 %collective-permute-start.9 = (bf16[16,3456]{1,0:T(8,128)(2,1)S(1)}, bf16[16,3456]{1,0:T(8,128)(2,1)S(1)}, u32[]{:S(2)}, u32[]{:S(2)}) collective-permute-start(bf16[16,3456]{1,0:T(8,128)(2,1)S(1)} %get-tuple-element.73), channel_id=1, source_target_pairs={{0,1},{1,0},{2,3},{3,2},{4,5},{5,4},{6,7},{7,6},{8,9},{9,8},{10,11... | collective-permute-start | bytes 331784 | tf_op jit(solution)/shard_map/ppermute | solution.py:408
  29.5 0.0 collective-permute-done.7.refs_2_
  29.5 2.5 %collective-permute-done.8.refs_3_ = bf16[16,3456]{1,0:T(8,128)(2,1)S(1)} collective-permute-done((bf16[16,3456]{1,0:T(8,128)(2,1)S(1)}, bf16[16,3456]{1,0:T(8,128)(2,1)S(1)}, u32[]{:S(2)}, u32[]{:S(2)}) %collective-permute-start.8) | collective-permute-done | bytes 110624 | tf_op jit(solution)/shard_map/ppermute | solution.py:408
  32.0 0.1 shard_map.85.one
  32.1 4.7 %collective-permute-start.12 = (bf16[16,3456]{1,0:T(8,128)(2,1)S(1)}, bf16[16,3456]{1,0:T(8,128)(2,1)S(1)}, u32[]{:S(2)}, u32[]{:S(2)}) collective-permute-start(bf16[16,3456]{1,0:T(8,128)(2,1)S(1)} %shard_map.85.one), channel_id=1, source_target_pairs={{0,4},{1,5},{2,6},{3,7},{4,0},{5,1},{6,2},{7,3},{8,12},{9,13},{10,... | collective-permute-start | bytes 331784 | tf_op jit(solution)/shard_map/ppermute | solution.py:408
  36.7 0.0 collective-permute-done.10.refs_2_
  36.7 0.0 collective-permute-done.11.refs_3_
  36.7 0.0 collective-permute-done.9.refs_1_
  36.7 0.1 shard_map.86.one
  36.8 3.5 %collective-permute-start.13 = (bf16[16,3456]{1,0:T(8,128)(2,1)S(1)}, bf16[16,3456]{1,0:T(8,128)(2,1)S(1)}, u32[]{:S(2)}, u32[]{:S(2)}) collective-permute-start(bf16[16,3456]{1,0:T(8,128)(2,1)S(1)} %shard_map.86.one), channel_id=1, source_target_pairs={{0,4},{1,5},{2,6},{3,7},{4,0},{5,1},{6,2},{7,3},{8,12},{9,13},{10,... | collective-permute-start | bytes 331784 | tf_op jit(solution)/shard_map/ppermute | solution.py:408
  40.3 0.0 collective-permute-done.12.two
  40.4 2.6 %collective-permute-start.14 = (bf16[16,3456]{1,0:T(8,128)(2,1)S(1)}, bf16[16,3456]{1,0:T(8,128)(2,1)S(1)}, u32[]{:S(2)}, u32[]{:S(2)}) collective-permute-start(bf16[16,3456]{1,0:T(8,128)(2,1)S(1)} %shard_map.87.one), channel_id=1, source_target_pairs={{0,8},{1,9},{2,10},{3,11},{4,12},{5,13},{6,14},{7,15},{8,0},{9,1},... | collective-permute-start | bytes 331784 | tf_op jit(solution)/shard_map/ppermute | solution.py:408
  43.0 1.5 %shard_map.88 = bf16[512,128]{1,0:T(8,128)(2,1)} custom-call(bf16[512,1152]{1,0:T(8,128)(2,1)S(1)} %get-tuple-element.78.st_own, bf16[512,128]{1,0:T(8,128)(2,1)S(1)} %get-tuple-element.46.grads, bf16[48,128]{1,0:T(8,128)(2,1)S(1)} %get-tuple-element.55.marks3, bf16[384,1152]{1,0:T(8,128)(2,1)S(1)} %get-tuple-element.44.w1_wide), custom_call_target="tpu_custom_call" | custom-call | flops 452984832 | bytes 2338816 | tf_op jit(solution)/shard_map/pallas_call | solution.py:34
  44.5 0.0 collective-permute-done.13.two
  44.5 3.3 %collective-permute-start.15 = (bf16[16,3456]{1,0:T(8,128)(2,1)S(1)}, bf16[16,3456]{1,0:T(8,128)(2,1)S(1)}, u32[]{:S(2)}, u32[]{:S(2)}) collective-permute-start(bf16[16,3456]{1,0:T(8,128)(2,1)S(1)} %shard_map.89.one), channel_id=1, source_target_pairs={{0,8},{1,9},{2,10},{3,11},{4,12},{5,13},{6,14},{7,15},{8,0},{9,1},... | collective-permute-start | bytes 331784 | tf_op jit(solution)/shard_map/ppermute | solution.py:408
  47.9 1.0 %collective-permute-start.20 = (bf16[16,3456]{1,0:T(8,128)(2,1)S(1)}, bf16[16,3456]{1,0:T(8,128)(2,1)S(1)}, u32[]{:S(2)}, u32[]{:S(2)}) collective-permute-start(bf16[16,3456]{1,0:T(8,128)(2,1)S(1)} %shard_map.90.refs_0_), channel_id=1, source_target_pairs={{0,1},{1,0},{2,3},{3,2},{4,5},{5,4},{6,7},{7,6},{8,9},{9,8},{10,11... | collective-permute-start | bytes 331784 | tf_op jit(solution)/shard_map/ppermute | solution.py:408
  48.8 1.3 %collective-permute-start.21 = (bf16[16,3456]{1,0:T(8,128)(2,1)S(1)}, bf16[16,3456]{1,0:T(8,128)(2,1)S(1)}, u32[]{:S(2)}, u32[]{:S(2)}) collective-permute-start(bf16[16,3456]{1,0:T(8,128)(2,1)S(1)} %shard_map.90.refs_0_), channel_id=1, source_target_pairs={{0,2},{1,3},{2,0},{3,1},{4,6},{5,7},{6,4},{7,5},{8,10},{9,11},{10,... | collective-permute-start | bytes 331784 | tf_op jit(solution)/shard_map/ppermute | solution.py:408
  50.2 1.3 %collective-permute-start.22 = (bf16[16,3456]{1,0:T(8,128)(2,1)S(1)}, bf16[16,3456]{1,0:T(8,128)(2,1)S(1)}, u32[]{:S(2)}, u32[]{:S(2)}) collective-permute-start(bf16[16,3456]{1,0:T(8,128)(2,1)S(1)} %shard_map.90.refs_0_), channel_id=1, source_target_pairs={{0,3},{1,2},{2,1},{3,0},{4,7},{5,6},{6,5},{7,4},{8,11},{9,10},{10,... | collective-permute-start | bytes 331784 | tf_op jit(solution)/shard_map/ppermute | solution.py:408
  51.4 0.3 collective-permute-done.15.two
  51.8 1.0 %collective-permute-start.16 = (bf16[16,3456]{1,0:T(8,128)(2,1)S(1)}, bf16[16,3456]{1,0:T(8,128)(2,1)S(1)}, u32[]{:S(2)}, u32[]{:S(2)}) collective-permute-start(bf16[16,3456]{1,0:T(8,128)(2,1)S(1)} %shard_map.91.refs_0_), channel_id=1, source_target_pairs={{0,1},{1,0},{2,3},{3,2},{4,5},{5,4},{6,7},{7,6},{8,9},{9,8},{10,11... | collective-permute-start | bytes 331784 | tf_op jit(solution)/shard_map/ppermute | solution.py:408
  52.7 1.0 %collective-permute-start.17 = (bf16[16,3456]{1,0:T(8,128)(2,1)S(1)}, bf16[16,3456]{1,0:T(8,128)(2,1)S(1)}, u32[]{:S(2)}, u32[]{:S(2)}) collective-permute-start(bf16[16,3456]{1,0:T(8,128)(2,1)S(1)} %shard_map.91.refs_0_), channel_id=1, source_target_pairs={{0,2},{1,3},{2,0},{3,1},{4,6},{5,7},{6,4},{7,5},{8,10},{9,11},{10,... | collective-permute-start | bytes 331784 | tf_op jit(solution)/shard_map/ppermute | solution.py:408
  53.7 1.8 %collective-permute-start.18 = (bf16[16,3456]{1,0:T(8,128)(2,1)S(1)}, bf16[16,3456]{1,0:T(8,128)(2,1)S(1)}, u32[]{:S(2)}, u32[]{:S(2)}) collective-permute-start(bf16[16,3456]{1,0:T(8,128)(2,1)S(1)} %shard_map.91.refs_0_), channel_id=1, source_target_pairs={{0,3},{1,2},{2,1},{3,0},{4,7},{5,6},{6,5},{7,4},{8,11},{9,10},{10,... | collective-permute-start | bytes 331784 | tf_op jit(solution)/shard_map/ppermute | solution.py:408
  55.6 1.0 %collective-permute-done.21.refs_2_ = bf16[16,3456]{1,0:T(8,128)(2,1)S(1)} collective-permute-done((bf16[16,3456]{1,0:T(8,128)(2,1)S(1)}, bf16[16,3456]{1,0:T(8,128)(2,1)S(1)}, u32[]{:S(2)}, u32[]{:S(2)}) %collective-permute-start.21) | collective-permute-done | bytes 110624 | tf_op jit(solution)/shard_map/ppermute | solution.py:408
  56.5 0.6 collective-permute-done.22.refs_3_
  57.1 0.1 collective-permute-start.23
  57.2 1.4 %collective-permute-done.16.refs_1_ = bf16[16,3456]{1,0:T(8,128)(2,1)S(1)} collective-permute-done((bf16[16,3456]{1,0:T(8,128)(2,1)S(1)}, bf16[16,3456]{1,0:T(8,128)(2,1)S(1)}, u32[]{:S(2)}, u32[]{:S(2)}) %collective-permute-start.16) | collective-permute-done | bytes 110624 | tf_op jit(solution)/shard_map/ppermute | solution.py:408
  58.6 2.1 %collective-permute-done.17.refs_2_ = bf16[16,3456]{1,0:T(8,128)(2,1)S(1)} collective-permute-done((bf16[16,3456]{1,0:T(8,128)(2,1)S(1)}, bf16[16,3456]{1,0:T(8,128)(2,1)S(1)}, u32[]{:S(2)}, u32[]{:S(2)}) %collective-permute-start.17) | collective-permute-done | bytes 110624 | tf_op jit(solution)/shard_map/ppermute | solution.py:408
  60.7 0.0 collective-permute-done.18.refs_3_
  60.7 0.1 collective-permute-start.19
  60.8 0.0 collective-permute-done.23.other
  60.8 1.3 %shard_map.95 = f32[3456,128]{1,0:T(8,128)} custom-call(bf16[64,3456]{1,0:T(8,128)(2,1)S(1)} %shard_map.94.own, bf16[64,3456]{1,0:T(8,128)(2,1)S(1)} %collective-permute-done.23.other), custom_call_target="tpu_custom_call" | custom-call | bytes 2654208 | tf_op jit(solution)/shard_map/pallas_call | solution.py:34
  62.2 0.4 collective-permute-done.19.other
  62.6 1.3 %shard_map.93 = f32[3456,128]{1,0:T(8,128)} custom-call(bf16[64,3456]{1,0:T(8,128)(2,1)S(1)} %shard_map.92.own, bf16[64,3456]{1,0:T(8,128)(2,1)S(1)} %collective-permute-done.19.other), custom_call_target="tpu_custom_call" | custom-call | bytes 2654208 | tf_op jit(solution)/shard_map/pallas_call | solution.py:34
  (12 shorter events, 0.2 us)
Async XLA Ops:
  1.3 0.9 %copy-start.2 = (bf16[1,512,128]{2,1,0:T(8,128)(2,1)S(1)}, bf16[1,512,128]{2,1,0:T(8,128)(2,1)}, u32[]{:S(2)}) copy-start(bf16[1,512,128]{2,1,0:T(8,128)(2,1)} %param.5) | copy-start | bytes 393220
  2.2 0.9 %copy-start.3 = (bf16[1,512,128]{2,1,0:T(8,128)(2,1)S(1)}, bf16[1,512,128]{2,1,0:T(8,128)(2,1)}, u32[]{:S(2)}) copy-start(bf16[1,512,128]{2,1,0:T(8,128)(2,1)} %param.9) | copy-start | bytes 393220
  3.2 6.6 %collective-permute-start = (bf16[272,128]{1,0:T(8,128)(2,1)S(1)}, bf16[272,128]{1,0:T(8,128)(2,1)S(1)}, u32[]{:S(2)}, u32[]{:S(2)}) collective-permute-start(bf16[272,128]{1,0:T(8,128)(2,1)S(1)} %get-tuple-element.48), channel_id=1, source_target_pairs={{0,1},{1,0},{2,3},{3,2},{4,5},{5,4},{6,7},{7,6},{8,9},{9,8},{10,11... | collective-permute-start | bytes 208904 | tf_op jit(solution)/shard_map/ppermute | solution.py:611
  6.2 3.6 %collective-permute-start.1 = (bf16[272,128]{1,0:T(8,128)(2,1)S(1)}, bf16[272,128]{1,0:T(8,128)(2,1)S(1)}, u32[]{:S(2)}, u32[]{:S(2)}) collective-permute-start(bf16[272,128]{1,0:T(8,128)(2,1)S(1)} %get-tuple-element.49), channel_id=1, source_target_pairs={{1,2},{2,1},{5,6},{6,5},{9,10},{10,9},{13,14},{14,13},{17,18},{18,... | collective-permute-start | bytes 208904 | tf_op jit(solution)/shard_map/ppermute | solution.py:611
  6.9 1.2 %copy-start = (bf16[3456,128]{1,0:T(8,128)(2,1)S(1)}, bf16[3456,128]{1,0:T(8,128)(2,1)}, u32[]{:S(2)}) copy-start(bf16[3456,128]{1,0:T(8,128)(2,1)} %src.3) | copy-start | bytes 2654212
  8.4 1.2 %copy-start.1 = (bf16[3456,128]{1,0:T(8,128)(2,1)S(1)}, bf16[3456,128]{1,0:T(8,128)(2,1)}, u32[]{:S(2)}) copy-start(bf16[3456,128]{1,0:T(8,128)(2,1)} %src.2) | copy-start | bytes 2654212
  9.9 4.8 %collective-permute-start.2 = (bf16[432,128]{1,0:T(8,128)(2,1)S(1)}, bf16[432,128]{1,0:T(8,128)(2,1)S(1)}, u32[]{:S(2)}, u32[]{:S(2)}) collective-permute-start(bf16[432,128]{1,0:T(8,128)(2,1)S(1)} %get-tuple-element.56), channel_id=1, source_target_pairs={{0,4},{4,0},{1,5},{5,1},{2,6},{6,2},{3,7},{7,3},{8,12},{12,8},{9,1... | collective-permute-start | bytes 331784 | tf_op jit(solution)/shard_map/ppermute | solution.py:611
  11.6 3.2 %collective-permute-start.3 = (bf16[432,128]{1,0:T(8,128)(2,1)S(1)}, bf16[432,128]{1,0:T(8,128)(2,1)S(1)}, u32[]{:S(2)}, u32[]{:S(2)}) collective-permute-start(bf16[432,128]{1,0:T(8,128)(2,1)S(1)} %get-tuple-element.57), channel_id=1, source_target_pairs={{4,8},{8,4},{5,9},{9,5},{6,10},{10,6},{7,11},{11,7},{20,24},{24,20... | collective-permute-start | bytes 331784 | tf_op jit(solution)/shard_map/ppermute | solution.py:611
  16.7 2.4 %collective-permute-start.5 = (bf16[64,3456]{1,0:T(8,128)(2,1)S(1)}, bf16[64,3456]{1,0:T(8,128)(2,1)S(1)}, u32[]{:S(2)}, u32[]{:S(2)}) collective-permute-start(bf16[64,3456]{1,0:T(8,128)(2,1)S(1)} %get-tuple-element.66), channel_id=1, source_target_pairs={{0,16},{16,0},{1,17},{17,1},{2,18},{18,2},{3,19},{19,3},{4,20},{20... | collective-permute-start | bytes 1327112 | tf_op jit(solution)/shard_map/ppermute | solution.py:398
  18.6 7.1 %collective-permute-start.4 = (bf16[64,3456]{1,0:T(8,128)(2,1)S(1)}, bf16[64,3456]{1,0:T(8,128)(2,1)S(1)}, u32[]{:S(2)}, u32[]{:S(2)}) collective-permute-start(bf16[64,3456]{1,0:T(8,128)(2,1)S(1)} %get-tuple-element.63), channel_id=1, source_target_pairs={{0,16},{16,0},{1,17},{17,1},{2,18},{18,2},{3,19},{19,3},{4,20},{20... | collective-permute-start | bytes 1327112 | tf_op jit(solution)/shard_map/ppermute | solution.py:398
  19.3 9.4 %collective-permute-start.6 = (bf16[16,3456]{1,0:T(8,128)(2,1)S(1)}, bf16[16,3456]{1,0:T(8,128)(2,1)S(1)}, u32[]{:S(2)}, u32[]{:S(2)}) collective-permute-start(bf16[16,3456]{1,0:T(8,128)(2,1)S(1)} %get-tuple-element.69), channel_id=1, source_target_pairs={{0,1},{1,0},{2,3},{3,2},{4,5},{5,4},{6,7},{7,6},{8,9},{9,8},{10,11... | collective-permute-start | bytes 331784 | tf_op jit(solution)/shard_map/ppermute | solution.py:408
  23.6 5.9 %collective-permute-start.7 = (bf16[16,3456]{1,0:T(8,128)(2,1)S(1)}, bf16[16,3456]{1,0:T(8,128)(2,1)S(1)}, u32[]{:S(2)}, u32[]{:S(2)}) collective-permute-start(bf16[16,3456]{1,0:T(8,128)(2,1)S(1)} %get-tuple-element.70), channel_id=1, source_target_pairs={{0,2},{1,3},{2,0},{3,1},{4,6},{5,7},{6,4},{7,5},{8,10},{9,11},{10,... | collective-permute-start | bytes 331784 | tf_op jit(solution)/shard_map/ppermute | solution.py:408
  24.4 7.6 %collective-permute-start.8 = (bf16[16,3456]{1,0:T(8,128)(2,1)S(1)}, bf16[16,3456]{1,0:T(8,128)(2,1)S(1)}, u32[]{:S(2)}, u32[]{:S(2)}) collective-permute-start(bf16[16,3456]{1,0:T(8,128)(2,1)S(1)} %get-tuple-element.71), channel_id=1, source_target_pairs={{0,3},{1,2},{2,1},{3,0},{4,7},{5,6},{6,5},{7,4},{8,11},{9,10},{10,... | collective-permute-start | bytes 331784 | tf_op jit(solution)/shard_map/ppermute | solution.py:408
  25.8 10.9 %collective-permute-start.10 = (bf16[16,3456]{1,0:T(8,128)(2,1)S(1)}, bf16[16,3456]{1,0:T(8,128)(2,1)S(1)}, u32[]{:S(2)}, u32[]{:S(2)}) collective-permute-start(bf16[16,3456]{1,0:T(8,128)(2,1)S(1)} %get-tuple-element.74), channel_id=1, source_target_pairs={{0,2},{1,3},{2,0},{3,1},{4,6},{5,7},{6,4},{7,5},{8,10},{9,11},{10,... | collective-permute-start | bytes 331784 | tf_op jit(solution)/shard_map/ppermute | solution.py:408
  27.9 8.8 %collective-permute-start.11 = (bf16[16,3456]{1,0:T(8,128)(2,1)S(1)}, bf16[16,3456]{1,0:T(8,128)(2,1)S(1)}, u32[]{:S(2)}, u32[]{:S(2)}) collective-permute-start(bf16[16,3456]{1,0:T(8,128)(2,1)S(1)} %get-tuple-element.75), channel_id=1, source_target_pairs={{0,3},{1,2},{2,1},{3,0},{4,7},{5,6},{6,5},{7,4},{8,11},{9,10},{10,... | collective-permute-start | bytes 331784 | tf_op jit(solution)/shard_map/ppermute | solution.py:408
  28.7 8.1 %collective-permute-start.9 = (bf16[16,3456]{1,0:T(8,128)(2,1)S(1)}, bf16[16,3456]{1,0:T(8,128)(2,1)S(1)}, u32[]{:S(2)}, u32[]{:S(2)}) collective-permute-start(bf16[16,3456]{1,0:T(8,128)(2,1)S(1)} %get-tuple-element.73), channel_id=1, source_target_pairs={{0,1},{1,0},{2,3},{3,2},{4,5},{5,4},{6,7},{7,6},{8,9},{9,8},{10,11... | collective-permute-start | bytes 331784 | tf_op jit(solution)/shard_map/ppermute | solution.py:408
  32.1 8.3 %collective-permute-start.12 = (bf16[16,3456]{1,0:T(8,128)(2,1)S(1)}, bf16[16,3456]{1,0:T(8,128)(2,1)S(1)}, u32[]{:S(2)}, u32[]{:S(2)}) collective-permute-start(bf16[16,3456]{1,0:T(8,128)(2,1)S(1)} %shard_map.85.one), channel_id=1, source_target_pairs={{0,4},{1,5},{2,6},{3,7},{4,0},{5,1},{6,2},{7,3},{8,12},{9,13},{10,... | collective-permute-start | bytes 331784 | tf_op jit(solution)/shard_map/ppermute | solution.py:408
  36.8 7.7 %collective-permute-start.13 = (bf16[16,3456]{1,0:T(8,128)(2,1)S(1)}, bf16[16,3456]{1,0:T(8,128)(2,1)S(1)}, u32[]{:S(2)}, u32[]{:S(2)}) collective-permute-start(bf16[16,3456]{1,0:T(8,128)(2,1)S(1)} %shard_map.86.one), channel_id=1, source_target_pairs={{0,4},{1,5},{2,6},{3,7},{4,0},{5,1},{6,2},{7,3},{8,12},{9,13},{10,... | collective-permute-start | bytes 331784 | tf_op jit(solution)/shard_map/ppermute | solution.py:408
  40.4 7.4 %collective-permute-start.14 = (bf16[16,3456]{1,0:T(8,128)(2,1)S(1)}, bf16[16,3456]{1,0:T(8,128)(2,1)S(1)}, u32[]{:S(2)}, u32[]{:S(2)}) collective-permute-start(bf16[16,3456]{1,0:T(8,128)(2,1)S(1)} %shard_map.87.one), channel_id=1, source_target_pairs={{0,8},{1,9},{2,10},{3,11},{4,12},{5,13},{6,14},{7,15},{8,0},{9,1},... | collective-permute-start | bytes 331784 | tf_op jit(solution)/shard_map/ppermute | solution.py:408
  44.5 7.2 %collective-permute-start.15 = (bf16[16,3456]{1,0:T(8,128)(2,1)S(1)}, bf16[16,3456]{1,0:T(8,128)(2,1)S(1)}, u32[]{:S(2)}, u32[]{:S(2)}) collective-permute-start(bf16[16,3456]{1,0:T(8,128)(2,1)S(1)} %shard_map.89.one), channel_id=1, source_target_pairs={{0,8},{1,9},{2,10},{3,11},{4,12},{5,13},{6,14},{7,15},{8,0},{9,1},... | collective-permute-start | bytes 331784 | tf_op jit(solution)/shard_map/ppermute | solution.py:408
  47.9 5.9 %collective-permute-start.20 = (bf16[16,3456]{1,0:T(8,128)(2,1)S(1)}, bf16[16,3456]{1,0:T(8,128)(2,1)S(1)}, u32[]{:S(2)}, u32[]{:S(2)}) collective-permute-start(bf16[16,3456]{1,0:T(8,128)(2,1)S(1)} %shard_map.90.refs_0_), channel_id=1, source_target_pairs={{0,1},{1,0},{2,3},{3,2},{4,5},{5,4},{6,7},{7,6},{8,9},{9,8},{10,11... | collective-permute-start | bytes 331784 | tf_op jit(solution)/shard_map/ppermute | solution.py:408
  48.8 7.7 %collective-permute-start.21 = (bf16[16,3456]{1,0:T(8,128)(2,1)S(1)}, bf16[16,3456]{1,0:T(8,128)(2,1)S(1)}, u32[]{:S(2)}, u32[]{:S(2)}) collective-permute-start(bf16[16,3456]{1,0:T(8,128)(2,1)S(1)} %shard_map.90.refs_0_), channel_id=1, source_target_pairs={{0,2},{1,3},{2,0},{3,1},{4,6},{5,7},{6,4},{7,5},{8,10},{9,11},{10,... | collective-permute-start | bytes 331784 | tf_op jit(solution)/shard_map/ppermute | solution.py:408
  50.2 6.9 %collective-permute-start.22 = (bf16[16,3456]{1,0:T(8,128)(2,1)S(1)}, bf16[16,3456]{1,0:T(8,128)(2,1)S(1)}, u32[]{:S(2)}, u32[]{:S(2)}) collective-permute-start(bf16[16,3456]{1,0:T(8,128)(2,1)S(1)} %shard_map.90.refs_0_), channel_id=1, source_target_pairs={{0,3},{1,2},{2,1},{3,0},{4,7},{5,6},{6,5},{7,4},{8,11},{9,10},{10,... | collective-permute-start | bytes 331784 | tf_op jit(solution)/shard_map/ppermute | solution.py:408
  51.8 6.8 %collective-permute-start.16 = (bf16[16,3456]{1,0:T(8,128)(2,1)S(1)}, bf16[16,3456]{1,0:T(8,128)(2,1)S(1)}, u32[]{:S(2)}, u32[]{:S(2)}) collective-permute-start(bf16[16,3456]{1,0:T(8,128)(2,1)S(1)} %shard_map.91.refs_0_), channel_id=1, source_target_pairs={{0,1},{1,0},{2,3},{3,2},{4,5},{5,4},{6,7},{7,6},{8,9},{9,8},{10,11... | collective-permute-start | bytes 331784 | tf_op jit(solution)/shard_map/ppermute | solution.py:408
  52.7 7.9 %collective-permute-start.17 = (bf16[16,3456]{1,0:T(8,128)(2,1)S(1)}, bf16[16,3456]{1,0:T(8,128)(2,1)S(1)}, u32[]{:S(2)}, u32[]{:S(2)}) collective-permute-start(bf16[16,3456]{1,0:T(8,128)(2,1)S(1)} %shard_map.91.refs_0_), channel_id=1, source_target_pairs={{0,2},{1,3},{2,0},{3,1},{4,6},{5,7},{6,4},{7,5},{8,10},{9,11},{10,... | collective-permute-start | bytes 331784 | tf_op jit(solution)/shard_map/ppermute | solution.py:408
  53.7 7.0 %collective-permute-start.18 = (bf16[16,3456]{1,0:T(8,128)(2,1)S(1)}, bf16[16,3456]{1,0:T(8,128)(2,1)S(1)}, u32[]{:S(2)}, u32[]{:S(2)}) collective-permute-start(bf16[16,3456]{1,0:T(8,128)(2,1)S(1)} %shard_map.91.refs_0_), channel_id=1, source_target_pairs={{0,3},{1,2},{2,1},{3,0},{4,7},{5,6},{6,5},{7,4},{8,11},{9,10},{10,... | collective-permute-start | bytes 331784 | tf_op jit(solution)/shard_map/ppermute | solution.py:408
  57.1 3.7 %collective-permute-start.23 = (bf16[64,3456]{1,0:T(8,128)(2,1)S(1)}, bf16[64,3456]{1,0:T(8,128)(2,1)S(1)}, u32[]{:S(2)}, u32[]{:S(2)}) collective-permute-start(bf16[64,3456]{1,0:T(8,128)(2,1)S(1)} %shard_map.94.own), channel_id=1, source_target_pairs={{0,16},{16,0},{1,17},{17,1},{2,18},{18,2},{3,19},{19,3},{4,20},{20... | collective-permute-start | bytes 1327112 | tf_op jit(solution)/shard_map/ppermute | solution.py:398
  60.7 1.9 %collective-permute-start.19 = (bf16[64,3456]{1,0:T(8,128)(2,1)S(1)}, bf16[64,3456]{1,0:T(8,128)(2,1)S(1)}, u32[]{:S(2)}, u32[]{:S(2)}) collective-permute-start(bf16[64,3456]{1,0:T(8,128)(2,1)S(1)} %shard_map.92.own), channel_id=1, source_target_pairs={{0,16},{16,0},{1,17},{17,1},{2,18},{18,2},{3,19},{19,3},{4,20},{20... | collective-permute-start | bytes 1327112 | tf_op jit(solution)/shard_map/ppermute | solution.py:398

commit v3 on v2

--- a/solution.py
+++ b/solution.py
@@ -50,7 +50,7 @@
     return lax.axis_index("blk") // stride % 2
 
 
-def pack_depth(planes, tile_of, mask_rows, mask, feat, cot, inp, grads, marks, even, odd, wide):
+def pack_depth(planes, tile_of, mask_rows, mask, both, inp, grads, marks, even, odd, wide):
     lines = planes * TILE
     row = lax.broadcasted_iota(jnp.int32, (mask_rows, 128), 0)
     filled = jnp.zeros((mask_rows, 128), F32)
@@ -62,10 +62,10 @@
     even[4 * lines :, :] = filled
     odd[4 * lines :, :] = filled
     side = parity(1)
-    for at, (src, dst) in enumerate(((feat, inp), (cot, grads))):
+    for at, dst in enumerate((inp, grads)):
         for e in range(planes):
             rows = slice(e * FACE, (e + 1) * FACE)
-            kept = src[rows, :].astype(F32) * kept_of[e]
+            kept = both[at, rows, :].astype(F32) * kept_of[e]
             wide[rows, :] = kept
             dst[rows, :] = kept.astype(BF)
 
@@ -85,7 +85,7 @@
 
 
 def pack_lines(
-    planes, mask_rows, inp, grads, marks, z_even, z_odd, even, odd, deep_in, deep_g, marks3
+    planes, mask_rows, inp, grads, marks, z_odd, z_even, even, odd, deep_in, deep_g, marks3
 ):
     lines = planes * TILE
     plane = TILE * GROWN
@@ -224,12 +224,12 @@
     @pl.when(core == 0)
     def _():
         kept[:, columns] = value[:half]
-        sent[:, columns] = value[half:].astype(BF)
+        sent[:, columns] = value[half:]
 
     @pl.when(core == 1)
     def _():
         kept[:, columns] = value[half:]
-        sent[:, columns] = value[:half].astype(BF)
+        sent[:, columns] = value[:half]
 
 
 def marked(planes, mask_rows, marks3, y_even, y_odd):
@@ -311,7 +311,7 @@
 
 def forward(
     planes, deep, mask_rows,
-    deep_in, deep_g, marks3, y_even, y_odd, inner, w1_tall,
+    deep_in, deep_g, marks3, y_odd, y_even, inner, w1_tall,
     kept, sent, act, grid_g,
     grid_in, outer, pair, single, st_own, hidden,
 ):
@@ -409,7 +409,7 @@
 
 
 def turned(k):
-    return {0: 0, 1: 1 + lax.axis_index("dp"), 2: 2 - lax.axis_index("dp"), 3: 3}[k]
+    return {0: 0, 1: 3, 2: 1 + lax.axis_index("dp"), 3: 2 - lax.axis_index("dp")}[k]
 
 
 def split_rows(parts, kept, got, own, *sent):
@@ -443,6 +443,15 @@
     out[...] = (one[...].astype(F32) + two[...].astype(F32)).astype(BF)
 
 
+def lay_rows(one, two, out, wide):
+    rows = one.shape[0]
+    for tap in range(TAPS):
+        columns = slice(tap * 128, (tap + 1) * 128)
+        total = one[:, columns].astype(F32) + two[:, columns].astype(F32)
+        wide[pl.ds(tap, rows, stride=TAPS), :] = total
+    out[...] = wide[...].astype(BF)
+
+
 def add_all(parts, *refs):
     value = refs[0][...]
     for ref in refs[1:parts]:
@@ -470,20 +479,15 @@
     core = lax.axis_index("dp")
     half = own.shape[0]
 
-    def write(low, high):
-        for at, ref in ((0, low), (half, high)):
-            for tap in range(TAPS):
-                out[pl.ds(at * TAPS + tap, half, stride=TAPS), :] = ref[
-                    :, tap * 128 : (tap + 1) * 128
-                ].astype(F32)
-
     @pl.when(core == 0)
     def _():
-        write(own, other)
+        out[:half, :] = own[...].astype(F32)
+        out[half:, :] = other[...].astype(F32)
 
     @pl.when(core == 1)
     def _():
-        write(other, own)
+        out[:half, :] = other[...].astype(F32)
+        out[half:, :] = own[...].astype(F32)
 
 
 def after(value, *others):
@@ -491,7 +495,7 @@
 
 
 def near(values):
-    return [cross(v, bits) for v, bits in zip(values, ((1, 2), (2, 1), (3, 3)))]
+    return [cross(v, bits) for v, bits in zip(values, ((3, 3), (1, 2), (2, 1)))]
 
 
 def far(values):
@@ -511,6 +515,11 @@
 def sum_stage(own, gots):
     parts = len(gots) + 1
     return call(functools.partial(add_all, parts), [shape(own.shape, BF)], [own] + gots)[0]
+
+
+def laid_pair(value, got):
+    laid = (value.shape[0] * TAPS, 128)
+    return call(lay_rows, [shape(laid, BF)], [value, got], scratch=[pltpu.VMEM(laid, F32)])[0]
 
 
 def pair_stage(value, got):
@@ -542,25 +551,27 @@
 
 
 def finished(mine, other):
-    return call(finish, [shape((2 * mine.shape[0] * TAPS, 128), F32)], [mine, other])[0]
+    return call(finish, [shape((2 * mine.shape[0], 128), F32)], [mine, other])[0]
 
 
 def across(owns, gots, beside):
     outer = lax.axis_size("blk") // INNER
     if outer > 4:
-        one, two = [wide_sum(own, got) for own, got in zip(owns, gots)]
+        sums = [wide_sum(own, got) for own, got in zip(owns, gots)]
+        one, two = [laid_pair(value, jnp.zeros_like(value)) for value in sums]
         return one, two, beside(one)
     one = sum_stage(owns[0], gots[0])
     two = sum_stage(after(owns[1], one), gots[1])
     steps = [INNER << k for k in range(outer.bit_length() - 1)]
     other = None
     for bits in zip(steps, reversed(steps)):
+        add = laid_pair if bits[0] == steps[-1] else pair_stage
         got_one, got_two = cross(one, bits), cross(two, bits)
-        one = pair_stage(after(one, two), got_one)
+        one = add(after(one, two), got_one)
         if other is None:
             other = beside(one)
             two = after(two, other)
-        two = pair_stage(after(two, one), got_two)
+        two = add(after(two, one), got_two)
     return one, two, other
 
 
@@ -619,7 +630,7 @@
         [shape((cells, width), BF)] * 2
         + [shape((mask_rows, width), BF)]
         + [shape((side, width), BF)] * 2,
-        [mask, feat, cot],
+        [mask, jnp.stack([feat, cot])],
         scratch=[pltpu.VMEM((cells, width), F32)],
         smem=(0,),
     )
@@ -639,7 +650,7 @@
         [shape((edge, width), BF)] * 2
         + [shape((lines * GROWN + SPARE, width), F32)] * 2
         + [shape((3 * mask_rows, width), BF)],
-        [inp, grads, marks, z_even, z_odd],
+        [inp, grads, marks, z_odd, z_even],
     )
     y_even, y_odd = beside(even, odd, 4, 4)
     outer = count // INNER
@@ -648,7 +659,7 @@
     n_out = size_x + 2 * deep
     half = width // 2
     work = 2 * size_x * FACE * TAPS * width * width
-    terms = [shape((half, columns), F32), shape((half, columns), BF)]
+    terms = [shape((half, columns), F32)] * 2
 
     def parts_of(rows):
         return [pltpu.VMEM((rows, 2 * width), F32), pltpu.VMEM((rows, width), F32)]
@@ -667,7 +678,7 @@
     kept_a, sent_a, act, grid_g = call(
         functools.partial(forward, planes, deep, mask_rows),
         terms + [shape((n_out * PITCH, width), F32), shape((n_in * IN_PITCH, width), F32)],
-        [deep_in, deep_g, marks3, y_even, y_odd, inner_act, w1_tall],
+        [deep_in, deep_g, marks3, y_odd, y_even, inner_act, w1_tall],
         scratch=[
             pltpu.VMEM((n_in * IN_PITCH, width), F32),
             pltpu.VMEM((planes * OUTER_PITCH, 9 * width), BF),

time: 64.2 us -> 62 us (0.966)
  starting transfers between devices: 38.3 us -> 32.9 us
  waiting for transfers between devices: 8.78 us -> 12.7 us
  local copies, waits for them, and re-layouts: 4.13 us -> 2.33 us
  other arithmetic: 0 us -> 0.99 us
    ppermute x16, starting transfers between devices: 31.6 us -> 20.6 us  [cross(): return lax.ppermute(value, ('dp', 'blk'), pairs)]
    ppermute x2, starting transfers between devices: 4.64 us -> 10.2 us  [beside(): lax.ppermute(one, 'blk', pairs[0])]
    ppermute x16, waiting for transfers between devices: 7.87 us -> 11.3 us  [cross(): return lax.ppermute(value, ('dp', 'blk'), pairs)]
    unnamed x8 -> x4, local copies, waits for them, and re-layouts: 4.13 us -> 2.33 us
    another operation x0 -> x1, other arithmetic: none -> 0.99 us  [on_device(): jnp.stack([feat, cot])]
  transfers between devices with their start and end apart: 24 -> 24, of which waited for: 8 -> 17; matrix products, arithmetic and copies ran while one was open for 0% -> 0% of each run, Pallas kernels for 12% -> 13%
where the time goes in v3:
time: 62 us; the launch traced here: 61.7 us
  starting transfers between devices  32.9 us (53%)
  waiting for transfers between devices  12.7 us (20%)
  Pallas kernels  11.3 us (18%)
  local copies, waits for them, and re-layouts  2.33 us (4%)
  between operations  1.46 us (2%)
  other arithmetic  0.99 us (2%)
    ppermute x16, starting transfers between devices, cross(): return lax.ppermute(value, ('dp', 'blk'), pairs)  20.6 us
    pallas_call x20, Pallas kernels, call(): pl.pallas_call(body, out_shape=list(outs), in_specs=specs, out_specs=[VM]...  11.3 us
    ppermute x16, waiting for transfers between devices, cross(): return lax.ppermute(value, ('dp', 'blk'), pairs)  11.3 us
    ppermute x2, starting transfers between devices, beside(): lax.ppermute(one, 'blk', pairs[0])  10.2 us
    unnamed x4, local copies, waits for them, and re-layouts  2.33 us
    ppermute x2, starting transfers between devices, beside(): lax.ppermute(two, 'blk', pairs[1])  1.33 us
  transfers between devices with their start and end apart: 24, of which 17 were waited for; matrix products, arithmetic and copies ran while one was open for 0% of the time, Pallas kernels for 13%

profile of v3, /device:TPU:0, one launch (start us, length us, event | category | flops | bytes accessed | tf_op | source)
XLA Modules:
  0.0 61.7 jit_solution(1720566999813072795)
XLA Ops:
  1.3 1.0 %pad_maximum_fusion.both = bf16[2,512,128]{2,1,0:T(8,128)(2,1)S(1)} fusion(bf16[1,512,128]{2,1,0:T(8,128)(2,1)} %param.9, bf16[1,512,128]{2,1,0:T(8,128)(2,1)} %param.5), kind=kLoop, calls=%fused_computation | loop fusion | flops 131072 | bytes 524288 | tf_op jit(solution)/shard_map/stack | solution.py:633
  2.3 0.1 shard_map.76
  2.4 0.7 %collective-permute-start = (bf16[272,128]{1,0:T(8,128)(2,1)S(1)}, bf16[272,128]{1,0:T(8,128)(2,1)S(1)}, u32[]{:S(2)}, u32[]{:S(2)}) collective-permute-start(bf16[272,128]{1,0:T(8,128)(2,1)S(1)} %get-tuple-element.48), channel_id=1, source_target_pairs={{1,2},{2,1},{5,6},{6,5},{9,10},{10,9},{13,14},{14,13},{17,18},{18,... | collective-permute-start | bytes 208904 | tf_op jit(solution)/shard_map/ppermute | solution.py:622
  3.1 5.7 %collective-permute-start.1 = (bf16[272,128]{1,0:T(8,128)(2,1)S(1)}, bf16[272,128]{1,0:T(8,128)(2,1)S(1)}, u32[]{:S(2)}, u32[]{:S(2)}) collective-permute-start(bf16[272,128]{1,0:T(8,128)(2,1)S(1)} %get-tuple-element.49), channel_id=1, source_target_pairs={{0,1},{1,0},{2,3},{3,2},{4,5},{5,4},{6,7},{7,6},{8,9},{9,8},{10,11... | collective-permute-start | bytes 208904 | tf_op jit(solution)/shard_map/ppermute | solution.py:622
  8.8 1.2 %copy-done = bf16[3456,128]{1,0:T(8,128)(2,1)S(1)} copy-done((bf16[3456,128]{1,0:T(8,128)(2,1)S(1)}, bf16[3456,128]{1,0:T(8,128)(2,1)}, u32[]{:S(2)}) %copy-start) | copy-done | bytes 884760
  10.0 0.3 shard_map.78
  10.3 0.0 copy-start.1
  10.3 1.2 %copy-done.1 = bf16[3456,128]{1,0:T(8,128)(2,1)S(1)} copy-done((bf16[3456,128]{1,0:T(8,128)(2,1)S(1)}, bf16[3456,128]{1,0:T(8,128)(2,1)}, u32[]{:S(2)}) %copy-start.1) | copy-done | bytes 884760
  11.5 0.3 shard_map.77.w2_wide
  11.8 0.0 collective-permute-done.z_odd
  11.8 0.3 collective-permute-done.1.z_even
  12.1 0.1 shard_map.79
  12.2 0.7 %collective-permute-start.2 = (bf16[432,128]{1,0:T(8,128)(2,1)S(1)}, bf16[432,128]{1,0:T(8,128)(2,1)S(1)}, u32[]{:S(2)}, u32[]{:S(2)}) collective-permute-start(bf16[432,128]{1,0:T(8,128)(2,1)S(1)} %get-tuple-element.56), channel_id=1, source_target_pairs={{4,8},{8,4},{5,9},{9,5},{6,10},{10,6},{7,11},{11,7},{20,24},{24,20... | collective-permute-start | bytes 331784 | tf_op jit(solution)/shard_map/ppermute | solution.py:622
  12.9 4.5 %collective-permute-start.3 = (bf16[432,128]{1,0:T(8,128)(2,1)S(1)}, bf16[432,128]{1,0:T(8,128)(2,1)S(1)}, u32[]{:S(2)}, u32[]{:S(2)}) collective-permute-start(bf16[432,128]{1,0:T(8,128)(2,1)S(1)} %get-tuple-element.57), channel_id=1, source_target_pairs={{0,4},{4,0},{1,5},{5,1},{2,6},{6,2},{3,7},{7,3},{8,12},{12,8},{9,1... | collective-permute-start | bytes 331784 | tf_op jit(solution)/shard_map/ppermute | solution.py:622
  17.3 2.0 %shard_map.80 = (f32[640,128]{1,0:T(8,128)S(1)}, f32[640,128]{1,0:T(8,128)S(1)}, bf16[128,640]{1,0:T(8,128)(2,1)S(1)}) custom-call(f32[784,128]{1,0:T(8,128)S(1)} %get-tuple-element.50.deep_in, f32[784,128]{1,0:T(8,128)S(1)} %get-tuple-element.51.deep_g, bf16[512,128]{1,0:T(8,128)(2,1)S(1)} %get-tuple-element.45.inp, ...), custom_call_target="tpu_custom_call" | custom-call | flops 905969664 | bytes 3522560 | tf_op jit(solution)/shard_map/pallas_call | solution.py:34
  19.4 0.0 collective-permute-done.2.y_odd
  19.4 0.7 %collective-permute-done.3.y_even = bf16[432,128]{1,0:T(8,128)(2,1)S(1)} collective-permute-done((bf16[432,128]{1,0:T(8,128)(2,1)S(1)}, bf16[432,128]{1,0:T(8,128)(2,1)S(1)}, u32[]{:S(2)}, u32[]{:S(2)}) %collective-permute-start.3) | collective-permute-done | bytes 110624 | tf_op jit(solution)/shard_map/ppermute | solution.py:622
  20.1 2.0 %shard_map.81 = (f32[64,3456]{1,0:T(8,128)S(1)}, f32[64,3456]{1,0:T(8,128)S(1)}, f32[1024,128]{1,0:T(8,128)S(1)}, f32[1600,128]{1,0:T(8,128)S(1)}) custom-call(f32[784,128]{1,0:T(8,128)S(1)} %get-tuple-element.50.deep_in, f32[784,128]{1,0:T(8,128)S(1)} %get-tuple-element.51.deep_g, bf16[48,128]{1,0:T(8,128)(2,1)S(1)} %get-tuple-element.55.marks3, ...), custom_call_target="tpu_custom_call" | custom-call | flops 905969664 | bytes 5361664 | tf_op jit(solution)/shard_map/pallas_call | solution.py:34
  22.0 0.1 collective-permute-start.5
  22.1 1.8 %shard_map.82 = (f32[64,3456]{1,0:T(8,128)S(1)}, f32[64,3456]{1,0:T(8,128)S(1)}, bf16[512,1152]{1,0:T(8,128)(2,1)S(1)}) custom-call(f32[1600,128]{1,0:T(8,128)S(1)} %get-tuple-element.59.grid_g, f32[1024,128]{1,0:T(8,128)S(1)} %get-tuple-element.60.act, f32[640,128]{1,0:T(8,128)S(1)} %get-tuple-element.61.inner, ...), custom_call_target="tpu_custom_call" | custom-call | flops 905969664 | bytes 5902336 | tf_op jit(solution)/shard_map/pallas_call | solution.py:34
  23.9 0.6 collective-permute-start.4
  24.5 0.0 collective-permute-done.5.got
  24.5 0.1 shard_map.84
  24.6 1.5 %collective-permute-start.6 = (bf16[16,3456]{1,0:T(8,128)(2,1)S(1)}, bf16[16,3456]{1,0:T(8,128)(2,1)S(1)}, u32[]{:S(2)}, u32[]{:S(2)}) collective-permute-start(bf16[16,3456]{1,0:T(8,128)(2,1)S(1)} %get-tuple-element.69), channel_id=1, source_target_pairs={{0,3},{1,2},{2,1},{3,0},{4,7},{5,6},{6,5},{7,4},{8,11},{9,10},{10,... | collective-permute-start | bytes 331784 | tf_op jit(solution)/shard_map/ppermute | solution.py:408
  26.1 1.0 %collective-permute-start.7 = (bf16[16,3456]{1,0:T(8,128)(2,1)S(1)}, bf16[16,3456]{1,0:T(8,128)(2,1)S(1)}, u32[]{:S(2)}, u32[]{:S(2)}) collective-permute-start(bf16[16,3456]{1,0:T(8,128)(2,1)S(1)} %get-tuple-element.70), channel_id=1, source_target_pairs={{0,1},{1,0},{2,3},{3,2},{4,5},{5,4},{6,7},{7,6},{8,9},{9,8},{10,11... | collective-permute-start | bytes 331784 | tf_op jit(solution)/shard_map/ppermute | solution.py:408
  27.1 1.0 %collective-permute-start.8 = (bf16[16,3456]{1,0:T(8,128)(2,1)S(1)}, bf16[16,3456]{1,0:T(8,128)(2,1)S(1)}, u32[]{:S(2)}, u32[]{:S(2)}) collective-permute-start(bf16[16,3456]{1,0:T(8,128)(2,1)S(1)} %get-tuple-element.71), channel_id=1, source_target_pairs={{0,2},{1,3},{2,0},{3,1},{4,6},{5,7},{6,4},{7,5},{8,10},{9,11},{10,... | collective-permute-start | bytes 331784 | tf_op jit(solution)/shard_map/ppermute | solution.py:408
  28.2 0.0 collective-permute-done.4.got
  28.2 0.1 shard_map.83
  28.3 1.1 %collective-permute-start.10 = (bf16[16,3456]{1,0:T(8,128)(2,1)S(1)}, bf16[16,3456]{1,0:T(8,128)(2,1)S(1)}, u32[]{:S(2)}, u32[]{:S(2)}) collective-permute-start(bf16[16,3456]{1,0:T(8,128)(2,1)S(1)} %get-tuple-element.74), channel_id=1, source_target_pairs={{0,1},{1,0},{2,3},{3,2},{4,5},{5,4},{6,7},{7,6},{8,9},{9,8},{10,11... | collective-permute-start | bytes 331784 | tf_op jit(solution)/shard_map/ppermute | solution.py:408
  29.3 1.0 %collective-permute-start.11 = (bf16[16,3456]{1,0:T(8,128)(2,1)S(1)}, bf16[16,3456]{1,0:T(8,128)(2,1)S(1)}, u32[]{:S(2)}, u32[]{:S(2)}) collective-permute-start(bf16[16,3456]{1,0:T(8,128)(2,1)S(1)} %get-tuple-element.75), channel_id=1, source_target_pairs={{0,2},{1,3},{2,0},{3,1},{4,6},{5,7},{6,4},{7,5},{8,10},{9,11},{10,... | collective-permute-start | bytes 331784 | tf_op jit(solution)/shard_map/ppermute | solution.py:408
  30.3 1.2 %collective-permute-done.6.refs_1_ = bf16[16,3456]{1,0:T(8,128)(2,1)S(1)} collective-permute-done((bf16[16,3456]{1,0:T(8,128)(2,1)S(1)}, bf16[16,3456]{1,0:T(8,128)(2,1)S(1)}, u32[]{:S(2)}, u32[]{:S(2)}) %collective-permute-start.6) | collective-permute-done | bytes 110624 | tf_op jit(solution)/shard_map/ppermute | solution.py:408
  31.5 1.4 %collective-permute-start.9 = (bf16[16,3456]{1,0:T(8,128)(2,1)S(1)}, bf16[16,3456]{1,0:T(8,128)(2,1)S(1)}, u32[]{:S(2)}, u32[]{:S(2)}) collective-permute-start(bf16[16,3456]{1,0:T(8,128)(2,1)S(1)} %get-tuple-element.73), channel_id=1, source_target_pairs={{0,3},{1,2},{2,1},{3,0},{4,7},{5,6},{6,5},{7,4},{8,11},{9,10},{10,... | collective-permute-start | bytes 331784 | tf_op jit(solution)/shard_map/ppermute | solution.py:408
  32.9 0.5 collective-permute-done.7.refs_2_
  33.4 0.1 collective-permute-done.8.refs_3_
  33.5 0.1 shard_map.85.one
  33.6 2.1 %collective-permute-start.12 = (bf16[16,3456]{1,0:T(8,128)(2,1)S(1)}, bf16[16,3456]{1,0:T(8,128)(2,1)S(1)}, u32[]{:S(2)}, u32[]{:S(2)}) collective-permute-start(bf16[16,3456]{1,0:T(8,128)(2,1)S(1)} %shard_map.85.one), channel_id=1, source_target_pairs={{0,4},{1,5},{2,6},{3,7},{4,0},{5,1},{6,2},{7,3},{8,12},{9,13},{10,... | collective-permute-start | bytes 331784 | tf_op jit(solution)/shard_map/ppermute | solution.py:408
  35.7 0.1 collective-permute-done.10.refs_2_
  35.7 0.5 collective-permute-done.11.refs_3_
  36.2 1.6 %collective-permute-done.9.refs_1_ = bf16[16,3456]{1,0:T(8,128)(2,1)S(1)} collective-permute-done((bf16[16,3456]{1,0:T(8,128)(2,1)S(1)}, bf16[16,3456]{1,0:T(8,128)(2,1)S(1)}, u32[]{:S(2)}, u32[]{:S(2)}) %collective-permute-start.9) | collective-permute-done | bytes 110624 | tf_op jit(solution)/shard_map/ppermute | solution.py:408
  37.8 0.1 shard_map.86.one
  37.9 2.1 %collective-permute-start.13 = (bf16[16,3456]{1,0:T(8,128)(2,1)S(1)}, bf16[16,3456]{1,0:T(8,128)(2,1)S(1)}, u32[]{:S(2)}, u32[]{:S(2)}) collective-permute-start(bf16[16,3456]{1,0:T(8,128)(2,1)S(1)} %shard_map.86.one), channel_id=1, source_target_pairs={{0,4},{1,5},{2,6},{3,7},{4,0},{5,1},{6,2},{7,3},{8,12},{9,13},{10,... | collective-permute-start | bytes 331784 | tf_op jit(solution)/shard_map/ppermute | solution.py:408
  39.9 0.0 collective-permute-done.12.two
  40.0 0.8 %collective-permute-start.14 = (bf16[16,3456]{1,0:T(8,128)(2,1)S(1)}, bf16[16,3456]{1,0:T(8,128)(2,1)S(1)}, u32[]{:S(2)}, u32[]{:S(2)}) collective-permute-start(bf16[16,3456]{1,0:T(8,128)(2,1)S(1)} %shard_map.87.one), channel_id=1, source_target_pairs={{0,8},{1,9},{2,10},{3,11},{4,12},{5,13},{6,14},{7,15},{8,0},{9,1},... | collective-permute-start | bytes 331784 | tf_op jit(solution)/shard_map/ppermute | solution.py:408
  40.8 1.5 %shard_map.88 = bf16[512,128]{1,0:T(8,128)(2,1)} custom-call(bf16[512,1152]{1,0:T(8,128)(2,1)S(1)} %get-tuple-element.78.st_own, bf16[512,128]{1,0:T(8,128)(2,1)S(1)} %get-tuple-element.46.grads, bf16[48,128]{1,0:T(8,128)(2,1)S(1)} %get-tuple-element.55.marks3, bf16[384,1152]{1,0:T(8,128)(2,1)S(1)} %get-tuple-element.44.w1_wide), custom_call_target="tpu_custom_call" | custom-call | flops 452984832 | bytes 2338816 | tf_op jit(solution)/shard_map/pallas_call | solution.py:34
  42.3 2.0 %collective-permute-done.13.two = bf16[16,3456]{1,0:T(8,128)(2,1)S(1)} collective-permute-done((bf16[16,3456]{1,0:T(8,128)(2,1)S(1)}, bf16[16,3456]{1,0:T(8,128)(2,1)S(1)}, u32[]{:S(2)}, u32[]{:S(2)}) %collective-permute-start.13) | collective-permute-done | bytes 110624 | tf_op jit(solution)/shard_map/ppermute | solution.py:408
  44.3 1.5 %collective-permute-start.15 = (bf16[16,3456]{1,0:T(8,128)(2,1)S(1)}, bf16[16,3456]{1,0:T(8,128)(2,1)S(1)}, u32[]{:S(2)}, u32[]{:S(2)}) collective-permute-start(bf16[16,3456]{1,0:T(8,128)(2,1)S(1)} %shard_map.89.one), channel_id=1, source_target_pairs={{0,8},{1,9},{2,10},{3,11},{4,12},{5,13},{6,14},{7,15},{8,0},{9,1},... | collective-permute-start | bytes 331784 | tf_op jit(solution)/shard_map/ppermute | solution.py:408
  45.8 0.5 collective-permute-done.14.two
  46.3 1.5 %collective-permute-start.20 = (bf16[432,128]{1,0:T(8,128)(2,1)S(1)}, bf16[432,128]{1,0:T(8,128)(2,1)S(1)}, u32[]{:S(2)}, u32[]{:S(2)}) collective-permute-start(bf16[432,128]{1,0:T(8,128)(2,1)S(1)} %shard_map.90.refs_0_), channel_id=1, source_target_pairs={{0,3},{1,2},{2,1},{3,0},{4,7},{5,6},{6,5},{7,4},{8,11},{9,10},{10,... | collective-permute-start | bytes 331784 | tf_op jit(solution)/shard_map/ppermute | solution.py:408
  47.8 1.0 %collective-permute-start.21 = (bf16[432,128]{1,0:T(8,128)(2,1)S(1)}, bf16[432,128]{1,0:T(8,128)(2,1)S(1)}, u32[]{:S(2)}, u32[]{:S(2)}) collective-permute-start(bf16[432,128]{1,0:T(8,128)(2,1)S(1)} %shard_map.90.refs_0_), channel_id=1, source_target_pairs={{0,1},{1,0},{2,3},{3,2},{4,5},{5,4},{6,7},{7,6},{8,9},{9,8},{10,11... | collective-permute-start | bytes 331784 | tf_op jit(solution)/shard_map/ppermute | solution.py:408
  48.8 1.1 %collective-permute-start.22 = (bf16[432,128]{1,0:T(8,128)(2,1)S(1)}, bf16[432,128]{1,0:T(8,128)(2,1)S(1)}, u32[]{:S(2)}, u32[]{:S(2)}) collective-permute-start(bf16[432,128]{1,0:T(8,128)(2,1)S(1)} %shard_map.90.refs_0_), channel_id=1, source_target_pairs={{0,2},{1,3},{2,0},{3,1},{4,6},{5,7},{6,4},{7,5},{8,10},{9,11},{10,... | collective-permute-start | bytes 331784 | tf_op jit(solution)/shard_map/ppermute | solution.py:408
  49.8 1.4 %collective-permute-done.15.two = bf16[16,3456]{1,0:T(8,128)(2,1)S(1)} collective-permute-done((bf16[16,3456]{1,0:T(8,128)(2,1)S(1)}, bf16[16,3456]{1,0:T(8,128)(2,1)S(1)}, u32[]{:S(2)}, u32[]{:S(2)}) %collective-permute-start.15) | collective-permute-done | bytes 110624 | tf_op jit(solution)/shard_map/ppermute | solution.py:408
  51.2 1.5 %collective-permute-start.16 = (bf16[432,128]{1,0:T(8,128)(2,1)S(1)}, bf16[432,128]{1,0:T(8,128)(2,1)S(1)}, u32[]{:S(2)}, u32[]{:S(2)}) collective-permute-start(bf16[432,128]{1,0:T(8,128)(2,1)S(1)} %shard_map.91.refs_0_), channel_id=1, source_target_pairs={{0,3},{1,2},{2,1},{3,0},{4,7},{5,6},{6,5},{7,4},{8,11},{9,10},{10,... | collective-permute-start | bytes 331784 | tf_op jit(solution)/shard_map/ppermute | solution.py:408
  52.7 1.0 %collective-permute-start.17 = (bf16[432,128]{1,0:T(8,128)(2,1)S(1)}, bf16[432,128]{1,0:T(8,128)(2,1)S(1)}, u32[]{:S(2)}, u32[]{:S(2)}) collective-permute-start(bf16[432,128]{1,0:T(8,128)(2,1)S(1)} %shard_map.91.refs_0_), channel_id=1, source_target_pairs={{0,1},{1,0},{2,3},{3,2},{4,5},{5,4},{6,7},{7,6},{8,9},{9,8},{10,11... | collective-permute-start | bytes 331784 | tf_op jit(solution)/shard_map/ppermute | solution.py:408
  53.8 1.0 %collective-permute-start.18 = (bf16[432,128]{1,0:T(8,128)(2,1)S(1)}, bf16[432,128]{1,0:T(8,128)(2,1)S(1)}, u32[]{:S(2)}, u32[]{:S(2)}) collective-permute-start(bf16[432,128]{1,0:T(8,128)(2,1)S(1)} %shard_map.91.refs_0_), channel_id=1, source_target_pairs={{0,2},{1,3},{2,0},{3,1},{4,6},{5,7},{6,4},{7,5},{8,10},{9,11},{10,... | collective-permute-start | bytes 331784 | tf_op jit(solution)/shard_map/ppermute | solution.py:408
  54.8 0.2 collective-permute-done.21.refs_2_
  55.0 0.4 collective-permute-done.22.refs_3_
  55.5 0.1 collective-permute-start.23
  55.6 1.3 %collective-permute-done.16.refs_1_ = bf16[432,128]{1,0:T(8,128)(2,1)S(1)} collective-permute-done((bf16[432,128]{1,0:T(8,128)(2,1)S(1)}, bf16[432,128]{1,0:T(8,128)(2,1)S(1)}, u32[]{:S(2)}, u32[]{:S(2)}) %collective-permute-start.16) | collective-permute-done | bytes 110624 | tf_op jit(solution)/shard_map/ppermute | solution.py:408
  57.0 0.7 %collective-permute-done.17.refs_2_ = bf16[432,128]{1,0:T(8,128)(2,1)S(1)} collective-permute-done((bf16[432,128]{1,0:T(8,128)(2,1)S(1)}, bf16[432,128]{1,0:T(8,128)(2,1)S(1)}, u32[]{:S(2)}, u32[]{:S(2)}) %collective-permute-start.17) | collective-permute-done | bytes 110624 | tf_op jit(solution)/shard_map/ppermute | solution.py:408
  57.7 0.8 %collective-permute-done.18.refs_3_ = bf16[432,128]{1,0:T(8,128)(2,1)S(1)} collective-permute-done((bf16[432,128]{1,0:T(8,128)(2,1)S(1)}, bf16[432,128]{1,0:T(8,128)(2,1)S(1)}, u32[]{:S(2)}, u32[]{:S(2)}) %collective-permute-start.18) | collective-permute-done | bytes 110624 | tf_op jit(solution)/shard_map/ppermute | solution.py:408
  58.6 0.1 collective-permute-start.19
  58.6 1.3 %shard_map.95 = f32[3456,128]{1,0:T(8,128)} custom-call(bf16[1728,128]{1,0:T(8,128)(2,1)S(1)} %shard_map.94.own, bf16[1728,128]{1,0:T(8,128)(2,1)S(1)} %collective-permute-done.23.other), custom_call_target="tpu_custom_call" | custom-call | bytes 2654208 | tf_op jit(solution)/shard_map/pallas_call | solution.py:34
  60.0 0.4 collective-permute-done.19.other
  60.4 1.3 %shard_map.93 = f32[3456,128]{1,0:T(8,128)} custom-call(bf16[1728,128]{1,0:T(8,128)(2,1)S(1)} %shard_map.92.own, bf16[1728,128]{1,0:T(8,128)(2,1)S(1)} %collective-permute-done.19.other), custom_call_target="tpu_custom_call" | custom-call | bytes 2654208 | tf_op jit(solution)/shard_map/pallas_call | solution.py:34
  (9 shorter events, 0.2 us)
Async XLA Ops:
  2.4 9.4 %collective-permute-start = (bf16[272,128]{1,0:T(8,128)(2,1)S(1)}, bf16[272,128]{1,0:T(8,128)(2,1)S(1)}, u32[]{:S(2)}, u32[]{:S(2)}) collective-permute-start(bf16[272,128]{1,0:T(8,128)(2,1)S(1)} %get-tuple-element.48), channel_id=1, source_target_pairs={{1,2},{2,1},{5,6},{6,5},{9,10},{10,9},{13,14},{14,13},{17,18},{18,... | collective-permute-start | bytes 208904 | tf_op jit(solution)/shard_map/ppermute | solution.py:622
  3.1 9.0 %collective-permute-start.1 = (bf16[272,128]{1,0:T(8,128)(2,1)S(1)}, bf16[272,128]{1,0:T(8,128)(2,1)S(1)}, u32[]{:S(2)}, u32[]{:S(2)}) collective-permute-start(bf16[272,128]{1,0:T(8,128)(2,1)S(1)} %get-tuple-element.49), channel_id=1, source_target_pairs={{0,1},{1,0},{2,3},{3,2},{4,5},{5,4},{6,7},{7,6},{8,9},{9,8},{10,11... | collective-permute-start | bytes 208904 | tf_op jit(solution)/shard_map/ppermute | solution.py:622
  8.8 1.2 %copy-start = (bf16[3456,128]{1,0:T(8,128)(2,1)S(1)}, bf16[3456,128]{1,0:T(8,128)(2,1)}, u32[]{:S(2)}) copy-start(bf16[3456,128]{1,0:T(8,128)(2,1)} %src.3) | copy-start | bytes 2654212
  10.3 1.2 %copy-start.1 = (bf16[3456,128]{1,0:T(8,128)(2,1)S(1)}, bf16[3456,128]{1,0:T(8,128)(2,1)}, u32[]{:S(2)}) copy-start(bf16[3456,128]{1,0:T(8,128)(2,1)} %src.2) | copy-start | bytes 2654212
  12.2 7.2 %collective-permute-start.2 = (bf16[432,128]{1,0:T(8,128)(2,1)S(1)}, bf16[432,128]{1,0:T(8,128)(2,1)S(1)}, u32[]{:S(2)}, u32[]{:S(2)}) collective-permute-start(bf16[432,128]{1,0:T(8,128)(2,1)S(1)} %get-tuple-element.56), channel_id=1, source_target_pairs={{4,8},{8,4},{5,9},{9,5},{6,10},{10,6},{7,11},{11,7},{20,24},{24,20... | collective-permute-start | bytes 331784 | tf_op jit(solution)/shard_map/ppermute | solution.py:622
  12.9 7.2 %collective-permute-start.3 = (bf16[432,128]{1,0:T(8,128)(2,1)S(1)}, bf16[432,128]{1,0:T(8,128)(2,1)S(1)}, u32[]{:S(2)}, u32[]{:S(2)}) collective-permute-start(bf16[432,128]{1,0:T(8,128)(2,1)S(1)} %get-tuple-element.57), channel_id=1, source_target_pairs={{0,4},{4,0},{1,5},{5,1},{2,6},{6,2},{3,7},{7,3},{8,12},{12,8},{9,1... | collective-permute-start | bytes 331784 | tf_op jit(solution)/shard_map/ppermute | solution.py:622
  22.0 2.5 %collective-permute-start.5 = (f32[64,3456]{1,0:T(8,128)S(1)}, f32[64,3456]{1,0:T(8,128)S(1)}, u32[]{:S(2)}, u32[]{:S(2)}) collective-permute-start(f32[64,3456]{1,0:T(8,128)S(1)} %get-tuple-element.66), channel_id=1, source_target_pairs={{0,16},{16,0},{1,17},{17,1},{2,18},{18,2},{3,19},{19,3},{4,20},{20... | collective-permute-start | bytes 2654216 | tf_op jit(solution)/shard_map/ppermute | solution.py:398
  23.9 4.2 %collective-permute-start.4 = (f32[64,3456]{1,0:T(8,128)S(1)}, f32[64,3456]{1,0:T(8,128)S(1)}, u32[]{:S(2)}, u32[]{:S(2)}) collective-permute-start(f32[64,3456]{1,0:T(8,128)S(1)} %get-tuple-element.63), channel_id=1, source_target_pairs={{0,16},{16,0},{1,17},{17,1},{2,18},{18,2},{3,19},{19,3},{4,20},{20... | collective-permute-start | bytes 2654216 | tf_op jit(solution)/shard_map/ppermute | solution.py:398
  24.6 6.9 %collective-permute-start.6 = (bf16[16,3456]{1,0:T(8,128)(2,1)S(1)}, bf16[16,3456]{1,0:T(8,128)(2,1)S(1)}, u32[]{:S(2)}, u32[]{:S(2)}) collective-permute-start(bf16[16,3456]{1,0:T(8,128)(2,1)S(1)} %get-tuple-element.69), channel_id=1, source_target_pairs={{0,3},{1,2},{2,1},{3,0},{4,7},{5,6},{6,5},{7,4},{8,11},{9,10},{10,... | collective-permute-start | bytes 331784 | tf_op jit(solution)/shard_map/ppermute | solution.py:408
  26.1 7.3 %collective-permute-start.7 = (bf16[16,3456]{1,0:T(8,128)(2,1)S(1)}, bf16[16,3456]{1,0:T(8,128)(2,1)S(1)}, u32[]{:S(2)}, u32[]{:S(2)}) collective-permute-start(bf16[16,3456]{1,0:T(8,128)(2,1)S(1)} %get-tuple-element.70), channel_id=1, source_target_pairs={{0,1},{1,0},{2,3},{3,2},{4,5},{5,4},{6,7},{7,6},{8,9},{9,8},{10,11... | collective-permute-start | bytes 331784 | tf_op jit(solution)/shard_map/ppermute | solution.py:408
  27.1 6.4 %collective-permute-start.8 = (bf16[16,3456]{1,0:T(8,128)(2,1)S(1)}, bf16[16,3456]{1,0:T(8,128)(2,1)S(1)}, u32[]{:S(2)}, u32[]{:S(2)}) collective-permute-start(bf16[16,3456]{1,0:T(8,128)(2,1)S(1)} %get-tuple-element.71), channel_id=1, source_target_pairs={{0,2},{1,3},{2,0},{3,1},{4,6},{5,7},{6,4},{7,5},{8,10},{9,11},{10,... | collective-permute-start | bytes 331784 | tf_op jit(solution)/shard_map/ppermute | solution.py:408
  28.3 7.5 %collective-permute-start.10 = (bf16[16,3456]{1,0:T(8,128)(2,1)S(1)}, bf16[16,3456]{1,0:T(8,128)(2,1)S(1)}, u32[]{:S(2)}, u32[]{:S(2)}) collective-permute-start(bf16[16,3456]{1,0:T(8,128)(2,1)S(1)} %get-tuple-element.74), channel_id=1, source_target_pairs={{0,1},{1,0},{2,3},{3,2},{4,5},{5,4},{6,7},{7,6},{8,9},{9,8},{10,11... | collective-permute-start | bytes 331784 | tf_op jit(solution)/shard_map/ppermute | solution.py:408
  29.3 6.9 %collective-permute-start.11 = (bf16[16,3456]{1,0:T(8,128)(2,1)S(1)}, bf16[16,3456]{1,0:T(8,128)(2,1)S(1)}, u32[]{:S(2)}, u32[]{:S(2)}) collective-permute-start(bf16[16,3456]{1,0:T(8,128)(2,1)S(1)} %get-tuple-element.75), channel_id=1, source_target_pairs={{0,2},{1,3},{2,0},{3,1},{4,6},{5,7},{6,4},{7,5},{8,10},{9,11},{10,... | collective-permute-start | bytes 331784 | tf_op jit(solution)/shard_map/ppermute | solution.py:408
  31.5 6.3 %collective-permute-start.9 = (bf16[16,3456]{1,0:T(8,128)(2,1)S(1)}, bf16[16,3456]{1,0:T(8,128)(2,1)S(1)}, u32[]{:S(2)}, u32[]{:S(2)}) collective-permute-start(bf16[16,3456]{1,0:T(8,128)(2,1)S(1)} %get-tuple-element.73), channel_id=1, source_target_pairs={{0,3},{1,2},{2,1},{3,0},{4,7},{5,6},{6,5},{7,4},{8,11},{9,10},{10,... | collective-permute-start | bytes 331784 | tf_op jit(solution)/shard_map/ppermute | solution.py:408
  33.6 6.4 %collective-permute-start.12 = (bf16[16,3456]{1,0:T(8,128)(2,1)S(1)}, bf16[16,3456]{1,0:T(8,128)(2,1)S(1)}, u32[]{:S(2)}, u32[]{:S(2)}) collective-permute-start(bf16[16,3456]{1,0:T(8,128)(2,1)S(1)} %shard_map.85.one), channel_id=1, source_target_pairs={{0,4},{1,5},{2,6},{3,7},{4,0},{5,1},{6,2},{7,3},{8,12},{9,13},{10,... | collective-permute-start | bytes 331784 | tf_op jit(solution)/shard_map/ppermute | solution.py:408
  37.9 6.4 %collective-permute-start.13 = (bf16[16,3456]{1,0:T(8,128)(2,1)S(1)}, bf16[16,3456]{1,0:T(8,128)(2,1)S(1)}, u32[]{:S(2)}, u32[]{:S(2)}) collective-permute-start(bf16[16,3456]{1,0:T(8,128)(2,1)S(1)} %shard_map.86.one), channel_id=1, source_target_pairs={{0,4},{1,5},{2,6},{3,7},{4,0},{5,1},{6,2},{7,3},{8,12},{9,13},{10,... | collective-permute-start | bytes 331784 | tf_op jit(solution)/shard_map/ppermute | solution.py:408
  40.0 6.3 %collective-permute-start.14 = (bf16[16,3456]{1,0:T(8,128)(2,1)S(1)}, bf16[16,3456]{1,0:T(8,128)(2,1)S(1)}, u32[]{:S(2)}, u32[]{:S(2)}) collective-permute-start(bf16[16,3456]{1,0:T(8,128)(2,1)S(1)} %shard_map.87.one), channel_id=1, source_target_pairs={{0,8},{1,9},{2,10},{3,11},{4,12},{5,13},{6,14},{7,15},{8,0},{9,1},... | collective-permute-start | bytes 331784 | tf_op jit(solution)/shard_map/ppermute | solution.py:408
  44.3 6.9 %collective-permute-start.15 = (bf16[16,3456]{1,0:T(8,128)(2,1)S(1)}, bf16[16,3456]{1,0:T(8,128)(2,1)S(1)}, u32[]{:S(2)}, u32[]{:S(2)}) collective-permute-start(bf16[16,3456]{1,0:T(8,128)(2,1)S(1)} %shard_map.89.one), channel_id=1, source_target_pairs={{0,8},{1,9},{2,10},{3,11},{4,12},{5,13},{6,14},{7,15},{8,0},{9,1},... | collective-permute-start | bytes 331784 | tf_op jit(solution)/shard_map/ppermute | solution.py:408
  46.3 7.5 %collective-permute-start.20 = (bf16[432,128]{1,0:T(8,128)(2,1)S(1)}, bf16[432,128]{1,0:T(8,128)(2,1)S(1)}, u32[]{:S(2)}, u32[]{:S(2)}) collective-permute-start(bf16[432,128]{1,0:T(8,128)(2,1)S(1)} %shard_map.90.refs_0_), channel_id=1, source_target_pairs={{0,3},{1,2},{2,1},{3,0},{4,7},{5,6},{6,5},{7,4},{8,11},{9,10},{10,... | collective-permute-start | bytes 331784 | tf_op jit(solution)/shard_map/ppermute | solution.py:408
  47.8 7.2 %collective-permute-start.21 = (bf16[432,128]{1,0:T(8,128)(2,1)S(1)}, bf16[432,128]{1,0:T(8,128)(2,1)S(1)}, u32[]{:S(2)}, u32[]{:S(2)}) collective-permute-start(bf16[432,128]{1,0:T(8,128)(2,1)S(1)} %shard_map.90.refs_0_), channel_id=1, source_target_pairs={{0,1},{1,0},{2,3},{3,2},{4,5},{5,4},{6,7},{7,6},{8,9},{9,8},{10,11... | collective-permute-start | bytes 331784 | tf_op jit(solution)/shard_map/ppermute | solution.py:408
  48.8 6.7 %collective-permute-start.22 = (bf16[432,128]{1,0:T(8,128)(2,1)S(1)}, bf16[432,128]{1,0:T(8,128)(2,1)S(1)}, u32[]{:S(2)}, u32[]{:S(2)}) collective-permute-start(bf16[432,128]{1,0:T(8,128)(2,1)S(1)} %shard_map.90.refs_0_), channel_id=1, source_target_pairs={{0,2},{1,3},{2,0},{3,1},{4,6},{5,7},{6,4},{7,5},{8,10},{9,11},{10,... | collective-permute-start | bytes 331784 | tf_op jit(solution)/shard_map/ppermute | solution.py:408
  51.2 5.7 %collective-permute-start.16 = (bf16[432,128]{1,0:T(8,128)(2,1)S(1)}, bf16[432,128]{1,0:T(8,128)(2,1)S(1)}, u32[]{:S(2)}, u32[]{:S(2)}) collective-permute-start(bf16[432,128]{1,0:T(8,128)(2,1)S(1)} %shard_map.91.refs_0_), channel_id=1, source_target_pairs={{0,3},{1,2},{2,1},{3,0},{4,7},{5,6},{6,5},{7,4},{8,11},{9,10},{10,... | collective-permute-start | bytes 331784 | tf_op jit(solution)/shard_map/ppermute | solution.py:408
  52.7 4.9 %collective-permute-start.17 = (bf16[432,128]{1,0:T(8,128)(2,1)S(1)}, bf16[432,128]{1,0:T(8,128)(2,1)S(1)}, u32[]{:S(2)}, u32[]{:S(2)}) collective-permute-start(bf16[432,128]{1,0:T(8,128)(2,1)S(1)} %shard_map.91.refs_0_), channel_id=1, source_target_pairs={{0,1},{1,0},{2,3},{3,2},{4,5},{5,4},{6,7},{7,6},{8,9},{9,8},{10,11... | collective-permute-start | bytes 331784 | tf_op jit(solution)/shard_map/ppermute | solution.py:408
  53.8 4.7 %collective-permute-start.18 = (bf16[432,128]{1,0:T(8,128)(2,1)S(1)}, bf16[432,128]{1,0:T(8,128)(2,1)S(1)}, u32[]{:S(2)}, u32[]{:S(2)}) collective-permute-start(bf16[432,128]{1,0:T(8,128)(2,1)S(1)} %shard_map.91.refs_0_), channel_id=1, source_target_pairs={{0,2},{1,3},{2,0},{3,1},{4,6},{5,7},{6,4},{7,5},{8,10},{9,11},{10,... | collective-permute-start | bytes 331784 | tf_op jit(solution)/shard_map/ppermute | solution.py:408
  55.5 3.1 %collective-permute-start.23 = (bf16[1728,128]{1,0:T(8,128)(2,1)S(1)}, bf16[1728,128]{1,0:T(8,128)(2,1)S(1)}, u32[]{:S(2)}, u32[]{:S(2)}) collective-permute-start(bf16[1728,128]{1,0:T(8,128)(2,1)S(1)} %shard_map.94.own), channel_id=1, source_target_pairs={{0,16},{16,0},{1,17},{17,1},{2,18},{18,2},{3,19},{19,3},{4,20},{20... | collective-permute-start | bytes 1327112 | tf_op jit(solution)/shard_map/ppermute | solution.py:398
  58.6 1.9 %collective-permute-start.19 = (bf16[1728,128]{1,0:T(8,128)(2,1)S(1)}, bf16[1728,128]{1,0:T(8,128)(2,1)S(1)}, u32[]{:S(2)}, u32[]{:S(2)}) collective-permute-start(bf16[1728,128]{1,0:T(8,128)(2,1)S(1)} %shard_map.92.own), channel_id=1, source_target_pairs={{0,16},{16,0},{1,17},{17,1},{2,18},{18,2},{3,19},{19,3},{4,20},{20... | collective-permute-start | bytes 1327112 | tf_op jit(solution)/shard_map/ppermute | solution.py:398

commit v4 on v3

--- a/solution.py
+++ b/solution.py
@@ -135,15 +135,15 @@
             faces(even, odd)
 
 
-def lay_weights(src, *refs):
-    *outs, wide = refs
-    wide[...] = src[...].astype(F32)
-    for tap in range(TAPS):
-        a, bc = tap // 9, tap % 9
-        block = wide[pl.ds(tap, 128, stride=TAPS), :].astype(BF)
-        outs[0][a * 128 : (a + 1) * 128, bc * 128 : (bc + 1) * 128] = block
-        for out in outs[1:]:
-            out[bc * 128 : (bc + 1) * 128, a * 128 : (a + 1) * 128] = block
+def lay_weights(src, wide_1, tall_1, wide_2, rows):
+    for at, (broad, upright) in enumerate(((wide_1, tall_1), (wide_2, None))):
+        rows[...] = src[at].astype(F32)
+        for tap in range(TAPS):
+            a, bc = tap // 9, tap % 9
+            block = rows[pl.ds(tap, 128, stride=TAPS), :].astype(BF)
+            broad[a * 128 : (a + 1) * 128, bc * 128 : (bc + 1) * 128] = block
+            if upright is not None:
+                upright[bc * 128 : (bc + 1) * 128, a * 128 : (a + 1) * 128] = block
 
 
 def dot(a, b):
@@ -408,20 +408,26 @@
     return lax.ppermute(value, ("dp", "blk"), pairs)
 
 
-def turned(k):
-    return {0: 0, 1: 3, 2: 1 + lax.axis_index("dp"), 3: 2 - lax.axis_index("dp")}[k]
-
-
-def split_rows(parts, kept, got, own, *sent):
-    me = lax.axis_index("blk") % INNER
+PLANE = ((1, 2), (2, 1), (0, 3, 1, 2))
+MIXED = ((1, 4), (2, 4), (0, 3, 2, 1))
+
+
+def spot(group):
+    chip, core = lax.axis_index("blk"), lax.axis_index("dp")
+    places = [chip // one % 2 + 2 * (chip // two % 2) for one, two in group[:2]]
+    return jnp.where(core == 0, places[0], places[1])
+
+
+def split_rows(group, kept, got, own, *sent):
+    me = spot(group)
     rows = own.shape[0]
-    for k in range(parts):
-        at = pl.ds(pl.multiple_of((me ^ turned(k)) * rows, rows), rows)
+    for n, k in enumerate(group[2]):
+        at = pl.ds(pl.multiple_of((me ^ k) * rows, rows), rows)
         value = kept[at, :] + got[at, :].astype(F32)
-        if k == 0:
+        if n == 0:
             own[...] = value
         else:
-            sent[k - 1][...] = value.astype(BF)
+            sent[n - 1][...] = value.astype(BF)
 
 
 def split_columns(parts, *refs):
@@ -467,12 +473,12 @@
         out[:, pl.ds(pl.multiple_of((me ^ k) * columns, 128), columns)] = refs[k][...]
 
 
-def join_rows(parts, *refs):
-    me = lax.axis_index("blk") % INNER
-    out = refs[parts]
+def join_rows(group, *refs):
+    me = spot(group)
+    out = refs[INNER]
     rows = refs[0].shape[0]
-    for k in range(parts):
-        out[pl.ds(pl.multiple_of((me ^ turned(k)) * rows, rows), rows), :] = refs[k][...]
+    for n, k in enumerate(group[2]):
+        out[pl.ds(pl.multiple_of((me ^ k) * rows, rows), rows), :] = refs[n][...]
 
 
 def finish(own, other, out):
@@ -494,19 +500,22 @@
     return lax.optimization_barrier((value, *others))[0]
 
 
-def near(values):
-    return [cross(v, bits) for v, bits in zip(values, ((3, 3), (1, 2), (2, 1)))]
+def near(group, values):
+    return [
+        cross(v, [one * (k % 2) + two * (k // 2) for one, two in group[:2]])
+        for v, k in zip(values, group[2][1:])
+    ]
 
 
 def far(values):
     return [swap(v, "blk", INNER * (k + 1)) for k, v in enumerate(values)]
 
 
-def split_stage(kept, got):
+def split_stage(group, kept, got):
     half, columns = kept.shape
     rows = half // INNER
     return call(
-        functools.partial(split_rows, INNER),
+        functools.partial(split_rows, group),
         [shape((rows, columns), F32)] + [shape((rows, columns), BF)] * (INNER - 1),
         [kept, got],
     )
@@ -526,10 +535,10 @@
     return call(add_pair, [shape(value.shape, BF)], [value, got])[0]
 
 
-def back_stage(wide, gots):
+def back_stage(group, wide, gots):
     rows, columns = wide.shape
     return call(
-        functools.partial(join_rows, INNER), [shape((rows * INNER, columns), BF)], [wide] + gots
+        functools.partial(join_rows, group), [shape((rows * INNER, columns), BF)], [wide] + gots
     )[0]
 
 
@@ -554,19 +563,25 @@
     return call(finish, [shape((2 * mine.shape[0], 128), F32)], [mine, other])[0]
 
 
-def across(owns, gots, beside):
-    outer = lax.axis_size("blk") // INNER
-    if outer > 4:
+def rest_steps(group):
+    count = lax.axis_size("blk")
+    bits = [1 << k for k in range(count.bit_length() - 1)]
+    left = [[bit for bit in bits if bit not in used] for used in group[:2]]
+    return list(zip(left[0], reversed(left[1])))
+
+
+def across(groups, owns, gots, beside):
+    if lax.axis_size("blk") // INNER > 4:
         sums = [wide_sum(own, got) for own, got in zip(owns, gots)]
         one, two = [laid_pair(value, jnp.zeros_like(value)) for value in sums]
         return one, two, beside(one)
     one = sum_stage(owns[0], gots[0])
     two = sum_stage(after(owns[1], one), gots[1])
-    steps = [INNER << k for k in range(outer.bit_length() - 1)]
+    steps = [rest_steps(group) for group in groups]
     other = None
-    for bits in zip(steps, reversed(steps)):
-        add = laid_pair if bits[0] == steps[-1] else pair_stage
-        got_one, got_two = cross(one, bits), cross(two, bits)
+    for n, (bits_one, bits_two) in enumerate(zip(*steps)):
+        add = laid_pair if n == len(steps[0]) - 1 else pair_stage
+        got_one, got_two = cross(one, bits_one), cross(two, bits_two)
         one = add(after(one, two), got_one)
         if other is None:
             other = beside(one)
@@ -638,12 +653,13 @@
     broad = shape((3 * width, 9 * width), BF)
     upright = shape((9 * width, 3 * width), BF)
 
-    def laid(weight, outs):
-        return call(lay_weights, outs, [weight], scratch=[pltpu.VMEM((TAPS * width, width), F32)])
-
-    (w2_wide,) = laid(w_second, [broad])
-    w1_wide, w1_tall = laid(w_first, [broad, upright])
-    inp = after(inp, w2_wide, w1_wide)
+    w1_wide, w1_tall, w2_wide = call(
+        lay_weights,
+        [broad, upright, broad],
+        [jnp.stack([w_first, w_second])],
+        scratch=[pltpu.VMEM((TAPS * width, width), F32)],
+    )
+    inp = after(inp, w2_wide)
     edge = 4 * planes * GROWN + 3 * mask_rows
     even, odd, deep_in, deep_g, marks3 = call(
         functools.partial(pack_lines, planes, mask_rows),
@@ -690,7 +706,8 @@
         ],
         flops=2 * work,
     )
-    own_a, *send_a = split_stage(kept_a, swap(sent_a, "dp", 1))
+    groups = (PLANE, MIXED if outer <= 4 else PLANE)
+    own_a, *send_a = split_stage(groups[0], kept_a, swap(sent_a, "dp", 1))
     kept_b, sent_b, st_own = call(
         functools.partial(backward, planes, deep, mask_rows, tile_of),
         terms + [shape((n_out * FACE, 9 * width), BF)],
@@ -700,9 +717,9 @@
         + [pltpu.VMEM((n_out * PITCH, width), F32)],
         flops=2 * work,
     )
-    own_b, *send_b = split_stage(kept_b, swap(sent_b, "dp", 1))
-    gots_a = near(send_a)
-    gots_b = near(send_b)
+    own_b, *send_b = split_stage(groups[1], kept_b, swap(sent_b, "dp", 1))
+    gots_a = near(groups[0], send_a)
+    gots_b = near(groups[1], send_b)
     own_a = after(own_a, own_b)
 
     def last_part(cue):
@@ -714,11 +731,11 @@
             flops=work,
         )[0]
 
-    value_a, value_b, result = across((own_a, own_b), (gots_a, gots_b), last_part)
-    gots_a = near([value_a] * (INNER - 1))
-    gots_b = near([value_b] * (INNER - 1))
-    mine_a = back_stage(value_a, gots_a)
-    mine_b = back_stage(value_b, gots_b)
+    value_a, value_b, result = across(groups, (own_a, own_b), (gots_a, gots_b), last_part)
+    gots_a = near(groups[0], [value_a] * (INNER - 1))
+    gots_b = near(groups[1], [value_b] * (INNER - 1))
+    mine_a = back_stage(groups[0], value_a, gots_a)
+    mine_b = back_stage(groups[1], value_b, gots_b)
     grad_second = finished(mine_a, swap(mine_a, "dp", 1))
     grad_first = finished(mine_b, swap(mine_b, "dp", 1))
     return (grad_first, grad_second, result[None])

time: 62 us -> 60.3 us (0.973)
  local copies, waits for them, and re-layouts: 2.33 us -> 0 us
  waiting for transfers between devices: 12.7 us -> 10.4 us
  other arithmetic: 0.99 us -> 2.59 us
  starting transfers between devices: 32.9 us -> 34.4 us
    ppermute x16, waiting for transfers between devices: 11.3 us -> 8.15 us  [cross(): return lax.ppermute(value, ('dp', 'blk'), pairs)]
    unnamed x4 -> x0, local copies, waits for them, and re-layouts: 2.33 us -> none
    another operation x0 -> x1, other arithmetic: none -> 1.6 us  [on_device(): jnp.stack([w_first, w_second])]
    ppermute x16, starting transfers between devices: 20.6 us -> 22.1 us  [cross(): return lax.ppermute(value, ('dp', 'blk'), pairs)]
    ppermute x2, waiting for transfers between devices: 1 us -> 1.74 us  [beside(): lax.ppermute(one, 'blk', pairs[0])]
    pallas_call x20 -> x19, Pallas kernels: 11.3 us -> 11.3 us  [call(): pl.pallas_call(body, out_shape=list(outs), in_specs=specs, out_specs=[VM]...]
  transfers between devices with their start and end apart: 24 -> 24, of which waited for: 17 -> 12; matrix products, arithmetic and copies ran while one was open for 0% -> 3% of each run, Pallas kernels for 13% -> 13%
where the time goes in v4:
time: 60.3 us; the launch traced here: 60.1 us
  starting transfers between devices  34.4 us (57%)
  Pallas kernels  11.3 us (19%)
  waiting for transfers between devices  10.4 us (17%)
  other arithmetic  2.59 us (4%)
  between operations  1.46 us (2%)
    ppermute x16, starting transfers between devices, cross(): return lax.ppermute(value, ('dp', 'blk'), pairs)  22.1 us
    pallas_call x19, Pallas kernels, call(): pl.pallas_call(body, out_shape=list(outs), in_specs=specs, out_specs=[VM]...  11.3 us
    ppermute x2, starting transfers between devices, beside(): lax.ppermute(one, 'blk', pairs[0])  10.2 us
    ppermute x16, waiting for transfers between devices, cross(): return lax.ppermute(value, ('dp', 'blk'), pairs)  8.15 us
    ppermute x2, waiting for transfers between devices, beside(): lax.ppermute(one, 'blk', pairs[0])  1.74 us
    another operation x1, other arithmetic, on_device(): jnp.stack([w_first, w_second])  1.6 us
    ppermute x2, starting transfers between devices, beside(): lax.ppermute(two, 'blk', pairs[1])  1.33 us
  transfers between devices with their start and end apart: 24, of which 12 were waited for; matrix products, arithmetic and copies ran while one was open for 3% of the time, Pallas kernels for 13%

profile of v4, /device:TPU:0, one launch (start us, length us, event | category | flops | bytes accessed | tf_op | source)
XLA Modules:
  0.0 60.1 jit_solution(683268558019292492)
XLA Ops:
  1.3 1.0 %pad_maximum_fusion.1.both = bf16[2,512,128]{2,1,0:T(8,128)(2,1)S(1)} fusion(bf16[1,512,128]{2,1,0:T(8,128)(2,1)} %param.9, bf16[1,512,128]{2,1,0:T(8,128)(2,1)} %param.5), kind=kLoop, calls=%fused_computation.1 | loop fusion | flops 131072 | bytes 524288 | tf_op jit(solution)/shard_map/stack | solution.py:648
  2.3 0.1 shard_map.76
  2.4 0.7 %collective-permute-start = (bf16[272,128]{1,0:T(8,128)(2,1)S(1)}, bf16[272,128]{1,0:T(8,128)(2,1)S(1)}, u32[]{:S(2)}, u32[]{:S(2)}) collective-permute-start(bf16[272,128]{1,0:T(8,128)(2,1)S(1)} %get-tuple-element.49), channel_id=1, source_target_pairs={{1,2},{2,1},{5,6},{6,5},{9,10},{10,9},{13,14},{14,13},{17,18},{18,... | collective-permute-start | bytes 208904 | tf_op jit(solution)/shard_map/ppermute | solution.py:637
  3.1 5.7 %collective-permute-start.1 = (bf16[272,128]{1,0:T(8,128)(2,1)S(1)}, bf16[272,128]{1,0:T(8,128)(2,1)S(1)}, u32[]{:S(2)}, u32[]{:S(2)}) collective-permute-start(bf16[272,128]{1,0:T(8,128)(2,1)S(1)} %get-tuple-element.50), channel_id=1, source_target_pairs={{0,1},{1,0},{2,3},{3,2},{4,5},{5,4},{6,7},{7,6},{8,9},{9,8},{10,11... | collective-permute-start | bytes 208904 | tf_op jit(solution)/shard_map/ppermute | solution.py:637
  8.8 1.6 %pad_maximum_fusion.src = bf16[2,3456,128]{2,1,0:T(8,128)(2,1)S(1)} fusion(bf16[1,3456,128]{2,1,0:T(8,128)(2,1)} %bitcast.3, bf16[1,3456,128]{2,1,0:T(8,128)(2,1)} %bitcast.4), kind=kLoop, calls=%fused_computation | loop fusion | flops 884736 | bytes 3538944 | tf_op jit(solution)/shard_map/stack | solution.py:659
  10.4 0.6 %shard_map.77 = (bf16[384,1152]{1,0:T(8,128)(2,1)S(1)}, bf16[1152,384]{1,0:T(8,128)(2,1)S(1)}, bf16[384,1152]{1,0:T(8,128)(2,1)S(1)}) custom-call(bf16[2,3456,128]{2,1,0:T(8,128)(2,1)S(1)} %pad_maximum_fusion.src), custom_call_target="tpu_custom_call" | custom-call | bytes 4423680 | tf_op jit(solution)/shard_map/pallas_call | solution.py:34
  11.0 0.0 collective-permute-done.z_odd
  11.0 1.1 %collective-permute-done.1.z_even = bf16[272,128]{1,0:T(8,128)(2,1)S(1)} collective-permute-done((bf16[272,128]{1,0:T(8,128)(2,1)S(1)}, bf16[272,128]{1,0:T(8,128)(2,1)S(1)}, u32[]{:S(2)}, u32[]{:S(2)}) %collective-permute-start.1) | collective-permute-done | bytes 69664 | tf_op jit(solution)/shard_map/ppermute | solution.py:637
  12.1 0.1 shard_map.78
  12.2 0.7 %collective-permute-start.2 = (bf16[432,128]{1,0:T(8,128)(2,1)S(1)}, bf16[432,128]{1,0:T(8,128)(2,1)S(1)}, u32[]{:S(2)}, u32[]{:S(2)}) collective-permute-start(bf16[432,128]{1,0:T(8,128)(2,1)S(1)} %get-tuple-element.57), channel_id=1, source_target_pairs={{4,8},{8,4},{5,9},{9,5},{6,10},{10,6},{7,11},{11,7},{20,24},{24,20... | collective-permute-start | bytes 331784 | tf_op jit(solution)/shard_map/ppermute | solution.py:637
  12.9 4.5 %collective-permute-start.3 = (bf16[432,128]{1,0:T(8,128)(2,1)S(1)}, bf16[432,128]{1,0:T(8,128)(2,1)S(1)}, u32[]{:S(2)}, u32[]{:S(2)}) collective-permute-start(bf16[432,128]{1,0:T(8,128)(2,1)S(1)} %get-tuple-element.58), channel_id=1, source_target_pairs={{0,4},{4,0},{1,5},{5,1},{2,6},{6,2},{3,7},{7,3},{8,12},{12,8},{9,1... | collective-permute-start | bytes 331784 | tf_op jit(solution)/shard_map/ppermute | solution.py:637
  17.3 2.0 %shard_map.79 = (f32[640,128]{1,0:T(8,128)S(1)}, f32[640,128]{1,0:T(8,128)S(1)}, bf16[128,640]{1,0:T(8,128)(2,1)S(1)}) custom-call(f32[784,128]{1,0:T(8,128)S(1)} %get-tuple-element.51.deep_in, f32[784,128]{1,0:T(8,128)S(1)} %get-tuple-element.52.deep_g, bf16[512,128]{1,0:T(8,128)(2,1)S(1)} %get-tuple-element.46.inp, ...), custom_call_target="tpu_custom_call" | custom-call | flops 905969664 | bytes 3522560 | tf_op jit(solution)/shard_map/pallas_call | solution.py:34
  19.4 0.0 collective-permute-done.2.y_odd
  19.4 0.7 %collective-permute-done.3.y_even = bf16[432,128]{1,0:T(8,128)(2,1)S(1)} collective-permute-done((bf16[432,128]{1,0:T(8,128)(2,1)S(1)}, bf16[432,128]{1,0:T(8,128)(2,1)S(1)}, u32[]{:S(2)}, u32[]{:S(2)}) %collective-permute-start.3) | collective-permute-done | bytes 110624 | tf_op jit(solution)/shard_map/ppermute | solution.py:637
  20.1 2.0 %shard_map.80 = (f32[64,3456]{1,0:T(8,128)S(1)}, f32[64,3456]{1,0:T(8,128)S(1)}, f32[1024,128]{1,0:T(8,128)S(1)}, f32[1600,128]{1,0:T(8,128)S(1)}) custom-call(f32[784,128]{1,0:T(8,128)S(1)} %get-tuple-element.51.deep_in, f32[784,128]{1,0:T(8,128)S(1)} %get-tuple-element.52.deep_g, bf16[48,128]{1,0:T(8,128)(2,1)S(1)} %get-tuple-element.56.marks3, ...), custom_call_target="tpu_custom_call" | custom-call | flops 905969664 | bytes 5361664 | tf_op jit(solution)/shard_map/pallas_call | solution.py:34
  22.0 0.1 collective-permute-start.5
  22.1 1.8 %shard_map.81 = (f32[64,3456]{1,0:T(8,128)S(1)}, f32[64,3456]{1,0:T(8,128)S(1)}, bf16[512,1152]{1,0:T(8,128)(2,1)S(1)}) custom-call(f32[1600,128]{1,0:T(8,128)S(1)} %get-tuple-element.60.grid_g, f32[1024,128]{1,0:T(8,128)S(1)} %get-tuple-element.61.act, f32[640,128]{1,0:T(8,128)S(1)} %get-tuple-element.62.inner, ...), custom_call_target="tpu_custom_call" | custom-call | flops 905969664 | bytes 5902336 | tf_op jit(solution)/shard_map/pallas_call | solution.py:34
  23.9 0.6 collective-permute-start.4
  24.5 0.1 collective-permute-done.5.got
  24.5 0.1 shard_map.83
  24.6 1.5 %collective-permute-start.6 = (bf16[16,3456]{1,0:T(8,128)(2,1)S(1)}, bf16[16,3456]{1,0:T(8,128)(2,1)S(1)}, u32[]{:S(2)}, u32[]{:S(2)}) collective-permute-start(bf16[16,3456]{1,0:T(8,128)(2,1)S(1)} %get-tuple-element.70), channel_id=1, source_target_pairs={{0,3},{1,2},{2,1},{3,0},{4,7},{5,6},{6,5},{7,4},{8,11},{9,10},{10,... | collective-permute-start | bytes 331784 | tf_op jit(solution)/shard_map/ppermute | solution.py:408
  26.1 1.0 %collective-permute-start.7 = (bf16[16,3456]{1,0:T(8,128)(2,1)S(1)}, bf16[16,3456]{1,0:T(8,128)(2,1)S(1)}, u32[]{:S(2)}, u32[]{:S(2)}) collective-permute-start(bf16[16,3456]{1,0:T(8,128)(2,1)S(1)} %get-tuple-element.71), channel_id=1, source_target_pairs={{0,1},{1,0},{2,3},{3,2},{4,5},{5,4},{6,7},{7,6},{8,9},{9,8},{10,11... | collective-permute-start | bytes 331784 | tf_op jit(solution)/shard_map/ppermute | solution.py:408
  27.1 1.0 %collective-permute-start.8 = (bf16[16,3456]{1,0:T(8,128)(2,1)S(1)}, bf16[16,3456]{1,0:T(8,128)(2,1)S(1)}, u32[]{:S(2)}, u32[]{:S(2)}) collective-permute-start(bf16[16,3456]{1,0:T(8,128)(2,1)S(1)} %get-tuple-element.72), channel_id=1, source_target_pairs={{0,2},{1,3},{2,0},{3,1},{4,6},{5,7},{6,4},{7,5},{8,10},{9,11},{10,... | collective-permute-start | bytes 331784 | tf_op jit(solution)/shard_map/ppermute | solution.py:408
  28.2 0.0 collective-permute-done.4.got
  28.2 0.1 shard_map.82
  28.3 2.1 %collective-permute-start.10 = (bf16[16,3456]{1,0:T(8,128)(2,1)S(1)}, bf16[16,3456]{1,0:T(8,128)(2,1)S(1)}, u32[]{:S(2)}, u32[]{:S(2)}) collective-permute-start(bf16[16,3456]{1,0:T(8,128)(2,1)S(1)} %get-tuple-element.75), channel_id=1, source_target_pairs={{0,4},{1,5},{2,6},{3,7},{4,0},{5,1},{6,2},{7,3},{8,12},{9,13},{10,... | collective-permute-start | bytes 331784 | tf_op jit(solution)/shard_map/ppermute | solution.py:408
  30.4 1.0 %collective-permute-start.11 = (bf16[16,3456]{1,0:T(8,128)(2,1)S(1)}, bf16[16,3456]{1,0:T(8,128)(2,1)S(1)}, u32[]{:S(2)}, u32[]{:S(2)}) collective-permute-start(bf16[16,3456]{1,0:T(8,128)(2,1)S(1)} %get-tuple-element.76), channel_id=1, source_target_pairs={{0,1},{1,0},{2,3},{3,2},{4,5},{5,4},{6,7},{7,6},{8,9},{9,8},{10,11... | collective-permute-start | bytes 331784 | tf_op jit(solution)/shard_map/ppermute | solution.py:408
  31.4 0.1 collective-permute-done.6.refs_1_
  31.5 2.5 %collective-permute-start.9 = (bf16[16,3456]{1,0:T(8,128)(2,1)S(1)}, bf16[16,3456]{1,0:T(8,128)(2,1)S(1)}, u32[]{:S(2)}, u32[]{:S(2)}) collective-permute-start(bf16[16,3456]{1,0:T(8,128)(2,1)S(1)} %get-tuple-element.74), channel_id=1, source_target_pairs={{0,5},{1,4},{2,7},{3,6},{4,1},{5,0},{6,3},{7,2},{8,13},{9,12},{10,... | collective-permute-start | bytes 331784 | tf_op jit(solution)/shard_map/ppermute | solution.py:408
  34.0 0.0 collective-permute-done.7.refs_2_
  34.0 0.0 collective-permute-done.8.refs_3_
  34.0 0.1 shard_map.84.one
  34.0 1.7 %collective-permute-start.12 = (bf16[16,3456]{1,0:T(8,128)(2,1)S(1)}, bf16[16,3456]{1,0:T(8,128)(2,1)S(1)}, u32[]{:S(2)}, u32[]{:S(2)}) collective-permute-start(bf16[16,3456]{1,0:T(8,128)(2,1)S(1)} %shard_map.84.one), channel_id=1, source_target_pairs={{0,4},{1,5},{2,6},{3,7},{4,0},{5,1},{6,2},{7,3},{8,12},{9,13},{10,... | collective-permute-start | bytes 331784 | tf_op jit(solution)/shard_map/ppermute | solution.py:408
  35.7 0.0 collective-permute-done.10.refs_2_
  35.7 0.0 collective-permute-done.11.refs_3_
  35.7 2.6 %collective-permute-done.9.refs_1_ = bf16[16,3456]{1,0:T(8,128)(2,1)S(1)} collective-permute-done((bf16[16,3456]{1,0:T(8,128)(2,1)S(1)}, bf16[16,3456]{1,0:T(8,128)(2,1)S(1)}, u32[]{:S(2)}, u32[]{:S(2)}) %collective-permute-start.9) | collective-permute-done | bytes 110624 | tf_op jit(solution)/shard_map/ppermute | solution.py:408
  38.3 0.1 shard_map.85.one
  38.4 1.0 %collective-permute-start.13 = (bf16[16,3456]{1,0:T(8,128)(2,1)S(1)}, bf16[16,3456]{1,0:T(8,128)(2,1)S(1)}, u32[]{:S(2)}, u32[]{:S(2)}) collective-permute-start(bf16[16,3456]{1,0:T(8,128)(2,1)S(1)} %shard_map.85.one), channel_id=1, source_target_pairs={{0,2},{1,3},{2,0},{3,1},{4,6},{5,7},{6,4},{7,5},{8,10},{9,11},{10,... | collective-permute-start | bytes 331784 | tf_op jit(solution)/shard_map/ppermute | solution.py:408
  39.4 0.0 collective-permute-done.12.two
  39.5 1.6 %collective-permute-start.14 = (bf16[16,3456]{1,0:T(8,128)(2,1)S(1)}, bf16[16,3456]{1,0:T(8,128)(2,1)S(1)}, u32[]{:S(2)}, u32[]{:S(2)}) collective-permute-start(bf16[16,3456]{1,0:T(8,128)(2,1)S(1)} %shard_map.86.one), channel_id=1, source_target_pairs={{0,8},{1,9},{2,10},{3,11},{4,12},{5,13},{6,14},{7,15},{8,0},{9,1},... | collective-permute-start | bytes 331784 | tf_op jit(solution)/shard_map/ppermute | solution.py:408
  41.0 1.5 %shard_map.87 = bf16[512,128]{1,0:T(8,128)(2,1)} custom-call(bf16[512,1152]{1,0:T(8,128)(2,1)S(1)} %get-tuple-element.79.st_own, bf16[512,128]{1,0:T(8,128)(2,1)S(1)} %get-tuple-element.47.grads, bf16[48,128]{1,0:T(8,128)(2,1)S(1)} %get-tuple-element.56.marks3, bf16[384,1152]{1,0:T(8,128)(2,1)S(1)} %get-tuple-element.80.w1_wide), custom_call_target="tpu_custom_call" | custom-call | flops 452984832 | bytes 2338816 | tf_op jit(solution)/shard_map/pallas_call | solution.py:34
  42.5 0.7 %collective-permute-done.13.two = bf16[16,3456]{1,0:T(8,128)(2,1)S(1)} collective-permute-done((bf16[16,3456]{1,0:T(8,128)(2,1)S(1)}, bf16[16,3456]{1,0:T(8,128)(2,1)S(1)}, u32[]{:S(2)}, u32[]{:S(2)}) %collective-permute-start.13) | collective-permute-done | bytes 110624 | tf_op jit(solution)/shard_map/ppermute | solution.py:408
  43.2 1.0 %collective-permute-start.15 = (bf16[16,3456]{1,0:T(8,128)(2,1)S(1)}, bf16[16,3456]{1,0:T(8,128)(2,1)S(1)}, u32[]{:S(2)}, u32[]{:S(2)}) collective-permute-start(bf16[16,3456]{1,0:T(8,128)(2,1)S(1)} %shard_map.88.one), channel_id=1, source_target_pairs={{0,8},{1,9},{2,10},{3,11},{4,12},{5,13},{6,14},{7,15},{8,0},{9,1},... | collective-permute-start | bytes 331784 | tf_op jit(solution)/shard_map/ppermute | solution.py:408
  44.2 0.9 %collective-permute-done.14.two = bf16[16,3456]{1,0:T(8,128)(2,1)S(1)} collective-permute-done((bf16[16,3456]{1,0:T(8,128)(2,1)S(1)}, bf16[16,3456]{1,0:T(8,128)(2,1)S(1)}, u32[]{:S(2)}, u32[]{:S(2)}) %collective-permute-start.14) | collective-permute-done | bytes 110624 | tf_op jit(solution)/shard_map/ppermute | solution.py:408
  45.2 1.5 %collective-permute-start.20 = (bf16[432,128]{1,0:T(8,128)(2,1)S(1)}, bf16[432,128]{1,0:T(8,128)(2,1)S(1)}, u32[]{:S(2)}, u32[]{:S(2)}) collective-permute-start(bf16[432,128]{1,0:T(8,128)(2,1)S(1)} %shard_map.89.refs_0_), channel_id=1, source_target_pairs={{0,3},{1,2},{2,1},{3,0},{4,7},{5,6},{6,5},{7,4},{8,11},{9,10},{10,... | collective-permute-start | bytes 331784 | tf_op jit(solution)/shard_map/ppermute | solution.py:408
  46.8 1.0 %collective-permute-start.21 = (bf16[432,128]{1,0:T(8,128)(2,1)S(1)}, bf16[432,128]{1,0:T(8,128)(2,1)S(1)}, u32[]{:S(2)}, u32[]{:S(2)}) collective-permute-start(bf16[432,128]{1,0:T(8,128)(2,1)S(1)} %shard_map.89.refs_0_), channel_id=1, source_target_pairs={{0,1},{1,0},{2,3},{3,2},{4,5},{5,4},{6,7},{7,6},{8,9},{9,8},{10,11... | collective-permute-start | bytes 331784 | tf_op jit(solution)/shard_map/ppermute | solution.py:408
  47.8 1.0 %collective-permute-start.22 = (bf16[432,128]{1,0:T(8,128)(2,1)S(1)}, bf16[432,128]{1,0:T(8,128)(2,1)S(1)}, u32[]{:S(2)}, u32[]{:S(2)}) collective-permute-start(bf16[432,128]{1,0:T(8,128)(2,1)S(1)} %shard_map.89.refs_0_), channel_id=1, source_target_pairs={{0,2},{1,3},{2,0},{3,1},{4,6},{5,7},{6,4},{7,5},{8,10},{9,11},{10,... | collective-permute-start | bytes 331784 | tf_op jit(solution)/shard_map/ppermute | solution.py:408
  48.8 0.2 collective-permute-done.15.two
  49.0 3.0 %collective-permute-start.16 = (bf16[432,128]{1,0:T(8,128)(2,1)S(1)}, bf16[432,128]{1,0:T(8,128)(2,1)S(1)}, u32[]{:S(2)}, u32[]{:S(2)}) collective-permute-start(bf16[432,128]{1,0:T(8,128)(2,1)S(1)} %shard_map.90.refs_0_), channel_id=1, source_target_pairs={{0,5},{1,4},{2,7},{3,6},{4,1},{5,0},{6,3},{7,2},{8,13},{9,12},{10,... | collective-permute-start | bytes 331784 | tf_op jit(solution)/shard_map/ppermute | solution.py:408
  52.1 0.0 collective-permute-start.17
  52.1 0.0 collective-permute-done.20.refs_1_
  52.1 1.0 %collective-permute-start.18 = (bf16[432,128]{1,0:T(8,128)(2,1)S(1)}, bf16[432,128]{1,0:T(8,128)(2,1)S(1)}, u32[]{:S(2)}, u32[]{:S(2)}) collective-permute-start(bf16[432,128]{1,0:T(8,128)(2,1)S(1)} %shard_map.90.refs_0_), channel_id=1, source_target_pairs={{0,1},{1,0},{2,3},{3,2},{4,5},{5,4},{6,7},{7,6},{8,9},{9,8},{10,11... | collective-permute-start | bytes 331784 | tf_op jit(solution)/shard_map/ppermute | solution.py:408
  53.1 0.0 collective-permute-done.21.refs_2_
  53.1 1.0 %collective-permute-done.22.refs_3_ = bf16[432,128]{1,0:T(8,128)(2,1)S(1)} collective-permute-done((bf16[432,128]{1,0:T(8,128)(2,1)S(1)}, bf16[432,128]{1,0:T(8,128)(2,1)S(1)}, u32[]{:S(2)}, u32[]{:S(2)}) %collective-permute-start.22) | collective-permute-done | bytes 110624 | tf_op jit(solution)/shard_map/ppermute | solution.py:408
  54.2 0.1 collective-permute-start.23
  54.2 0.6 collective-permute-done.16.refs_1_
  54.8 2.0 %collective-permute-done.17.refs_2_ = bf16[432,128]{1,0:T(8,128)(2,1)S(1)} collective-permute-done((bf16[432,128]{1,0:T(8,128)(2,1)S(1)}, bf16[432,128]{1,0:T(8,128)(2,1)S(1)}, u32[]{:S(2)}, u32[]{:S(2)}) %collective-permute-start.17) | collective-permute-done | bytes 110624 | tf_op jit(solution)/shard_map/ppermute | solution.py:408
  56.8 0.0 collective-permute-done.18.refs_3_
  56.8 0.1 shard_map.91.own
  56.9 0.1 collective-permute-start.19
  57.0 0.0 collective-permute-done.23.other
  57.0 1.3 %shard_map.94 = f32[3456,128]{1,0:T(8,128)} custom-call(bf16[1728,128]{1,0:T(8,128)(2,1)S(1)} %shard_map.93.own, bf16[1728,128]{1,0:T(8,128)(2,1)S(1)} %collective-permute-done.23.other), custom_call_target="tpu_custom_call" | custom-call | bytes 2654208 | tf_op jit(solution)/shard_map/pallas_call | solution.py:34
  58.3 0.4 collective-permute-done.19.other
  58.7 1.3 %shard_map.92 = f32[3456,128]{1,0:T(8,128)} custom-call(bf16[1728,128]{1,0:T(8,128)(2,1)S(1)} %shard_map.91.own, bf16[1728,128]{1,0:T(8,128)(2,1)S(1)} %collective-permute-done.19.other), custom_call_target="tpu_custom_call" | custom-call | bytes 2654208 | tf_op jit(solution)/shard_map/pallas_call | solution.py:34
  (5 shorter events, 0.2 us)
Async XLA Ops:
  2.4 8.6 %collective-permute-start = (bf16[272,128]{1,0:T(8,128)(2,1)S(1)}, bf16[272,128]{1,0:T(8,128)(2,1)S(1)}, u32[]{:S(2)}, u32[]{:S(2)}) collective-permute-start(bf16[272,128]{1,0:T(8,128)(2,1)S(1)} %get-tuple-element.49), channel_id=1, source_target_pairs={{1,2},{2,1},{5,6},{6,5},{9,10},{10,9},{13,14},{14,13},{17,18},{18,... | collective-permute-start | bytes 208904 | tf_op jit(solution)/shard_map/ppermute | solution.py:637
  3.1 9.0 %collective-permute-start.1 = (bf16[272,128]{1,0:T(8,128)(2,1)S(1)}, bf16[272,128]{1,0:T(8,128)(2,1)S(1)}, u32[]{:S(2)}, u32[]{:S(2)}) collective-permute-start(bf16[272,128]{1,0:T(8,128)(2,1)S(1)} %get-tuple-element.50), channel_id=1, source_target_pairs={{0,1},{1,0},{2,3},{3,2},{4,5},{5,4},{6,7},{7,6},{8,9},{9,8},{10,11... | collective-permute-start | bytes 208904 | tf_op jit(solution)/shard_map/ppermute | solution.py:637
  12.2 7.2 %collective-permute-start.2 = (bf16[432,128]{1,0:T(8,128)(2,1)S(1)}, bf16[432,128]{1,0:T(8,128)(2,1)S(1)}, u32[]{:S(2)}, u32[]{:S(2)}) collective-permute-start(bf16[432,128]{1,0:T(8,128)(2,1)S(1)} %get-tuple-element.57), channel_id=1, source_target_pairs={{4,8},{8,4},{5,9},{9,5},{6,10},{10,6},{7,11},{11,7},{20,24},{24,20... | collective-permute-start | bytes 331784 | tf_op jit(solution)/shard_map/ppermute | solution.py:637
  12.9 7.2 %collective-permute-start.3 = (bf16[432,128]{1,0:T(8,128)(2,1)S(1)}, bf16[432,128]{1,0:T(8,128)(2,1)S(1)}, u32[]{:S(2)}, u32[]{:S(2)}) collective-permute-start(bf16[432,128]{1,0:T(8,128)(2,1)S(1)} %get-tuple-element.58), channel_id=1, source_target_pairs={{0,4},{4,0},{1,5},{5,1},{2,6},{6,2},{3,7},{7,3},{8,12},{12,8},{9,1... | collective-permute-start | bytes 331784 | tf_op jit(solution)/shard_map/ppermute | solution.py:637
  22.0 2.5 %collective-permute-start.5 = (f32[64,3456]{1,0:T(8,128)S(1)}, f32[64,3456]{1,0:T(8,128)S(1)}, u32[]{:S(2)}, u32[]{:S(2)}) collective-permute-start(f32[64,3456]{1,0:T(8,128)S(1)} %get-tuple-element.67), channel_id=1, source_target_pairs={{0,16},{16,0},{1,17},{17,1},{2,18},{18,2},{3,19},{19,3},{4,20},{20... | collective-permute-start | bytes 2654216 | tf_op jit(solution)/shard_map/ppermute | solution.py:398
  23.9 4.3 %collective-permute-start.4 = (f32[64,3456]{1,0:T(8,128)S(1)}, f32[64,3456]{1,0:T(8,128)S(1)}, u32[]{:S(2)}, u32[]{:S(2)}) collective-permute-start(f32[64,3456]{1,0:T(8,128)S(1)} %get-tuple-element.64), channel_id=1, source_target_pairs={{0,16},{16,0},{1,17},{17,1},{2,18},{18,2},{3,19},{19,3},{4,20},{20... | collective-permute-start | bytes 2654216 | tf_op jit(solution)/shard_map/ppermute | solution.py:398
  24.6 6.9 %collective-permute-start.6 = (bf16[16,3456]{1,0:T(8,128)(2,1)S(1)}, bf16[16,3456]{1,0:T(8,128)(2,1)S(1)}, u32[]{:S(2)}, u32[]{:S(2)}) collective-permute-start(bf16[16,3456]{1,0:T(8,128)(2,1)S(1)} %get-tuple-element.70), channel_id=1, source_target_pairs={{0,3},{1,2},{2,1},{3,0},{4,7},{5,6},{6,5},{7,4},{8,11},{9,10},{10,... | collective-permute-start | bytes 331784 | tf_op jit(solution)/shard_map/ppermute | solution.py:408
  26.1 7.8 %collective-permute-start.7 = (bf16[16,3456]{1,0:T(8,128)(2,1)S(1)}, bf16[16,3456]{1,0:T(8,128)(2,1)S(1)}, u32[]{:S(2)}, u32[]{:S(2)}) collective-permute-start(bf16[16,3456]{1,0:T(8,128)(2,1)S(1)} %get-tuple-element.71), channel_id=1, source_target_pairs={{0,1},{1,0},{2,3},{3,2},{4,5},{5,4},{6,7},{7,6},{8,9},{9,8},{10,11... | collective-permute-start | bytes 331784 | tf_op jit(solution)/shard_map/ppermute | solution.py:408
  27.1 6.8 %collective-permute-start.8 = (bf16[16,3456]{1,0:T(8,128)(2,1)S(1)}, bf16[16,3456]{1,0:T(8,128)(2,1)S(1)}, u32[]{:S(2)}, u32[]{:S(2)}) collective-permute-start(bf16[16,3456]{1,0:T(8,128)(2,1)S(1)} %get-tuple-element.72), channel_id=1, source_target_pairs={{0,2},{1,3},{2,0},{3,1},{4,6},{5,7},{6,4},{7,5},{8,10},{9,11},{10,... | collective-permute-start | bytes 331784 | tf_op jit(solution)/shard_map/ppermute | solution.py:408
  28.3 7.4 %collective-permute-start.10 = (bf16[16,3456]{1,0:T(8,128)(2,1)S(1)}, bf16[16,3456]{1,0:T(8,128)(2,1)S(1)}, u32[]{:S(2)}, u32[]{:S(2)}) collective-permute-start(bf16[16,3456]{1,0:T(8,128)(2,1)S(1)} %get-tuple-element.75), channel_id=1, source_target_pairs={{0,4},{1,5},{2,6},{3,7},{4,0},{5,1},{6,2},{7,3},{8,12},{9,13},{10,... | collective-permute-start | bytes 331784 | tf_op jit(solution)/shard_map/ppermute | solution.py:408
  30.4 5.3 %collective-permute-start.11 = (bf16[16,3456]{1,0:T(8,128)(2,1)S(1)}, bf16[16,3456]{1,0:T(8,128)(2,1)S(1)}, u32[]{:S(2)}, u32[]{:S(2)}) collective-permute-start(bf16[16,3456]{1,0:T(8,128)(2,1)S(1)} %get-tuple-element.76), channel_id=1, source_target_pairs={{0,1},{1,0},{2,3},{3,2},{4,5},{5,4},{6,7},{7,6},{8,9},{9,8},{10,11... | collective-permute-start | bytes 331784 | tf_op jit(solution)/shard_map/ppermute | solution.py:408
  31.5 6.8 %collective-permute-start.9 = (bf16[16,3456]{1,0:T(8,128)(2,1)S(1)}, bf16[16,3456]{1,0:T(8,128)(2,1)S(1)}, u32[]{:S(2)}, u32[]{:S(2)}) collective-permute-start(bf16[16,3456]{1,0:T(8,128)(2,1)S(1)} %get-tuple-element.74), channel_id=1, source_target_pairs={{0,5},{1,4},{2,7},{3,6},{4,1},{5,0},{6,3},{7,2},{8,13},{9,12},{10,... | collective-permute-start | bytes 331784 | tf_op jit(solution)/shard_map/ppermute | solution.py:408
  34.0 5.4 %collective-permute-start.12 = (bf16[16,3456]{1,0:T(8,128)(2,1)S(1)}, bf16[16,3456]{1,0:T(8,128)(2,1)S(1)}, u32[]{:S(2)}, u32[]{:S(2)}) collective-permute-start(bf16[16,3456]{1,0:T(8,128)(2,1)S(1)} %shard_map.84.one), channel_id=1, source_target_pairs={{0,4},{1,5},{2,6},{3,7},{4,0},{5,1},{6,2},{7,3},{8,12},{9,13},{10,... | collective-permute-start | bytes 331784 | tf_op jit(solution)/shard_map/ppermute | solution.py:408
  38.4 4.8 %collective-permute-start.13 = (bf16[16,3456]{1,0:T(8,128)(2,1)S(1)}, bf16[16,3456]{1,0:T(8,128)(2,1)S(1)}, u32[]{:S(2)}, u32[]{:S(2)}) collective-permute-start(bf16[16,3456]{1,0:T(8,128)(2,1)S(1)} %shard_map.85.one), channel_id=1, source_target_pairs={{0,2},{1,3},{2,0},{3,1},{4,6},{5,7},{6,4},{7,5},{8,10},{9,11},{10,... | collective-permute-start | bytes 331784 | tf_op jit(solution)/shard_map/ppermute | solution.py:408
  39.5 5.7 %collective-permute-start.14 = (bf16[16,3456]{1,0:T(8,128)(2,1)S(1)}, bf16[16,3456]{1,0:T(8,128)(2,1)S(1)}, u32[]{:S(2)}, u32[]{:S(2)}) collective-permute-start(bf16[16,3456]{1,0:T(8,128)(2,1)S(1)} %shard_map.86.one), channel_id=1, source_target_pairs={{0,8},{1,9},{2,10},{3,11},{4,12},{5,13},{6,14},{7,15},{8,0},{9,1},... | collective-permute-start | bytes 331784 | tf_op jit(solution)/shard_map/ppermute | solution.py:408
  43.2 5.8 %collective-permute-start.15 = (bf16[16,3456]{1,0:T(8,128)(2,1)S(1)}, bf16[16,3456]{1,0:T(8,128)(2,1)S(1)}, u32[]{:S(2)}, u32[]{:S(2)}) collective-permute-start(bf16[16,3456]{1,0:T(8,128)(2,1)S(1)} %shard_map.88.one), channel_id=1, source_target_pairs={{0,8},{1,9},{2,10},{3,11},{4,12},{5,13},{6,14},{7,15},{8,0},{9,1},... | collective-permute-start | bytes 331784 | tf_op jit(solution)/shard_map/ppermute | solution.py:408
  45.2 6.9 %collective-permute-start.20 = (bf16[432,128]{1,0:T(8,128)(2,1)S(1)}, bf16[432,128]{1,0:T(8,128)(2,1)S(1)}, u32[]{:S(2)}, u32[]{:S(2)}) collective-permute-start(bf16[432,128]{1,0:T(8,128)(2,1)S(1)} %shard_map.89.refs_0_), channel_id=1, source_target_pairs={{0,3},{1,2},{2,1},{3,0},{4,7},{5,6},{6,5},{7,4},{8,11},{9,10},{10,... | collective-permute-start | bytes 331784 | tf_op jit(solution)/shard_map/ppermute | solution.py:408
  46.8 6.4 %collective-permute-start.21 = (bf16[432,128]{1,0:T(8,128)(2,1)S(1)}, bf16[432,128]{1,0:T(8,128)(2,1)S(1)}, u32[]{:S(2)}, u32[]{:S(2)}) collective-permute-start(bf16[432,128]{1,0:T(8,128)(2,1)S(1)} %shard_map.89.refs_0_), channel_id=1, source_target_pairs={{0,1},{1,0},{2,3},{3,2},{4,5},{5,4},{6,7},{7,6},{8,9},{9,8},{10,11... | collective-permute-start | bytes 331784 | tf_op jit(solution)/shard_map/ppermute | solution.py:408
  47.8 6.3 %collective-permute-start.22 = (bf16[432,128]{1,0:T(8,128)(2,1)S(1)}, bf16[432,128]{1,0:T(8,128)(2,1)S(1)}, u32[]{:S(2)}, u32[]{:S(2)}) collective-permute-start(bf16[432,128]{1,0:T(8,128)(2,1)S(1)} %shard_map.89.refs_0_), channel_id=1, source_target_pairs={{0,2},{1,3},{2,0},{3,1},{4,6},{5,7},{6,4},{7,5},{8,10},{9,11},{10,... | collective-permute-start | bytes 331784 | tf_op jit(solution)/shard_map/ppermute | solution.py:408
  49.0 5.8 %collective-permute-start.16 = (bf16[432,128]{1,0:T(8,128)(2,1)S(1)}, bf16[432,128]{1,0:T(8,128)(2,1)S(1)}, u32[]{:S(2)}, u32[]{:S(2)}) collective-permute-start(bf16[432,128]{1,0:T(8,128)(2,1)S(1)} %shard_map.90.refs_0_), channel_id=1, source_target_pairs={{0,5},{1,4},{2,7},{3,6},{4,1},{5,0},{6,3},{7,2},{8,13},{9,12},{10,... | collective-permute-start | bytes 331784 | tf_op jit(solution)/shard_map/ppermute | solution.py:408
  52.1 4.7 %collective-permute-start.17 = (bf16[432,128]{1,0:T(8,128)(2,1)S(1)}, bf16[432,128]{1,0:T(8,128)(2,1)S(1)}, u32[]{:S(2)}, u32[]{:S(2)}) collective-permute-start(bf16[432,128]{1,0:T(8,128)(2,1)S(1)} %shard_map.90.refs_0_), channel_id=1, source_target_pairs={{0,4},{1,5},{2,6},{3,7},{4,0},{5,1},{6,2},{7,3},{8,12},{9,13},{10,... | collective-permute-start | bytes 331784 | tf_op jit(solution)/shard_map/ppermute | solution.py:408
  52.1 4.7 %collective-permute-start.18 = (bf16[432,128]{1,0:T(8,128)(2,1)S(1)}, bf16[432,128]{1,0:T(8,128)(2,1)S(1)}, u32[]{:S(2)}, u32[]{:S(2)}) collective-permute-start(bf16[432,128]{1,0:T(8,128)(2,1)S(1)} %shard_map.90.refs_0_), channel_id=1, source_target_pairs={{0,1},{1,0},{2,3},{3,2},{4,5},{5,4},{6,7},{7,6},{8,9},{9,8},{10,11... | collective-permute-start | bytes 331784 | tf_op jit(solution)/shard_map/ppermute | solution.py:408
  54.2 2.8 %collective-permute-start.23 = (bf16[1728,128]{1,0:T(8,128)(2,1)S(1)}, bf16[1728,128]{1,0:T(8,128)(2,1)S(1)}, u32[]{:S(2)}, u32[]{:S(2)}) collective-permute-start(bf16[1728,128]{1,0:T(8,128)(2,1)S(1)} %shard_map.93.own), channel_id=1, source_target_pairs={{0,16},{16,0},{1,17},{17,1},{2,18},{18,2},{3,19},{19,3},{4,20},{20... | collective-permute-start | bytes 1327112 | tf_op jit(solution)/shard_map/ppermute | solution.py:398
  56.9 1.9 %collective-permute-start.19 = (bf16[1728,128]{1,0:T(8,128)(2,1)S(1)}, bf16[1728,128]{1,0:T(8,128)(2,1)S(1)}, u32[]{:S(2)}, u32[]{:S(2)}) collective-permute-start(bf16[1728,128]{1,0:T(8,128)(2,1)S(1)} %shard_map.91.own), channel_id=1, source_target_pairs={{0,16},{16,0},{1,17},{17,1},{2,18},{18,2},{3,19},{19,3},{4,20},{20... | collective-permute-start | bytes 1327112 | tf_op jit(solution)/shard_map/ppermute | solution.py:398

commit v5 on v4

--- a/solution.py
+++ b/solution.py
@@ -16,6 +16,7 @@
 INNER_PITCH = 80
 OUTER_PITCH = 48
 EDGE = 24
+LANES = 32
 SPARE = 16
 TAPS = 27
 INNER = 4
@@ -99,8 +100,11 @@
     left, right = sides(slice(4 * lines, 4 * lines + mask_rows))
     for at, rows in enumerate((left, marks[...].astype(F32), right)):
         marks3[at * mask_rows : (at + 1) * mask_rows, :] = rows.astype(BF)
+    lane = lax.broadcasted_iota(jnp.int32, (mask_rows, 128), 1)
+    own = marks[...].astype(F32)
+    packed = jnp.where(lane < LANES, left, jnp.where(lane < 2 * LANES, own, right)).astype(BF)
     for ref in (even, odd):
-        ref[4 * planes * GROWN :, :] = marks3[...]
+        ref[4 * planes * GROWN :, :] = packed
     side = parity(4)
     for at, (src, dst) in enumerate(((inp, deep_in), (grads, deep_g))):
         dst[lines * GROWN :, :] = jnp.zeros((SPARE, 128), F32)
@@ -217,32 +221,18 @@
                     )
 
 
-def emit(core, at, value, kept, sent):
-    half = value.shape[0] // 2
-    columns = slice(at, at + value.shape[1])
-
-    @pl.when(core == 0)
-    def _():
-        kept[:, columns] = value[:half]
-        sent[:, columns] = value[half:]
-
-    @pl.when(core == 1)
-    def _():
-        kept[:, columns] = value[half:]
-        sent[:, columns] = value[:half]
-
-
 def marked(planes, mask_rows, marks3, y_even, y_odd):
     tail = 4 * planes * GROWN
     swapped = parity(4) == 0
 
     def mark(by, bz, e):
-        at = bz * mask_rows + e
         if by == 1:
+            at = bz * mask_rows + e
             return marks3[at : at + 1, :].astype(F32)
-        one = y_even[tail + at : tail + at + 1, :].astype(F32)
-        two = y_odd[tail + at : tail + at + 1, :].astype(F32)
-        return jnp.where(swapped, two, one) if by == 0 else jnp.where(swapped, one, two)
+        one = y_even[tail + e : tail + e + 1, :].astype(F32)
+        two = y_odd[tail + e : tail + e + 1, :].astype(F32)
+        row = jnp.where(swapped, two, one) if by == 0 else jnp.where(swapped, one, two)
+        return row[:, LANES * bz : LANES * bz + 1]
 
     return mark
 
@@ -304,22 +294,31 @@
 OUTER_PARTS = ((0, EDGE), (PITCH - EDGE - TILE, EDGE))
 
 
-def correlate(turned_rows, stacked, columns):
-    left = jnp.concatenate([turned_rows[:, a * FACE : a * FACE + columns] for a in range(3)], 0)
-    return dot(left, stacked) * unscale
+def correlate(core, turned_rows, stacked, columns, kept, sent):
+    half = kept.shape[0]
+    third = stacked.shape[1]
+    halves = [pl.ds(pl.multiple_of(side * half, half), half) for side in (core, 1 - core)]
+    left = [
+        turned_rows[rows, a * FACE : a * FACE + columns] for rows in halves for a in range(3)
+    ]
+    part = dot(jnp.concatenate(left, 0), stacked) * unscale
+    for n, out in enumerate((kept, sent)):
+        for a in range(3):
+            at = (n * 3 + a) * half
+            out[:, a * third : (a + 1) * third] = part[at : at + half]
+    pad_terms(kept, sent)
 
 
 def forward(
     planes, deep, mask_rows,
     deep_in, deep_g, marks3, y_odd, y_even, inner, w1_tall,
     kept, sent, act, grid_g,
-    grid_in, outer, pair, single, st_own, hidden,
+    grid_in, outer, pair, single, st_own, hidden, hid_t,
 ):
     core = lax.axis_index("dp")
     size_x = planes - 4 * deep
     n_out = size_x + 2 * deep
     first = 1 - deep
-    third = 9 * 128
     spread(planes, first, 0, deep_in, y_even, y_odd, grid_in)
     stack(planes, first, IN_PITCH, OUTER_PARTS, grid_in, outer, OUTER_PITCH, False)
     pair[...] = dot(outer[...], w1_tall[:, 0:256])
@@ -339,10 +338,8 @@
             pre = own_lines(act, (p + deep) * PITCH + (y + 1) * GROWN + 1)
             to = (p + 1 + 2 * deep) * FACE + y * TILE
             hidden[to : to + 2 * TILE, :] = pre * jax.nn.sigmoid(pre) * keep
-    part = correlate(hidden[...].T.astype(BF), st_own[...], planes * FACE)
-    for a in range(3):
-        emit(core, a * third, part[a * 128 : (a + 1) * 128], kept, sent)
-    pad_terms(kept, sent)
+    hid_t[...] = hidden[...].T.astype(BF)
+    correlate(core, hid_t, st_own[...], planes * FACE, kept, sent)
 
 
 def backward(
@@ -354,7 +351,6 @@
     core = lax.axis_index("dp")
     size_x = planes - 4 * deep
     n_out = size_x + 2 * deep
-    third = 9 * 128
     mark = marked(planes, mask_rows, marks3, y_even, y_odd)
     in_line, in_depth = spans(PITCH, ((0, 0), (1, TILE), (RIM - 1, RIM - 1)))
     stack(planes, 1 - deep, IN_PITCH, OUTER_PARTS, grid_g, outer, OUTER_PITCH, True)
@@ -374,10 +370,7 @@
         grad = back * sigma * (1.0 + pre * (1.0 - sigma))
         pg[p * PITCH : (p + 1) * PITCH, :] = (grad * keep).astype(BF).astype(F32)
     stack_own(n_out, 0, PITCH, 0, pg, st_own)
-    part = correlate(in_t, st_own[...], n_out * FACE)
-    for a in range(3):
-        emit(core, a * third, part[a * 128 : (a + 1) * 128], kept, sent)
-    pad_terms(kept, sent)
+    correlate(core, in_t, st_own[...], n_out * FACE, kept, sent)
 
 
 def last(planes, deep, mask_rows, st_own, grads, marks3, w1_wide, result, pair, single):
@@ -408,8 +401,12 @@
     return lax.ppermute(value, ("dp", "blk"), pairs)
 
 
-PLANE = ((1, 2), (2, 1), (0, 3, 1, 2))
-MIXED = ((1, 4), (2, 4), (0, 3, 2, 1))
+PLANE = ((1, 2), (2, 1), ((0, 3, 1, 2), (0, 3, 1, 2)), ((0, 3, 1, 2), (0, 3, 2, 1)))
+MIXED = ((1, 4), (2, 4), ((0, 1, 3, 2), (0, 3, 2, 1)), ((0, 3, 2, 1), (0, 3, 2, 1)))
+
+
+def met(orders, n):
+    return jnp.where(lax.axis_index("dp") == 0, orders[0][n], orders[1][n])
 
 
 def spot(group):
@@ -421,8 +418,8 @@
 def split_rows(group, kept, got, own, *sent):
     me = spot(group)
     rows = own.shape[0]
-    for n, k in enumerate(group[2]):
-        at = pl.ds(pl.multiple_of((me ^ k) * rows, rows), rows)
+    for n in range(INNER):
+        at = pl.ds(pl.multiple_of((me ^ met(group[2], n)) * rows, rows), rows)
         value = kept[at, :] + got[at, :].astype(F32)
         if n == 0:
             own[...] = value
@@ -477,8 +474,8 @@
     me = spot(group)
     out = refs[INNER]
     rows = refs[0].shape[0]
-    for n, k in enumerate(group[2]):
-        out[pl.ds(pl.multiple_of((me ^ k) * rows, rows), rows), :] = refs[n][...]
+    for n in range(INNER):
+        out[pl.ds(pl.multiple_of((me ^ met(group[3], n)) * rows, rows), rows), :] = refs[n][...]
 
 
 def finish(own, other, out):
@@ -500,10 +497,10 @@
     return lax.optimization_barrier((value, *others))[0]
 
 
-def near(group, values):
+def near(group, values, orders):
     return [
-        cross(v, [one * (k % 2) + two * (k // 2) for one, two in group[:2]])
-        for v, k in zip(values, group[2][1:])
+        cross(v, [one * (k % 2) + two * (k // 2) for (one, two), k in zip(group, both)])
+        for v, both in list(zip(values, zip(*[order[1:] for order in orders])))
     ]
 
 
@@ -660,7 +657,7 @@
         scratch=[pltpu.VMEM((TAPS * width, width), F32)],
     )
     inp = after(inp, w2_wide)
-    edge = 4 * planes * GROWN + 3 * mask_rows
+    edge = 4 * planes * GROWN + mask_rows
     even, odd, deep_in, deep_g, marks3 = call(
         functools.partial(pack_lines, planes, mask_rows),
         [shape((edge, width), BF)] * 2
@@ -703,6 +700,7 @@
         + [
             pltpu.VMEM((planes * FACE, 9 * width), BF),
             pltpu.VMEM(((planes + 2) * FACE, width), F32),
+            pltpu.VMEM((width, (planes + 2) * FACE), BF),
         ],
         flops=2 * work,
     )
@@ -718,8 +716,8 @@
         flops=2 * work,
     )
     own_b, *send_b = split_stage(groups[1], kept_b, swap(sent_b, "dp", 1))
-    gots_a = near(groups[0], send_a)
-    gots_b = near(groups[1], send_b)
+    gots_a = near(groups[0], send_a, groups[0][2])
+    gots_b = near(groups[1], send_b, groups[1][2])
     own_a = after(own_a, own_b)
 
     def last_part(cue):
@@ -732,8 +730,8 @@
         )[0]
 
     value_a, value_b, result = across(groups, (own_a, own_b), (gots_a, gots_b), last_part)
-    gots_a = near(groups[0], [value_a] * (INNER - 1))
-    gots_b = near(groups[1], [value_b] * (INNER - 1))
+    gots_a = near(groups[0], [value_a] * (INNER - 1), groups[0][3])
+    gots_b = near(groups[1], [value_b] * (INNER - 1), groups[1][3])
     mine_a = back_stage(groups[0], value_a, gots_a)
     mine_b = back_stage(groups[1], value_b, gots_b)
     grad_second = finished(mine_a, swap(mine_a, "dp", 1))

time: 60.3 us -> 59.9 us (level)
  starting transfers between devices: 34.4 us -> 32.7 us
  waiting for transfers between devices: 10.4 us -> 11.9 us
    ppermute x16, starting transfers between devices: 22.1 us -> 20.4 us  [cross(): return lax.ppermute(value, ('dp', 'blk'), pairs)]
    ppermute x16, waiting for transfers between devices: 8.15 us -> 9.63 us  [cross(): return lax.ppermute(value, ('dp', 'blk'), pairs)]
  transfers between devices with their start and end apart: 24 -> 24, of which waited for: 12 -> 16; matrix products, arithmetic and copies ran while one was open for 3% -> 3% of each run, Pallas kernels for 13% -> 13%
where the time goes in v5:
time: 59.9 us; the launch traced here: 59.7 us
  starting transfers between devices  32.7 us (55%)
  waiting for transfers between devices  11.9 us (20%)
  Pallas kernels  11.1 us (19%)
  other arithmetic  2.59 us (4%)
  between operations  1.45 us (2%)
    ppermute x16, starting transfers between devices, cross(): return lax.ppermute(value, ('dp', 'blk'), pairs)  20.4 us
    pallas_call x19, Pallas kernels, call(): pl.pallas_call(body, out_shape=list(outs), in_specs=specs, out_specs=[VM]...  11.1 us
    ppermute x2, starting transfers between devices, beside(): lax.ppermute(one, 'blk', pairs[0])  10.2 us
    ppermute x16, waiting for transfers between devices, cross(): return lax.ppermute(value, ('dp', 'blk'), pairs)  9.63 us
    ppermute x2, waiting for transfers between devices, beside(): lax.ppermute(one, 'blk', pairs[0])  1.66 us
    another operation x1, other arithmetic, on_device(): jnp.stack([w_first, w_second])  1.6 us
    ppermute x2, starting transfers between devices, beside(): lax.ppermute(two, 'blk', pairs[1])  1.33 us
  transfers between devices with their start and end apart: 24, of which 16 were waited for; matrix products, arithmetic and copies ran while one was open for 3% of the time, Pallas kernels for 13%

profile of v5, /device:TPU:0, one launch (start us, length us, event | category | flops | bytes accessed | tf_op | source)
XLA Modules:
  0.0 59.7 jit_solution(15924064090605256071)
XLA Ops:
  1.3 1.0 %pad_maximum_fusion.1.both = bf16[2,512,128]{2,1,0:T(8,128)(2,1)S(1)} fusion(bf16[1,512,128]{2,1,0:T(8,128)(2,1)} %param.9, bf16[1,512,128]{2,1,0:T(8,128)(2,1)} %param.5), kind=kLoop, calls=%fused_computation.1 | loop fusion | flops 131072 | bytes 524288 | tf_op jit(solution)/shard_map/stack | solution.py:645
  2.3 0.1 shard_map.76
  2.4 0.7 %collective-permute-start = (bf16[272,128]{1,0:T(8,128)(2,1)S(1)}, bf16[272,128]{1,0:T(8,128)(2,1)S(1)}, u32[]{:S(2)}, u32[]{:S(2)}) collective-permute-start(bf16[272,128]{1,0:T(8,128)(2,1)S(1)} %get-tuple-element.49), channel_id=1, source_target_pairs={{1,2},{2,1},{5,6},{6,5},{9,10},{10,9},{13,14},{14,13},{17,18},{18,... | collective-permute-start | bytes 208904 | tf_op jit(solution)/shard_map/ppermute | solution.py:634
  3.1 5.7 %collective-permute-start.1 = (bf16[272,128]{1,0:T(8,128)(2,1)S(1)}, bf16[272,128]{1,0:T(8,128)(2,1)S(1)}, u32[]{:S(2)}, u32[]{:S(2)}) collective-permute-start(bf16[272,128]{1,0:T(8,128)(2,1)S(1)} %get-tuple-element.50), channel_id=1, source_target_pairs={{0,1},{1,0},{2,3},{3,2},{4,5},{5,4},{6,7},{7,6},{8,9},{9,8},{10,11... | collective-permute-start | bytes 208904 | tf_op jit(solution)/shard_map/ppermute | solution.py:634
  8.8 1.6 %pad_maximum_fusion.src = bf16[2,3456,128]{2,1,0:T(8,128)(2,1)S(1)} fusion(bf16[1,3456,128]{2,1,0:T(8,128)(2,1)} %bitcast.3, bf16[1,3456,128]{2,1,0:T(8,128)(2,1)} %bitcast.4), kind=kLoop, calls=%fused_computation | loop fusion | flops 884736 | bytes 3538944 | tf_op jit(solution)/shard_map/stack | solution.py:656
  10.4 0.6 %shard_map.77 = (bf16[384,1152]{1,0:T(8,128)(2,1)S(1)}, bf16[1152,384]{1,0:T(8,128)(2,1)S(1)}, bf16[384,1152]{1,0:T(8,128)(2,1)S(1)}) custom-call(bf16[2,3456,128]{2,1,0:T(8,128)(2,1)S(1)} %pad_maximum_fusion.src), custom_call_target="tpu_custom_call" | custom-call | bytes 4423680 | tf_op jit(solution)/shard_map/pallas_call | solution.py:35
  11.0 0.0 collective-permute-done.z_odd
  11.0 1.1 %collective-permute-done.1.z_even = bf16[272,128]{1,0:T(8,128)(2,1)S(1)} collective-permute-done((bf16[272,128]{1,0:T(8,128)(2,1)S(1)}, bf16[272,128]{1,0:T(8,128)(2,1)S(1)}, u32[]{:S(2)}, u32[]{:S(2)}) %collective-permute-start.1) | collective-permute-done | bytes 69664 | tf_op jit(solution)/shard_map/ppermute | solution.py:634
  12.1 0.1 shard_map.78
  12.2 0.7 %collective-permute-start.2 = (bf16[400,128]{1,0:T(8,128)(2,1)S(1)}, bf16[400,128]{1,0:T(8,128)(2,1)S(1)}, u32[]{:S(2)}, u32[]{:S(2)}) collective-permute-start(bf16[400,128]{1,0:T(8,128)(2,1)S(1)} %get-tuple-element.57), channel_id=1, source_target_pairs={{4,8},{8,4},{5,9},{9,5},{6,10},{10,6},{7,11},{11,7},{20,24},{24,20... | collective-permute-start | bytes 307208 | tf_op jit(solution)/shard_map/ppermute | solution.py:634
  12.9 4.5 %collective-permute-start.3 = (bf16[400,128]{1,0:T(8,128)(2,1)S(1)}, bf16[400,128]{1,0:T(8,128)(2,1)S(1)}, u32[]{:S(2)}, u32[]{:S(2)}) collective-permute-start(bf16[400,128]{1,0:T(8,128)(2,1)S(1)} %get-tuple-element.58), channel_id=1, source_target_pairs={{0,4},{4,0},{1,5},{5,1},{2,6},{6,2},{3,7},{7,3},{8,12},{12,8},{9,1... | collective-permute-start | bytes 307208 | tf_op jit(solution)/shard_map/ppermute | solution.py:634
  17.3 2.0 %shard_map.79 = (f32[640,128]{1,0:T(8,128)S(1)}, f32[640,128]{1,0:T(8,128)S(1)}, bf16[128,640]{1,0:T(8,128)(2,1)S(1)}) custom-call(f32[784,128]{1,0:T(8,128)S(1)} %get-tuple-element.51.deep_in, f32[784,128]{1,0:T(8,128)S(1)} %get-tuple-element.52.deep_g, bf16[512,128]{1,0:T(8,128)(2,1)S(1)} %get-tuple-element.46.inp, ...), custom_call_target="tpu_custom_call" | custom-call | flops 905969664 | bytes 3522560 | tf_op jit(solution)/shard_map/pallas_call | solution.py:35
  19.4 0.0 collective-permute-done.2.y_odd
  19.4 0.6 collective-permute-done.3.y_even
  20.0 1.9 %shard_map.80 = (f32[64,3456]{1,0:T(8,128)S(1)}, f32[64,3456]{1,0:T(8,128)S(1)}, f32[1024,128]{1,0:T(8,128)S(1)}, f32[1600,128]{1,0:T(8,128)S(1)}) custom-call(f32[784,128]{1,0:T(8,128)S(1)} %get-tuple-element.51.deep_in, f32[784,128]{1,0:T(8,128)S(1)} %get-tuple-element.52.deep_g, bf16[48,128]{1,0:T(8,128)(2,1)S(1)} %get-tuple-element.56.marks3, ...), custom_call_target="tpu_custom_call" | custom-call | flops 905969664 | bytes 5345280 | tf_op jit(solution)/shard_map/pallas_call | solution.py:35
  21.9 0.1 collective-permute-start.5
  22.0 1.7 %shard_map.81 = (f32[64,3456]{1,0:T(8,128)S(1)}, f32[64,3456]{1,0:T(8,128)S(1)}, bf16[512,1152]{1,0:T(8,128)(2,1)S(1)}) custom-call(f32[1600,128]{1,0:T(8,128)S(1)} %get-tuple-element.60.grid_g, f32[1024,128]{1,0:T(8,128)S(1)} %get-tuple-element.61.act, f32[640,128]{1,0:T(8,128)S(1)} %get-tuple-element.62.inner, ...), custom_call_target="tpu_custom_call" | custom-call | flops 905969664 | bytes 5885952 | tf_op jit(solution)/shard_map/pallas_call | solution.py:35
  23.7 0.6 collective-permute-start.4
  24.2 0.1 collective-permute-done.5.got
  24.4 0.1 shard_map.83
  24.5 1.5 %collective-permute-start.6 = (bf16[16,3456]{1,0:T(8,128)(2,1)S(1)}, bf16[16,3456]{1,0:T(8,128)(2,1)S(1)}, u32[]{:S(2)}, u32[]{:S(2)}) collective-permute-start(bf16[16,3456]{1,0:T(8,128)(2,1)S(1)} %get-tuple-element.70), channel_id=1, source_target_pairs={{0,3},{1,2},{2,1},{3,0},{4,7},{5,6},{6,5},{7,4},{8,11},{9,10},{10,... | collective-permute-start | bytes 331784 | tf_op jit(solution)/shard_map/ppermute | solution.py:401
  26.0 1.0 %collective-permute-start.7 = (bf16[16,3456]{1,0:T(8,128)(2,1)S(1)}, bf16[16,3456]{1,0:T(8,128)(2,1)S(1)}, u32[]{:S(2)}, u32[]{:S(2)}) collective-permute-start(bf16[16,3456]{1,0:T(8,128)(2,1)S(1)} %get-tuple-element.71), channel_id=1, source_target_pairs={{0,1},{1,0},{2,3},{3,2},{4,5},{5,4},{6,7},{7,6},{8,9},{9,8},{10,11... | collective-permute-start | bytes 331784 | tf_op jit(solution)/shard_map/ppermute | solution.py:401
  27.0 1.1 %collective-permute-start.8 = (bf16[16,3456]{1,0:T(8,128)(2,1)S(1)}, bf16[16,3456]{1,0:T(8,128)(2,1)S(1)}, u32[]{:S(2)}, u32[]{:S(2)}) collective-permute-start(bf16[16,3456]{1,0:T(8,128)(2,1)S(1)} %get-tuple-element.72), channel_id=1, source_target_pairs={{0,2},{1,3},{2,0},{3,1},{4,6},{5,7},{6,4},{7,5},{8,10},{9,11},{10,... | collective-permute-start | bytes 331784 | tf_op jit(solution)/shard_map/ppermute | solution.py:401
  28.0 0.0 collective-permute-done.4.got
  28.0 0.1 shard_map.82
  28.1 2.5 %collective-permute-start.10 = (bf16[16,3456]{1,0:T(8,128)(2,1)S(1)}, bf16[16,3456]{1,0:T(8,128)(2,1)S(1)}, u32[]{:S(2)}, u32[]{:S(2)}) collective-permute-start(bf16[16,3456]{1,0:T(8,128)(2,1)S(1)} %get-tuple-element.75), channel_id=1, source_target_pairs={{0,5},{1,4},{2,7},{3,6},{4,1},{5,0},{6,3},{7,2},{8,13},{9,12},{10,... | collective-permute-start | bytes 331784 | tf_op jit(solution)/shard_map/ppermute | solution.py:401
  30.6 0.0 collective-permute-start.11
  30.6 0.7 %collective-permute-done.6.refs_1_ = bf16[16,3456]{1,0:T(8,128)(2,1)S(1)} collective-permute-done((bf16[16,3456]{1,0:T(8,128)(2,1)S(1)}, bf16[16,3456]{1,0:T(8,128)(2,1)S(1)}, u32[]{:S(2)}, u32[]{:S(2)}) %collective-permute-start.6) | collective-permute-done | bytes 110624 | tf_op jit(solution)/shard_map/ppermute | solution.py:401
  31.3 1.0 %collective-permute-start.9 = (bf16[16,3456]{1,0:T(8,128)(2,1)S(1)}, bf16[16,3456]{1,0:T(8,128)(2,1)S(1)}, u32[]{:S(2)}, u32[]{:S(2)}) collective-permute-start(bf16[16,3456]{1,0:T(8,128)(2,1)S(1)} %get-tuple-element.74), channel_id=1, source_target_pairs={{0,1},{1,0},{2,3},{3,2},{4,5},{5,4},{6,7},{7,6},{8,9},{9,8},{10,11... | collective-permute-start | bytes 331784 | tf_op jit(solution)/shard_map/ppermute | solution.py:401
  32.3 0.1 collective-permute-done.7.refs_2_
  32.4 1.0 %collective-permute-done.8.refs_3_ = bf16[16,3456]{1,0:T(8,128)(2,1)S(1)} collective-permute-done((bf16[16,3456]{1,0:T(8,128)(2,1)S(1)}, bf16[16,3456]{1,0:T(8,128)(2,1)S(1)}, u32[]{:S(2)}, u32[]{:S(2)}) %collective-permute-start.8) | collective-permute-done | bytes 110624 | tf_op jit(solution)/shard_map/ppermute | solution.py:401
  33.4 0.1 shard_map.84.one
  33.4 2.1 %collective-permute-start.12 = (bf16[16,3456]{1,0:T(8,128)(2,1)S(1)}, bf16[16,3456]{1,0:T(8,128)(2,1)S(1)}, u32[]{:S(2)}, u32[]{:S(2)}) collective-permute-start(bf16[16,3456]{1,0:T(8,128)(2,1)S(1)} %shard_map.84.one), channel_id=1, source_target_pairs={{0,4},{1,5},{2,6},{3,7},{4,0},{5,1},{6,2},{7,3},{8,12},{9,13},{10,... | collective-permute-start | bytes 331784 | tf_op jit(solution)/shard_map/ppermute | solution.py:401
  35.5 0.0 collective-permute-done.10.refs_2_
  35.5 0.3 collective-permute-done.11.refs_3_
  35.8 0.2 collective-permute-done.9.refs_1_
  36.1 0.1 shard_map.85.one
  36.1 1.0 %collective-permute-start.13 = (bf16[16,3456]{1,0:T(8,128)(2,1)S(1)}, bf16[16,3456]{1,0:T(8,128)(2,1)S(1)}, u32[]{:S(2)}, u32[]{:S(2)}) collective-permute-start(bf16[16,3456]{1,0:T(8,128)(2,1)S(1)} %shard_map.85.one), channel_id=1, source_target_pairs={{0,2},{1,3},{2,0},{3,1},{4,6},{5,7},{6,4},{7,5},{8,10},{9,11},{10,... | collective-permute-start | bytes 331784 | tf_op jit(solution)/shard_map/ppermute | solution.py:401
  37.2 1.4 %collective-permute-done.12.two = bf16[16,3456]{1,0:T(8,128)(2,1)S(1)} collective-permute-done((bf16[16,3456]{1,0:T(8,128)(2,1)S(1)}, bf16[16,3456]{1,0:T(8,128)(2,1)S(1)}, u32[]{:S(2)}, u32[]{:S(2)}) %collective-permute-start.12) | collective-permute-done | bytes 110624 | tf_op jit(solution)/shard_map/ppermute | solution.py:401
  38.6 2.1 %collective-permute-start.14 = (bf16[16,3456]{1,0:T(8,128)(2,1)S(1)}, bf16[16,3456]{1,0:T(8,128)(2,1)S(1)}, u32[]{:S(2)}, u32[]{:S(2)}) collective-permute-start(bf16[16,3456]{1,0:T(8,128)(2,1)S(1)} %shard_map.86.one), channel_id=1, source_target_pairs={{0,8},{1,9},{2,10},{3,11},{4,12},{5,13},{6,14},{7,15},{8,0},{9,1},... | collective-permute-start | bytes 331784 | tf_op jit(solution)/shard_map/ppermute | solution.py:401
  40.6 1.5 %shard_map.87 = bf16[512,128]{1,0:T(8,128)(2,1)} custom-call(bf16[512,1152]{1,0:T(8,128)(2,1)S(1)} %get-tuple-element.79.st_own, bf16[512,128]{1,0:T(8,128)(2,1)S(1)} %get-tuple-element.47.grads, bf16[48,128]{1,0:T(8,128)(2,1)S(1)} %get-tuple-element.56.marks3, bf16[384,1152]{1,0:T(8,128)(2,1)S(1)} %get-tuple-element.80.w1_wide), custom_call_target="tpu_custom_call" | custom-call | flops 452984832 | bytes 2338816 | tf_op jit(solution)/shard_map/pallas_call | solution.py:35
  42.1 0.0 collective-permute-done.13.two
  42.1 1.0 %collective-permute-start.15 = (bf16[16,3456]{1,0:T(8,128)(2,1)S(1)}, bf16[16,3456]{1,0:T(8,128)(2,1)S(1)}, u32[]{:S(2)}, u32[]{:S(2)}) collective-permute-start(bf16[16,3456]{1,0:T(8,128)(2,1)S(1)} %shard_map.88.one), channel_id=1, source_target_pairs={{0,8},{1,9},{2,10},{3,11},{4,12},{5,13},{6,14},{7,15},{8,0},{9,1},... | collective-permute-start | bytes 331784 | tf_op jit(solution)/shard_map/ppermute | solution.py:401
  43.1 1.1 %collective-permute-done.14.two = bf16[16,3456]{1,0:T(8,128)(2,1)S(1)} collective-permute-done((bf16[16,3456]{1,0:T(8,128)(2,1)S(1)}, bf16[16,3456]{1,0:T(8,128)(2,1)S(1)}, u32[]{:S(2)}, u32[]{:S(2)}) %collective-permute-start.14) | collective-permute-done | bytes 110624 | tf_op jit(solution)/shard_map/ppermute | solution.py:401
  44.3 1.5 %collective-permute-start.20 = (bf16[432,128]{1,0:T(8,128)(2,1)S(1)}, bf16[432,128]{1,0:T(8,128)(2,1)S(1)}, u32[]{:S(2)}, u32[]{:S(2)}) collective-permute-start(bf16[432,128]{1,0:T(8,128)(2,1)S(1)} %shard_map.89.refs_0_), channel_id=1, source_target_pairs={{0,3},{1,2},{2,1},{3,0},{4,7},{5,6},{6,5},{7,4},{8,11},{9,10},{10,... | collective-permute-start | bytes 331784 | tf_op jit(solution)/shard_map/ppermute | solution.py:401
  45.8 1.0 %collective-permute-start.21 = (bf16[432,128]{1,0:T(8,128)(2,1)S(1)}, bf16[432,128]{1,0:T(8,128)(2,1)S(1)}, u32[]{:S(2)}, u32[]{:S(2)}) collective-permute-start(bf16[432,128]{1,0:T(8,128)(2,1)S(1)} %shard_map.89.refs_0_), channel_id=1, source_target_pairs={{0,1},{1,0},{2,3},{3,2},{4,5},{5,4},{6,7},{7,6},{8,9},{9,8},{10,11... | collective-permute-start | bytes 331784 | tf_op jit(solution)/shard_map/ppermute | solution.py:401
  46.8 1.1 %collective-permute-start.22 = (bf16[432,128]{1,0:T(8,128)(2,1)S(1)}, bf16[432,128]{1,0:T(8,128)(2,1)S(1)}, u32[]{:S(2)}, u32[]{:S(2)}) collective-permute-start(bf16[432,128]{1,0:T(8,128)(2,1)S(1)} %shard_map.89.refs_0_), channel_id=1, source_target_pairs={{0,2},{1,3},{2,0},{3,1},{4,6},{5,7},{6,4},{7,5},{8,10},{9,11},{10,... | collective-permute-start | bytes 331784 | tf_op jit(solution)/shard_map/ppermute | solution.py:401
  47.9 1.3 %collective-permute-done.15.two = bf16[16,3456]{1,0:T(8,128)(2,1)S(1)} collective-permute-done((bf16[16,3456]{1,0:T(8,128)(2,1)S(1)}, bf16[16,3456]{1,0:T(8,128)(2,1)S(1)}, u32[]{:S(2)}, u32[]{:S(2)}) %collective-permute-start.15) | collective-permute-done | bytes 110624 | tf_op jit(solution)/shard_map/ppermute | solution.py:401
  49.2 1.2 %collective-permute-start.16 = (bf16[432,128]{1,0:T(8,128)(2,1)S(1)}, bf16[432,128]{1,0:T(8,128)(2,1)S(1)}, u32[]{:S(2)}, u32[]{:S(2)}) collective-permute-start(bf16[432,128]{1,0:T(8,128)(2,1)S(1)} %shard_map.90.refs_0_), channel_id=1, source_target_pairs={{0,5},{1,4},{2,7},{3,6},{4,1},{5,0},{6,3},{7,2},{8,13},{9,12},{10,... | collective-permute-start | bytes 331784 | tf_op jit(solution)/shard_map/ppermute | solution.py:401
  50.3 1.4 %collective-permute-start.17 = (bf16[432,128]{1,0:T(8,128)(2,1)S(1)}, bf16[432,128]{1,0:T(8,128)(2,1)S(1)}, u32[]{:S(2)}, u32[]{:S(2)}) collective-permute-start(bf16[432,128]{1,0:T(8,128)(2,1)S(1)} %shard_map.90.refs_0_), channel_id=1, source_target_pairs={{0,4},{1,5},{2,6},{3,7},{4,0},{5,1},{6,2},{7,3},{8,12},{9,13},{10,... | collective-permute-start | bytes 331784 | tf_op jit(solution)/shard_map/ppermute | solution.py:401
  51.7 0.0 collective-permute-done.20.refs_1_
  51.7 1.0 %collective-permute-start.18 = (bf16[432,128]{1,0:T(8,128)(2,1)S(1)}, bf16[432,128]{1,0:T(8,128)(2,1)S(1)}, u32[]{:S(2)}, u32[]{:S(2)}) collective-permute-start(bf16[432,128]{1,0:T(8,128)(2,1)S(1)} %shard_map.90.refs_0_), channel_id=1, source_target_pairs={{0,1},{1,0},{2,3},{3,2},{4,5},{5,4},{6,7},{7,6},{8,9},{9,8},{10,11... | collective-permute-start | bytes 331784 | tf_op jit(solution)/shard_map/ppermute | solution.py:401
  52.8 0.0 collective-permute-done.21.refs_2_
  52.8 0.2 collective-permute-done.22.refs_3_
  53.0 0.1 collective-permute-start.23
  53.1 1.8 %collective-permute-done.16.refs_1_ = bf16[432,128]{1,0:T(8,128)(2,1)S(1)} collective-permute-done((bf16[432,128]{1,0:T(8,128)(2,1)S(1)}, bf16[432,128]{1,0:T(8,128)(2,1)S(1)}, u32[]{:S(2)}, u32[]{:S(2)}) %collective-permute-start.16) | collective-permute-done | bytes 110624 | tf_op jit(solution)/shard_map/ppermute | solution.py:401
  54.9 0.7 %collective-permute-done.17.refs_2_ = bf16[432,128]{1,0:T(8,128)(2,1)S(1)} collective-permute-done((bf16[432,128]{1,0:T(8,128)(2,1)S(1)}, bf16[432,128]{1,0:T(8,128)(2,1)S(1)}, u32[]{:S(2)}, u32[]{:S(2)}) %collective-permute-start.17) | collective-permute-done | bytes 110624 | tf_op jit(solution)/shard_map/ppermute | solution.py:401
  55.6 0.8 %collective-permute-done.18.refs_3_ = bf16[432,128]{1,0:T(8,128)(2,1)S(1)} collective-permute-done((bf16[432,128]{1,0:T(8,128)(2,1)S(1)}, bf16[432,128]{1,0:T(8,128)(2,1)S(1)}, u32[]{:S(2)}, u32[]{:S(2)}) %collective-permute-start.18) | collective-permute-done | bytes 110624 | tf_op jit(solution)/shard_map/ppermute | solution.py:401
  56.5 0.1 shard_map.91.own
  56.5 0.1 collective-permute-start.19
  56.6 0.0 collective-permute-done.23.other
  56.6 1.3 %shard_map.94 = f32[3456,128]{1,0:T(8,128)} custom-call(bf16[1728,128]{1,0:T(8,128)(2,1)S(1)} %shard_map.93.own, bf16[1728,128]{1,0:T(8,128)(2,1)S(1)} %collective-permute-done.23.other), custom_call_target="tpu_custom_call" | custom-call | bytes 2654208 | tf_op jit(solution)/shard_map/pallas_call | solution.py:35
  58.0 0.4 collective-permute-done.19.other
  58.4 1.3 %shard_map.92 = f32[3456,128]{1,0:T(8,128)} custom-call(bf16[1728,128]{1,0:T(8,128)(2,1)S(1)} %shard_map.91.own, bf16[1728,128]{1,0:T(8,128)(2,1)S(1)} %collective-permute-done.19.other), custom_call_target="tpu_custom_call" | custom-call | bytes 2654208 | tf_op jit(solution)/shard_map/pallas_call | solution.py:35
  (5 shorter events, 0.2 us)
Async XLA Ops:
  2.4 8.6 %collective-permute-start = (bf16[272,128]{1,0:T(8,128)(2,1)S(1)}, bf16[272,128]{1,0:T(8,128)(2,1)S(1)}, u32[]{:S(2)}, u32[]{:S(2)}) collective-permute-start(bf16[272,128]{1,0:T(8,128)(2,1)S(1)} %get-tuple-element.49), channel_id=1, source_target_pairs={{1,2},{2,1},{5,6},{6,5},{9,10},{10,9},{13,14},{14,13},{17,18},{18,... | collective-permute-start | bytes 208904 | tf_op jit(solution)/shard_map/ppermute | solution.py:634
  3.1 9.0 %collective-permute-start.1 = (bf16[272,128]{1,0:T(8,128)(2,1)S(1)}, bf16[272,128]{1,0:T(8,128)(2,1)S(1)}, u32[]{:S(2)}, u32[]{:S(2)}) collective-permute-start(bf16[272,128]{1,0:T(8,128)(2,1)S(1)} %get-tuple-element.50), channel_id=1, source_target_pairs={{0,1},{1,0},{2,3},{3,2},{4,5},{5,4},{6,7},{7,6},{8,9},{9,8},{10,11... | collective-permute-start | bytes 208904 | tf_op jit(solution)/shard_map/ppermute | solution.py:634
  12.2 7.2 %collective-permute-start.2 = (bf16[400,128]{1,0:T(8,128)(2,1)S(1)}, bf16[400,128]{1,0:T(8,128)(2,1)S(1)}, u32[]{:S(2)}, u32[]{:S(2)}) collective-permute-start(bf16[400,128]{1,0:T(8,128)(2,1)S(1)} %get-tuple-element.57), channel_id=1, source_target_pairs={{4,8},{8,4},{5,9},{9,5},{6,10},{10,6},{7,11},{11,7},{20,24},{24,20... | collective-permute-start | bytes 307208 | tf_op jit(solution)/shard_map/ppermute | solution.py:634
  12.9 7.1 %collective-permute-start.3 = (bf16[400,128]{1,0:T(8,128)(2,1)S(1)}, bf16[400,128]{1,0:T(8,128)(2,1)S(1)}, u32[]{:S(2)}, u32[]{:S(2)}) collective-permute-start(bf16[400,128]{1,0:T(8,128)(2,1)S(1)} %get-tuple-element.58), channel_id=1, source_target_pairs={{0,4},{4,0},{1,5},{5,1},{2,6},{6,2},{3,7},{7,3},{8,12},{12,8},{9,1... | collective-permute-start | bytes 307208 | tf_op jit(solution)/shard_map/ppermute | solution.py:634
  21.9 2.5 %collective-permute-start.5 = (f32[64,3456]{1,0:T(8,128)S(1)}, f32[64,3456]{1,0:T(8,128)S(1)}, u32[]{:S(2)}, u32[]{:S(2)}) collective-permute-start(f32[64,3456]{1,0:T(8,128)S(1)} %get-tuple-element.67), channel_id=1, source_target_pairs={{0,16},{16,0},{1,17},{17,1},{2,18},{18,2},{3,19},{19,3},{4,20},{20... | collective-permute-start | bytes 2654216 | tf_op jit(solution)/shard_map/ppermute | solution.py:391
  23.7 4.3 %collective-permute-start.4 = (f32[64,3456]{1,0:T(8,128)S(1)}, f32[64,3456]{1,0:T(8,128)S(1)}, u32[]{:S(2)}, u32[]{:S(2)}) collective-permute-start(f32[64,3456]{1,0:T(8,128)S(1)} %get-tuple-element.64), channel_id=1, source_target_pairs={{0,16},{16,0},{1,17},{17,1},{2,18},{18,2},{3,19},{19,3},{4,20},{20... | collective-permute-start | bytes 2654216 | tf_op jit(solution)/shard_map/ppermute | solution.py:391
  24.5 6.9 %collective-permute-start.6 = (bf16[16,3456]{1,0:T(8,128)(2,1)S(1)}, bf16[16,3456]{1,0:T(8,128)(2,1)S(1)}, u32[]{:S(2)}, u32[]{:S(2)}) collective-permute-start(bf16[16,3456]{1,0:T(8,128)(2,1)S(1)} %get-tuple-element.70), channel_id=1, source_target_pairs={{0,3},{1,2},{2,1},{3,0},{4,7},{5,6},{6,5},{7,4},{8,11},{9,10},{10,... | collective-permute-start | bytes 331784 | tf_op jit(solution)/shard_map/ppermute | solution.py:401
  26.0 6.4 %collective-permute-start.7 = (bf16[16,3456]{1,0:T(8,128)(2,1)S(1)}, bf16[16,3456]{1,0:T(8,128)(2,1)S(1)}, u32[]{:S(2)}, u32[]{:S(2)}) collective-permute-start(bf16[16,3456]{1,0:T(8,128)(2,1)S(1)} %get-tuple-element.71), channel_id=1, source_target_pairs={{0,1},{1,0},{2,3},{3,2},{4,5},{5,4},{6,7},{7,6},{8,9},{9,8},{10,11... | collective-permute-start | bytes 331784 | tf_op jit(solution)/shard_map/ppermute | solution.py:401
  27.0 6.4 %collective-permute-start.8 = (bf16[16,3456]{1,0:T(8,128)(2,1)S(1)}, bf16[16,3456]{1,0:T(8,128)(2,1)S(1)}, u32[]{:S(2)}, u32[]{:S(2)}) collective-permute-start(bf16[16,3456]{1,0:T(8,128)(2,1)S(1)} %get-tuple-element.72), channel_id=1, source_target_pairs={{0,2},{1,3},{2,0},{3,1},{4,6},{5,7},{6,4},{7,5},{8,10},{9,11},{10,... | collective-permute-start | bytes 331784 | tf_op jit(solution)/shard_map/ppermute | solution.py:401
  28.1 7.4 %collective-permute-start.10 = (bf16[16,3456]{1,0:T(8,128)(2,1)S(1)}, bf16[16,3456]{1,0:T(8,128)(2,1)S(1)}, u32[]{:S(2)}, u32[]{:S(2)}) collective-permute-start(bf16[16,3456]{1,0:T(8,128)(2,1)S(1)} %get-tuple-element.75), channel_id=1, source_target_pairs={{0,5},{1,4},{2,7},{3,6},{4,1},{5,0},{6,3},{7,2},{8,13},{9,12},{10,... | collective-permute-start | bytes 331784 | tf_op jit(solution)/shard_map/ppermute | solution.py:401
  30.6 5.2 %collective-permute-start.11 = (bf16[16,3456]{1,0:T(8,128)(2,1)S(1)}, bf16[16,3456]{1,0:T(8,128)(2,1)S(1)}, u32[]{:S(2)}, u32[]{:S(2)}) collective-permute-start(bf16[16,3456]{1,0:T(8,128)(2,1)S(1)} %get-tuple-element.76), channel_id=1, source_target_pairs={{0,4},{1,5},{2,6},{3,7},{4,0},{5,1},{6,2},{7,3},{8,12},{9,13},{10,... | collective-permute-start | bytes 331784 | tf_op jit(solution)/shard_map/ppermute | solution.py:401
  31.3 4.7 %collective-permute-start.9 = (bf16[16,3456]{1,0:T(8,128)(2,1)S(1)}, bf16[16,3456]{1,0:T(8,128)(2,1)S(1)}, u32[]{:S(2)}, u32[]{:S(2)}) collective-permute-start(bf16[16,3456]{1,0:T(8,128)(2,1)S(1)} %get-tuple-element.74), channel_id=1, source_target_pairs={{0,1},{1,0},{2,3},{3,2},{4,5},{5,4},{6,7},{7,6},{8,9},{9,8},{10,11... | collective-permute-start | bytes 331784 | tf_op jit(solution)/shard_map/ppermute | solution.py:401
  33.4 5.1 %collective-permute-start.12 = (bf16[16,3456]{1,0:T(8,128)(2,1)S(1)}, bf16[16,3456]{1,0:T(8,128)(2,1)S(1)}, u32[]{:S(2)}, u32[]{:S(2)}) collective-permute-start(bf16[16,3456]{1,0:T(8,128)(2,1)S(1)} %shard_map.84.one), channel_id=1, source_target_pairs={{0,4},{1,5},{2,6},{3,7},{4,0},{5,1},{6,2},{7,3},{8,12},{9,13},{10,... | collective-permute-start | bytes 331784 | tf_op jit(solution)/shard_map/ppermute | solution.py:401
  36.1 6.0 %collective-permute-start.13 = (bf16[16,3456]{1,0:T(8,128)(2,1)S(1)}, bf16[16,3456]{1,0:T(8,128)(2,1)S(1)}, u32[]{:S(2)}, u32[]{:S(2)}) collective-permute-start(bf16[16,3456]{1,0:T(8,128)(2,1)S(1)} %shard_map.85.one), channel_id=1, source_target_pairs={{0,2},{1,3},{2,0},{3,1},{4,6},{5,7},{6,4},{7,5},{8,10},{9,11},{10,... | collective-permute-start | bytes 331784 | tf_op jit(solution)/shard_map/ppermute | solution.py:401
  38.6 5.7 %collective-permute-start.14 = (bf16[16,3456]{1,0:T(8,128)(2,1)S(1)}, bf16[16,3456]{1,0:T(8,128)(2,1)S(1)}, u32[]{:S(2)}, u32[]{:S(2)}) collective-permute-start(bf16[16,3456]{1,0:T(8,128)(2,1)S(1)} %shard_map.86.one), channel_id=1, source_target_pairs={{0,8},{1,9},{2,10},{3,11},{4,12},{5,13},{6,14},{7,15},{8,0},{9,1},... | collective-permute-start | bytes 331784 | tf_op jit(solution)/shard_map/ppermute | solution.py:401
  42.1 7.0 %collective-permute-start.15 = (bf16[16,3456]{1,0:T(8,128)(2,1)S(1)}, bf16[16,3456]{1,0:T(8,128)(2,1)S(1)}, u32[]{:S(2)}, u32[]{:S(2)}) collective-permute-start(bf16[16,3456]{1,0:T(8,128)(2,1)S(1)} %shard_map.88.one), channel_id=1, source_target_pairs={{0,8},{1,9},{2,10},{3,11},{4,12},{5,13},{6,14},{7,15},{8,0},{9,1},... | collective-permute-start | bytes 331784 | tf_op jit(solution)/shard_map/ppermute | solution.py:401
  44.3 7.4 %collective-permute-start.20 = (bf16[432,128]{1,0:T(8,128)(2,1)S(1)}, bf16[432,128]{1,0:T(8,128)(2,1)S(1)}, u32[]{:S(2)}, u32[]{:S(2)}) collective-permute-start(bf16[432,128]{1,0:T(8,128)(2,1)S(1)} %shard_map.89.refs_0_), channel_id=1, source_target_pairs={{0,3},{1,2},{2,1},{3,0},{4,7},{5,6},{6,5},{7,4},{8,11},{9,10},{10,... | collective-permute-start | bytes 331784 | tf_op jit(solution)/shard_map/ppermute | solution.py:401
  45.8 7.0 %collective-permute-start.21 = (bf16[432,128]{1,0:T(8,128)(2,1)S(1)}, bf16[432,128]{1,0:T(8,128)(2,1)S(1)}, u32[]{:S(2)}, u32[]{:S(2)}) collective-permute-start(bf16[432,128]{1,0:T(8,128)(2,1)S(1)} %shard_map.89.refs_0_), channel_id=1, source_target_pairs={{0,1},{1,0},{2,3},{3,2},{4,5},{5,4},{6,7},{7,6},{8,9},{9,8},{10,11... | collective-permute-start | bytes 331784 | tf_op jit(solution)/shard_map/ppermute | solution.py:401
  46.8 6.2 %collective-permute-start.22 = (bf16[432,128]{1,0:T(8,128)(2,1)S(1)}, bf16[432,128]{1,0:T(8,128)(2,1)S(1)}, u32[]{:S(2)}, u32[]{:S(2)}) collective-permute-start(bf16[432,128]{1,0:T(8,128)(2,1)S(1)} %shard_map.89.refs_0_), channel_id=1, source_target_pairs={{0,2},{1,3},{2,0},{3,1},{4,6},{5,7},{6,4},{7,5},{8,10},{9,11},{10,... | collective-permute-start | bytes 331784 | tf_op jit(solution)/shard_map/ppermute | solution.py:401
  49.2 5.7 %collective-permute-start.16 = (bf16[432,128]{1,0:T(8,128)(2,1)S(1)}, bf16[432,128]{1,0:T(8,128)(2,1)S(1)}, u32[]{:S(2)}, u32[]{:S(2)}) collective-permute-start(bf16[432,128]{1,0:T(8,128)(2,1)S(1)} %shard_map.90.refs_0_), channel_id=1, source_target_pairs={{0,5},{1,4},{2,7},{3,6},{4,1},{5,0},{6,3},{7,2},{8,13},{9,12},{10,... | collective-permute-start | bytes 331784 | tf_op jit(solution)/shard_map/ppermute | solution.py:401
  50.3 5.3 %collective-permute-start.17 = (bf16[432,128]{1,0:T(8,128)(2,1)S(1)}, bf16[432,128]{1,0:T(8,128)(2,1)S(1)}, u32[]{:S(2)}, u32[]{:S(2)}) collective-permute-start(bf16[432,128]{1,0:T(8,128)(2,1)S(1)} %shard_map.90.refs_0_), channel_id=1, source_target_pairs={{0,4},{1,5},{2,6},{3,7},{4,0},{5,1},{6,2},{7,3},{8,12},{9,13},{10,... | collective-permute-start | bytes 331784 | tf_op jit(solution)/shard_map/ppermute | solution.py:401
  51.7 4.7 %collective-permute-start.18 = (bf16[432,128]{1,0:T(8,128)(2,1)S(1)}, bf16[432,128]{1,0:T(8,128)(2,1)S(1)}, u32[]{:S(2)}, u32[]{:S(2)}) collective-permute-start(bf16[432,128]{1,0:T(8,128)(2,1)S(1)} %shard_map.90.refs_0_), channel_id=1, source_target_pairs={{0,1},{1,0},{2,3},{3,2},{4,5},{5,4},{6,7},{7,6},{8,9},{9,8},{10,11... | collective-permute-start | bytes 331784 | tf_op jit(solution)/shard_map/ppermute | solution.py:401
  53.0 3.6 %collective-permute-start.23 = (bf16[1728,128]{1,0:T(8,128)(2,1)S(1)}, bf16[1728,128]{1,0:T(8,128)(2,1)S(1)}, u32[]{:S(2)}, u32[]{:S(2)}) collective-permute-start(bf16[1728,128]{1,0:T(8,128)(2,1)S(1)} %shard_map.93.own), channel_id=1, source_target_pairs={{0,16},{16,0},{1,17},{17,1},{2,18},{18,2},{3,19},{19,3},{4,20},{20... | collective-permute-start | bytes 1327112 | tf_op jit(solution)/shard_map/ppermute | solution.py:391
  56.5 1.9 %collective-permute-start.19 = (bf16[1728,128]{1,0:T(8,128)(2,1)S(1)}, bf16[1728,128]{1,0:T(8,128)(2,1)S(1)}, u32[]{:S(2)}, u32[]{:S(2)}) collective-permute-start(bf16[1728,128]{1,0:T(8,128)(2,1)S(1)} %shard_map.91.own), channel_id=1, source_target_pairs={{0,16},{16,0},{1,17},{17,1},{2,18},{18,2},{3,19},{19,3},{4,20},{20... | collective-permute-start | bytes 1327112 | tf_op jit(solution)/shard_map/ppermute | solution.py:391

commit v6 on v5

--- a/solution.py
+++ b/solution.py
@@ -581,9 +581,8 @@
         got_one, got_two = cross(one, bits_one), cross(two, bits_two)
         one = add(after(one, two), got_one)
         if other is None:
-            other = beside(one)
-            two = after(two, other)
-        two = add(after(two, one), got_two)
+            other = beside(two)
+        two = add(two, got_two)
     return one, two, other
 
 
@@ -718,7 +717,6 @@
     own_b, *send_b = split_stage(groups[1], kept_b, swap(sent_b, "dp", 1))
     gots_a = near(groups[0], send_a, groups[0][2])
     gots_b = near(groups[1], send_b, groups[1][2])
-    own_a = after(own_a, own_b)
 
     def last_part(cue):
         return call(

time: 59.9 us -> 59.7 us (level)
  waiting for transfers between devices: 11.9 us -> 10.7 us
  starting transfers between devices: 32.7 us -> 33.7 us
    ppermute x16, starting transfers between devices: 20.4 us -> 21.4 us  [cross(): return lax.ppermute(value, ('dp', 'blk'), pairs)]
    ppermute x16, waiting for transfers between devices: 9.63 us -> 8.85 us  [cross(): return lax.ppermute(value, ('dp', 'blk'), pairs)]
  transfers between devices with their start and end apart: 24 -> 24, of which waited for: 16 -> 15; matrix products, arithmetic and copies ran while one was open for 3% -> 3% of each run, Pallas kernels for 13% -> 13%
where the time goes in v6:
time: 59.7 us; the launch traced here: 59.5 us
  starting transfers between devices  33.7 us (56%)
  Pallas kernels  11.1 us (19%)
  waiting for transfers between devices  10.7 us (18%)
  other arithmetic  2.59 us (4%)
  between operations  1.44 us (2%)
    ppermute x16, starting transfers between devices, cross(): return lax.ppermute(value, ('dp', 'blk'), pairs)  21.4 us
    pallas_call x19, Pallas kernels, call(): pl.pallas_call(body, out_shape=list(outs), in_specs=specs, out_specs=[VM]...  11.1 us
    ppermute x2, starting transfers between devices, beside(): lax.ppermute(one, 'blk', pairs[0])  10.2 us
    ppermute x16, waiting for transfers between devices, cross(): return lax.ppermute(value, ('dp', 'blk'), pairs)  8.85 us
    ppermute x2, waiting for transfers between devices, beside(): lax.ppermute(one, 'blk', pairs[0])  1.66 us
    another operation x1, other arithmetic, on_device(): jnp.stack([w_first, w_second])  1.6 us
    ppermute x2, starting transfers between devices, beside(): lax.ppermute(two, 'blk', pairs[1])  1.33 us
  transfers between devices with their start and end apart: 24, of which 15 were waited for; matrix products, arithmetic and copies ran while one was open for 3% of the time, Pallas kernels for 13%

profile of v6, /device:TPU:0, one launch (start us, length us, event | category | flops | bytes accessed | tf_op | source)
XLA Modules:
  0.0 59.5 jit_solution(7430665043805143512)
XLA Ops:
  1.3 1.0 %pad_maximum_fusion.1.both = bf16[2,512,128]{2,1,0:T(8,128)(2,1)S(1)} fusion(bf16[1,512,128]{2,1,0:T(8,128)(2,1)} %param.9, bf16[1,512,128]{2,1,0:T(8,128)(2,1)} %param.5), kind=kLoop, calls=%fused_computation.1 | loop fusion | flops 131072 | bytes 524288 | tf_op jit(solution)/shard_map/stack | solution.py:644
  2.3 0.1 shard_map.76
  2.4 0.7 %collective-permute-start = (bf16[272,128]{1,0:T(8,128)(2,1)S(1)}, bf16[272,128]{1,0:T(8,128)(2,1)S(1)}, u32[]{:S(2)}, u32[]{:S(2)}) collective-permute-start(bf16[272,128]{1,0:T(8,128)(2,1)S(1)} %get-tuple-element.45), channel_id=1, source_target_pairs={{1,2},{2,1},{5,6},{6,5},{9,10},{10,9},{13,14},{14,13},{17,18},{18,... | collective-permute-start | bytes 208904 | tf_op jit(solution)/shard_map/ppermute | solution.py:633
  3.1 5.7 %collective-permute-start.1 = (bf16[272,128]{1,0:T(8,128)(2,1)S(1)}, bf16[272,128]{1,0:T(8,128)(2,1)S(1)}, u32[]{:S(2)}, u32[]{:S(2)}) collective-permute-start(bf16[272,128]{1,0:T(8,128)(2,1)S(1)} %get-tuple-element.46), channel_id=1, source_target_pairs={{0,1},{1,0},{2,3},{3,2},{4,5},{5,4},{6,7},{7,6},{8,9},{9,8},{10,11... | collective-permute-start | bytes 208904 | tf_op jit(solution)/shard_map/ppermute | solution.py:633
  8.8 1.6 %pad_maximum_fusion.src = bf16[2,3456,128]{2,1,0:T(8,128)(2,1)S(1)} fusion(bf16[1,3456,128]{2,1,0:T(8,128)(2,1)} %bitcast.3, bf16[1,3456,128]{2,1,0:T(8,128)(2,1)} %bitcast.4), kind=kLoop, calls=%fused_computation | loop fusion | flops 884736 | bytes 3538944 | tf_op jit(solution)/shard_map/stack | solution.py:655
  10.4 0.6 %shard_map.77 = (bf16[384,1152]{1,0:T(8,128)(2,1)S(1)}, bf16[1152,384]{1,0:T(8,128)(2,1)S(1)}, bf16[384,1152]{1,0:T(8,128)(2,1)S(1)}) custom-call(bf16[2,3456,128]{2,1,0:T(8,128)(2,1)S(1)} %pad_maximum_fusion.src), custom_call_target="tpu_custom_call" | custom-call | bytes 4423680 | tf_op jit(solution)/shard_map/pallas_call | solution.py:35
  11.0 0.0 collective-permute-done.z_odd
  11.0 1.1 %collective-permute-done.1.z_even = bf16[272,128]{1,0:T(8,128)(2,1)S(1)} collective-permute-done((bf16[272,128]{1,0:T(8,128)(2,1)S(1)}, bf16[272,128]{1,0:T(8,128)(2,1)S(1)}, u32[]{:S(2)}, u32[]{:S(2)}) %collective-permute-start.1) | collective-permute-done | bytes 69664 | tf_op jit(solution)/shard_map/ppermute | solution.py:633
  12.1 0.1 shard_map.78
  12.2 0.7 %collective-permute-start.2 = (bf16[400,128]{1,0:T(8,128)(2,1)S(1)}, bf16[400,128]{1,0:T(8,128)(2,1)S(1)}, u32[]{:S(2)}, u32[]{:S(2)}) collective-permute-start(bf16[400,128]{1,0:T(8,128)(2,1)S(1)} %get-tuple-element.53), channel_id=1, source_target_pairs={{4,8},{8,4},{5,9},{9,5},{6,10},{10,6},{7,11},{11,7},{20,24},{24,20... | collective-permute-start | bytes 307208 | tf_op jit(solution)/shard_map/ppermute | solution.py:633
  12.9 4.5 %collective-permute-start.3 = (bf16[400,128]{1,0:T(8,128)(2,1)S(1)}, bf16[400,128]{1,0:T(8,128)(2,1)S(1)}, u32[]{:S(2)}, u32[]{:S(2)}) collective-permute-start(bf16[400,128]{1,0:T(8,128)(2,1)S(1)} %get-tuple-element.54), channel_id=1, source_target_pairs={{0,4},{4,0},{1,5},{5,1},{2,6},{6,2},{3,7},{7,3},{8,12},{12,8},{9,1... | collective-permute-start | bytes 307208 | tf_op jit(solution)/shard_map/ppermute | solution.py:633
  17.3 2.0 %shard_map.79 = (f32[640,128]{1,0:T(8,128)S(1)}, f32[640,128]{1,0:T(8,128)S(1)}, bf16[128,640]{1,0:T(8,128)(2,1)S(1)}) custom-call(f32[784,128]{1,0:T(8,128)S(1)} %get-tuple-element.47.deep_in, f32[784,128]{1,0:T(8,128)S(1)} %get-tuple-element.48.deep_g, bf16[512,128]{1,0:T(8,128)(2,1)S(1)} %get-tuple-element.42.inp, ...), custom_call_target="tpu_custom_call" | custom-call | flops 905969664 | bytes 3522560 | tf_op jit(solution)/shard_map/pallas_call | solution.py:35
  19.4 0.0 collective-permute-done.2.y_odd
  19.4 0.6 collective-permute-done.3.y_even
  20.0 1.9 %shard_map.80 = (f32[64,3456]{1,0:T(8,128)S(1)}, f32[64,3456]{1,0:T(8,128)S(1)}, f32[1024,128]{1,0:T(8,128)S(1)}, f32[1600,128]{1,0:T(8,128)S(1)}) custom-call(f32[784,128]{1,0:T(8,128)S(1)} %get-tuple-element.47.deep_in, f32[784,128]{1,0:T(8,128)S(1)} %get-tuple-element.48.deep_g, bf16[48,128]{1,0:T(8,128)(2,1)S(1)} %get-tuple-element.52.marks3, ...), custom_call_target="tpu_custom_call" | custom-call | flops 905969664 | bytes 5345280 | tf_op jit(solution)/shard_map/pallas_call | solution.py:35
  21.9 0.1 collective-permute-start.5
  22.0 1.7 %shard_map.81 = (f32[64,3456]{1,0:T(8,128)S(1)}, f32[64,3456]{1,0:T(8,128)S(1)}, bf16[512,1152]{1,0:T(8,128)(2,1)S(1)}) custom-call(f32[1600,128]{1,0:T(8,128)S(1)} %get-tuple-element.56.grid_g, f32[1024,128]{1,0:T(8,128)S(1)} %get-tuple-element.57.act, f32[640,128]{1,0:T(8,128)S(1)} %get-tuple-element.58.inner, ...), custom_call_target="tpu_custom_call" | custom-call | flops 905969664 | bytes 5885952 | tf_op jit(solution)/shard_map/pallas_call | solution.py:35
  23.7 0.6 collective-permute-start.4
  24.2 0.1 collective-permute-done.5.got
  24.4 0.1 shard_map.83
  24.5 1.5 %collective-permute-start.6 = (bf16[16,3456]{1,0:T(8,128)(2,1)S(1)}, bf16[16,3456]{1,0:T(8,128)(2,1)S(1)}, u32[]{:S(2)}, u32[]{:S(2)}) collective-permute-start(bf16[16,3456]{1,0:T(8,128)(2,1)S(1)} %get-tuple-element.65), channel_id=1, source_target_pairs={{0,3},{1,2},{2,1},{3,0},{4,7},{5,6},{6,5},{7,4},{8,11},{9,10},{10,... | collective-permute-start | bytes 331784 | tf_op jit(solution)/shard_map/ppermute | solution.py:401
  26.0 1.0 %collective-permute-start.7 = (bf16[16,3456]{1,0:T(8,128)(2,1)S(1)}, bf16[16,3456]{1,0:T(8,128)(2,1)S(1)}, u32[]{:S(2)}, u32[]{:S(2)}) collective-permute-start(bf16[16,3456]{1,0:T(8,128)(2,1)S(1)} %get-tuple-element.66), channel_id=1, source_target_pairs={{0,1},{1,0},{2,3},{3,2},{4,5},{5,4},{6,7},{7,6},{8,9},{9,8},{10,11... | collective-permute-start | bytes 331784 | tf_op jit(solution)/shard_map/ppermute | solution.py:401
  27.0 1.1 %collective-permute-start.8 = (bf16[16,3456]{1,0:T(8,128)(2,1)S(1)}, bf16[16,3456]{1,0:T(8,128)(2,1)S(1)}, u32[]{:S(2)}, u32[]{:S(2)}) collective-permute-start(bf16[16,3456]{1,0:T(8,128)(2,1)S(1)} %get-tuple-element.67), channel_id=1, source_target_pairs={{0,2},{1,3},{2,0},{3,1},{4,6},{5,7},{6,4},{7,5},{8,10},{9,11},{10,... | collective-permute-start | bytes 331784 | tf_op jit(solution)/shard_map/ppermute | solution.py:401
  28.0 0.0 collective-permute-done.4.got
  28.0 0.1 shard_map.82
  28.1 2.5 %collective-permute-start.10 = (bf16[16,3456]{1,0:T(8,128)(2,1)S(1)}, bf16[16,3456]{1,0:T(8,128)(2,1)S(1)}, u32[]{:S(2)}, u32[]{:S(2)}) collective-permute-start(bf16[16,3456]{1,0:T(8,128)(2,1)S(1)} %get-tuple-element.70), channel_id=1, source_target_pairs={{0,5},{1,4},{2,7},{3,6},{4,1},{5,0},{6,3},{7,2},{8,13},{9,12},{10,... | collective-permute-start | bytes 331784 | tf_op jit(solution)/shard_map/ppermute | solution.py:401
  30.6 0.0 collective-permute-start.11
  30.6 0.7 %collective-permute-done.6.refs_1_ = bf16[16,3456]{1,0:T(8,128)(2,1)S(1)} collective-permute-done((bf16[16,3456]{1,0:T(8,128)(2,1)S(1)}, bf16[16,3456]{1,0:T(8,128)(2,1)S(1)}, u32[]{:S(2)}, u32[]{:S(2)}) %collective-permute-start.6) | collective-permute-done | bytes 110624 | tf_op jit(solution)/shard_map/ppermute | solution.py:401
  31.3 1.0 %collective-permute-start.9 = (bf16[16,3456]{1,0:T(8,128)(2,1)S(1)}, bf16[16,3456]{1,0:T(8,128)(2,1)S(1)}, u32[]{:S(2)}, u32[]{:S(2)}) collective-permute-start(bf16[16,3456]{1,0:T(8,128)(2,1)S(1)} %get-tuple-element.69), channel_id=1, source_target_pairs={{0,1},{1,0},{2,3},{3,2},{4,5},{5,4},{6,7},{7,6},{8,9},{9,8},{10,11... | collective-permute-start | bytes 331784 | tf_op jit(solution)/shard_map/ppermute | solution.py:401
  32.3 0.1 collective-permute-done.7.refs_2_
  32.4 1.0 %collective-permute-done.8.refs_3_ = bf16[16,3456]{1,0:T(8,128)(2,1)S(1)} collective-permute-done((bf16[16,3456]{1,0:T(8,128)(2,1)S(1)}, bf16[16,3456]{1,0:T(8,128)(2,1)S(1)}, u32[]{:S(2)}, u32[]{:S(2)}) %collective-permute-start.8) | collective-permute-done | bytes 110624 | tf_op jit(solution)/shard_map/ppermute | solution.py:401
  33.4 0.1 shard_map.84.one
  33.4 2.1 %collective-permute-start.18 = (bf16[16,3456]{1,0:T(8,128)(2,1)S(1)}, bf16[16,3456]{1,0:T(8,128)(2,1)S(1)}, u32[]{:S(2)}, u32[]{:S(2)}) collective-permute-start(bf16[16,3456]{1,0:T(8,128)(2,1)S(1)} %shard_map.84.one), channel_id=1, source_target_pairs={{0,4},{1,5},{2,6},{3,7},{4,0},{5,1},{6,2},{7,3},{8,12},{9,13},{10,... | collective-permute-start | bytes 331784 | tf_op jit(solution)/shard_map/ppermute | solution.py:401
  35.5 0.0 collective-permute-done.10.refs_2_
  35.5 0.3 collective-permute-done.11.refs_3_
  35.8 0.2 collective-permute-done.9.refs_1_
  36.1 0.1 shard_map.85.one
  36.1 1.0 %collective-permute-start.12 = (bf16[16,3456]{1,0:T(8,128)(2,1)S(1)}, bf16[16,3456]{1,0:T(8,128)(2,1)S(1)}, u32[]{:S(2)}, u32[]{:S(2)}) collective-permute-start(bf16[16,3456]{1,0:T(8,128)(2,1)S(1)} %shard_map.85.one), channel_id=1, source_target_pairs={{0,2},{1,3},{2,0},{3,1},{4,6},{5,7},{6,4},{7,5},{8,10},{9,11},{10,... | collective-permute-start | bytes 331784 | tf_op jit(solution)/shard_map/ppermute | solution.py:401
  37.2 1.4 %collective-permute-done.18.two = bf16[16,3456]{1,0:T(8,128)(2,1)S(1)} collective-permute-done((bf16[16,3456]{1,0:T(8,128)(2,1)S(1)}, bf16[16,3456]{1,0:T(8,128)(2,1)S(1)}, u32[]{:S(2)}, u32[]{:S(2)}) %collective-permute-start.18) | collective-permute-done | bytes 110624 | tf_op jit(solution)/shard_map/ppermute | solution.py:401
  38.6 2.1 %collective-permute-start.19 = (bf16[16,3456]{1,0:T(8,128)(2,1)S(1)}, bf16[16,3456]{1,0:T(8,128)(2,1)S(1)}, u32[]{:S(2)}, u32[]{:S(2)}) collective-permute-start(bf16[16,3456]{1,0:T(8,128)(2,1)S(1)} %shard_map.90.one), channel_id=1, source_target_pairs={{0,8},{1,9},{2,10},{3,11},{4,12},{5,13},{6,14},{7,15},{8,0},{9,1},... | collective-permute-start | bytes 331784 | tf_op jit(solution)/shard_map/ppermute | solution.py:401
  40.6 0.3 collective-permute-done.12.two
  41.0 2.0 %collective-permute-start.13 = (bf16[16,3456]{1,0:T(8,128)(2,1)S(1)}, bf16[16,3456]{1,0:T(8,128)(2,1)S(1)}, u32[]{:S(2)}, u32[]{:S(2)}) collective-permute-start(bf16[16,3456]{1,0:T(8,128)(2,1)S(1)} %shard_map.86.one), channel_id=1, source_target_pairs={{0,8},{1,9},{2,10},{3,11},{4,12},{5,13},{6,14},{7,15},{8,0},{9,1},... | collective-permute-start | bytes 331784 | tf_op jit(solution)/shard_map/ppermute | solution.py:401
  42.9 1.3 %collective-permute-done.19.two = bf16[16,3456]{1,0:T(8,128)(2,1)S(1)} collective-permute-done((bf16[16,3456]{1,0:T(8,128)(2,1)S(1)}, bf16[16,3456]{1,0:T(8,128)(2,1)S(1)}, u32[]{:S(2)}, u32[]{:S(2)}) %collective-permute-start.19) | collective-permute-done | bytes 110624 | tf_op jit(solution)/shard_map/ppermute | solution.py:401
  44.3 1.5 %collective-permute-start.20 = (bf16[432,128]{1,0:T(8,128)(2,1)S(1)}, bf16[432,128]{1,0:T(8,128)(2,1)S(1)}, u32[]{:S(2)}, u32[]{:S(2)}) collective-permute-start(bf16[432,128]{1,0:T(8,128)(2,1)S(1)} %shard_map.91.refs_0_), channel_id=1, source_target_pairs={{0,3},{1,2},{2,1},{3,0},{4,7},{5,6},{6,5},{7,4},{8,11},{9,10},{10,... | collective-permute-start | bytes 331784 | tf_op jit(solution)/shard_map/ppermute | solution.py:401
  45.8 1.0 %collective-permute-start.21 = (bf16[432,128]{1,0:T(8,128)(2,1)S(1)}, bf16[432,128]{1,0:T(8,128)(2,1)S(1)}, u32[]{:S(2)}, u32[]{:S(2)}) collective-permute-start(bf16[432,128]{1,0:T(8,128)(2,1)S(1)} %shard_map.91.refs_0_), channel_id=1, source_target_pairs={{0,1},{1,0},{2,3},{3,2},{4,5},{5,4},{6,7},{7,6},{8,9},{9,8},{10,11... | collective-permute-start | bytes 331784 | tf_op jit(solution)/shard_map/ppermute | solution.py:401
  46.8 1.1 %collective-permute-start.22 = (bf16[432,128]{1,0:T(8,128)(2,1)S(1)}, bf16[432,128]{1,0:T(8,128)(2,1)S(1)}, u32[]{:S(2)}, u32[]{:S(2)}) collective-permute-start(bf16[432,128]{1,0:T(8,128)(2,1)S(1)} %shard_map.91.refs_0_), channel_id=1, source_target_pairs={{0,2},{1,3},{2,0},{3,1},{4,6},{5,7},{6,4},{7,5},{8,10},{9,11},{10,... | collective-permute-start | bytes 331784 | tf_op jit(solution)/shard_map/ppermute | solution.py:401
  47.9 0.0 collective-permute-done.13.two
  47.9 2.4 %collective-permute-start.14 = (bf16[432,128]{1,0:T(8,128)(2,1)S(1)}, bf16[432,128]{1,0:T(8,128)(2,1)S(1)}, u32[]{:S(2)}, u32[]{:S(2)}) collective-permute-start(bf16[432,128]{1,0:T(8,128)(2,1)S(1)} %shard_map.87.refs_0_), channel_id=1, source_target_pairs={{0,5},{1,4},{2,7},{3,6},{4,1},{5,0},{6,3},{7,2},{8,13},{9,12},{10,... | collective-permute-start | bytes 331784 | tf_op jit(solution)/shard_map/ppermute | solution.py:401
  50.4 0.1 collective-permute-start.15
  50.5 0.0 collective-permute-done.20.refs_1_
  50.5 1.0 %collective-permute-start.16 = (bf16[432,128]{1,0:T(8,128)(2,1)S(1)}, bf16[432,128]{1,0:T(8,128)(2,1)S(1)}, u32[]{:S(2)}, u32[]{:S(2)}) collective-permute-start(bf16[432,128]{1,0:T(8,128)(2,1)S(1)} %shard_map.87.refs_0_), channel_id=1, source_target_pairs={{0,1},{1,0},{2,3},{3,2},{4,5},{5,4},{6,7},{7,6},{8,9},{9,8},{10,11... | collective-permute-start | bytes 331784 | tf_op jit(solution)/shard_map/ppermute | solution.py:401
  51.5 0.0 collective-permute-done.21.refs_2_
  51.5 1.2 %collective-permute-done.22.refs_3_ = bf16[432,128]{1,0:T(8,128)(2,1)S(1)} collective-permute-done((bf16[432,128]{1,0:T(8,128)(2,1)S(1)}, bf16[432,128]{1,0:T(8,128)(2,1)S(1)}, u32[]{:S(2)}, u32[]{:S(2)}) %collective-permute-start.22) | collective-permute-done | bytes 110624 | tf_op jit(solution)/shard_map/ppermute | solution.py:401
  52.7 0.1 collective-permute-start.23
  52.8 0.8 %collective-permute-done.14.refs_1_ = bf16[432,128]{1,0:T(8,128)(2,1)S(1)} collective-permute-done((bf16[432,128]{1,0:T(8,128)(2,1)S(1)}, bf16[432,128]{1,0:T(8,128)(2,1)S(1)}, u32[]{:S(2)}, u32[]{:S(2)}) %collective-permute-start.14) | collective-permute-done | bytes 110624 | tf_op jit(solution)/shard_map/ppermute | solution.py:401
  53.6 1.5 %collective-permute-done.15.refs_2_ = bf16[432,128]{1,0:T(8,128)(2,1)S(1)} collective-permute-done((bf16[432,128]{1,0:T(8,128)(2,1)S(1)}, bf16[432,128]{1,0:T(8,128)(2,1)S(1)}, u32[]{:S(2)}, u32[]{:S(2)}) %collective-permute-start.15) | collective-permute-done | bytes 110624 | tf_op jit(solution)/shard_map/ppermute | solution.py:401
  55.1 0.1 collective-permute-done.16.refs_3_
  55.2 0.1 shard_map.88.own
  55.3 0.1 collective-permute-start.17
  55.3 1.5 %shard_map.94 = bf16[512,128]{1,0:T(8,128)(2,1)} custom-call(bf16[512,1152]{1,0:T(8,128)(2,1)S(1)} %get-tuple-element.75.st_own, bf16[512,128]{1,0:T(8,128)(2,1)S(1)} %get-tuple-element.43.grads, bf16[48,128]{1,0:T(8,128)(2,1)S(1)} %get-tuple-element.52.marks3, bf16[384,1152]{1,0:T(8,128)(2,1)S(1)} %get-tuple-element.76.w1_wide), custom_call_target="tpu_custom_call" | custom-call | flops 452984832 | bytes 2338816 | tf_op jit(solution)/shard_map/pallas_call | solution.py:35
  56.8 0.0 collective-permute-done.23.other
  56.8 1.3 %shard_map.93 = f32[3456,128]{1,0:T(8,128)} custom-call(bf16[1728,128]{1,0:T(8,128)(2,1)S(1)} %shard_map.92.own, bf16[1728,128]{1,0:T(8,128)(2,1)S(1)} %collective-permute-done.23.other), custom_call_target="tpu_custom_call" | custom-call | bytes 2654208 | tf_op jit(solution)/shard_map/pallas_call | solution.py:35
  58.2 0.0 collective-permute-done.17.other
  58.2 1.3 %shard_map.89 = f32[3456,128]{1,0:T(8,128)} custom-call(bf16[1728,128]{1,0:T(8,128)(2,1)S(1)} %shard_map.88.own, bf16[1728,128]{1,0:T(8,128)(2,1)S(1)} %collective-permute-done.17.other), custom_call_target="tpu_custom_call" | custom-call | bytes 2654208 | tf_op jit(solution)/shard_map/pallas_call | solution.py:35
  (5 shorter events, 0.2 us)
Async XLA Ops:
  2.4 8.6 %collective-permute-start = (bf16[272,128]{1,0:T(8,128)(2,1)S(1)}, bf16[272,128]{1,0:T(8,128)(2,1)S(1)}, u32[]{:S(2)}, u32[]{:S(2)}) collective-permute-start(bf16[272,128]{1,0:T(8,128)(2,1)S(1)} %get-tuple-element.45), channel_id=1, source_target_pairs={{1,2},{2,1},{5,6},{6,5},{9,10},{10,9},{13,14},{14,13},{17,18},{18,... | collective-permute-start | bytes 208904 | tf_op jit(solution)/shard_map/ppermute | solution.py:633
  3.1 9.0 %collective-permute-start.1 = (bf16[272,128]{1,0:T(8,128)(2,1)S(1)}, bf16[272,128]{1,0:T(8,128)(2,1)S(1)}, u32[]{:S(2)}, u32[]{:S(2)}) collective-permute-start(bf16[272,128]{1,0:T(8,128)(2,1)S(1)} %get-tuple-element.46), channel_id=1, source_target_pairs={{0,1},{1,0},{2,3},{3,2},{4,5},{5,4},{6,7},{7,6},{8,9},{9,8},{10,11... | collective-permute-start | bytes 208904 | tf_op jit(solution)/shard_map/ppermute | solution.py:633
  12.2 7.2 %collective-permute-start.2 = (bf16[400,128]{1,0:T(8,128)(2,1)S(1)}, bf16[400,128]{1,0:T(8,128)(2,1)S(1)}, u32[]{:S(2)}, u32[]{:S(2)}) collective-permute-start(bf16[400,128]{1,0:T(8,128)(2,1)S(1)} %get-tuple-element.53), channel_id=1, source_target_pairs={{4,8},{8,4},{5,9},{9,5},{6,10},{10,6},{7,11},{11,7},{20,24},{24,20... | collective-permute-start | bytes 307208 | tf_op jit(solution)/shard_map/ppermute | solution.py:633
  12.9 7.1 %collective-permute-start.3 = (bf16[400,128]{1,0:T(8,128)(2,1)S(1)}, bf16[400,128]{1,0:T(8,128)(2,1)S(1)}, u32[]{:S(2)}, u32[]{:S(2)}) collective-permute-start(bf16[400,128]{1,0:T(8,128)(2,1)S(1)} %get-tuple-element.54), channel_id=1, source_target_pairs={{0,4},{4,0},{1,5},{5,1},{2,6},{6,2},{3,7},{7,3},{8,12},{12,8},{9,1... | collective-permute-start | bytes 307208 | tf_op jit(solution)/shard_map/ppermute | solution.py:633
  21.9 2.5 %collective-permute-start.5 = (f32[64,3456]{1,0:T(8,128)S(1)}, f32[64,3456]{1,0:T(8,128)S(1)}, u32[]{:S(2)}, u32[]{:S(2)}) collective-permute-start(f32[64,3456]{1,0:T(8,128)S(1)} %get-tuple-element.63), channel_id=1, source_target_pairs={{0,16},{16,0},{1,17},{17,1},{2,18},{18,2},{3,19},{19,3},{4,20},{20... | collective-permute-start | bytes 2654216 | tf_op jit(solution)/shard_map/ppermute | solution.py:391
  23.7 4.3 %collective-permute-start.4 = (f32[64,3456]{1,0:T(8,128)S(1)}, f32[64,3456]{1,0:T(8,128)S(1)}, u32[]{:S(2)}, u32[]{:S(2)}) collective-permute-start(f32[64,3456]{1,0:T(8,128)S(1)} %get-tuple-element.60), channel_id=1, source_target_pairs={{0,16},{16,0},{1,17},{17,1},{2,18},{18,2},{3,19},{19,3},{4,20},{20... | collective-permute-start | bytes 2654216 | tf_op jit(solution)/shard_map/ppermute | solution.py:391
  24.5 6.9 %collective-permute-start.6 = (bf16[16,3456]{1,0:T(8,128)(2,1)S(1)}, bf16[16,3456]{1,0:T(8,128)(2,1)S(1)}, u32[]{:S(2)}, u32[]{:S(2)}) collective-permute-start(bf16[16,3456]{1,0:T(8,128)(2,1)S(1)} %get-tuple-element.65), channel_id=1, source_target_pairs={{0,3},{1,2},{2,1},{3,0},{4,7},{5,6},{6,5},{7,4},{8,11},{9,10},{10,... | collective-permute-start | bytes 331784 | tf_op jit(solution)/shard_map/ppermute | solution.py:401
  26.0 6.4 %collective-permute-start.7 = (bf16[16,3456]{1,0:T(8,128)(2,1)S(1)}, bf16[16,3456]{1,0:T(8,128)(2,1)S(1)}, u32[]{:S(2)}, u32[]{:S(2)}) collective-permute-start(bf16[16,3456]{1,0:T(8,128)(2,1)S(1)} %get-tuple-element.66), channel_id=1, source_target_pairs={{0,1},{1,0},{2,3},{3,2},{4,5},{5,4},{6,7},{7,6},{8,9},{9,8},{10,11... | collective-permute-start | bytes 331784 | tf_op jit(solution)/shard_map/ppermute | solution.py:401
  27.0 6.4 %collective-permute-start.8 = (bf16[16,3456]{1,0:T(8,128)(2,1)S(1)}, bf16[16,3456]{1,0:T(8,128)(2,1)S(1)}, u32[]{:S(2)}, u32[]{:S(2)}) collective-permute-start(bf16[16,3456]{1,0:T(8,128)(2,1)S(1)} %get-tuple-element.67), channel_id=1, source_target_pairs={{0,2},{1,3},{2,0},{3,1},{4,6},{5,7},{6,4},{7,5},{8,10},{9,11},{10,... | collective-permute-start | bytes 331784 | tf_op jit(solution)/shard_map/ppermute | solution.py:401
  28.1 7.4 %collective-permute-start.10 = (bf16[16,3456]{1,0:T(8,128)(2,1)S(1)}, bf16[16,3456]{1,0:T(8,128)(2,1)S(1)}, u32[]{:S(2)}, u32[]{:S(2)}) collective-permute-start(bf16[16,3456]{1,0:T(8,128)(2,1)S(1)} %get-tuple-element.70), channel_id=1, source_target_pairs={{0,5},{1,4},{2,7},{3,6},{4,1},{5,0},{6,3},{7,2},{8,13},{9,12},{10,... | collective-permute-start | bytes 331784 | tf_op jit(solution)/shard_map/ppermute | solution.py:401
  30.6 5.2 %collective-permute-start.11 = (bf16[16,3456]{1,0:T(8,128)(2,1)S(1)}, bf16[16,3456]{1,0:T(8,128)(2,1)S(1)}, u32[]{:S(2)}, u32[]{:S(2)}) collective-permute-start(bf16[16,3456]{1,0:T(8,128)(2,1)S(1)} %get-tuple-element.71), channel_id=1, source_target_pairs={{0,4},{1,5},{2,6},{3,7},{4,0},{5,1},{6,2},{7,3},{8,12},{9,13},{10,... | collective-permute-start | bytes 331784 | tf_op jit(solution)/shard_map/ppermute | solution.py:401
  31.3 4.7 %collective-permute-start.9 = (bf16[16,3456]{1,0:T(8,128)(2,1)S(1)}, bf16[16,3456]{1,0:T(8,128)(2,1)S(1)}, u32[]{:S(2)}, u32[]{:S(2)}) collective-permute-start(bf16[16,3456]{1,0:T(8,128)(2,1)S(1)} %get-tuple-element.69), channel_id=1, source_target_pairs={{0,1},{1,0},{2,3},{3,2},{4,5},{5,4},{6,7},{7,6},{8,9},{9,8},{10,11... | collective-permute-start | bytes 331784 | tf_op jit(solution)/shard_map/ppermute | solution.py:401
  33.4 5.1 %collective-permute-start.18 = (bf16[16,3456]{1,0:T(8,128)(2,1)S(1)}, bf16[16,3456]{1,0:T(8,128)(2,1)S(1)}, u32[]{:S(2)}, u32[]{:S(2)}) collective-permute-start(bf16[16,3456]{1,0:T(8,128)(2,1)S(1)} %shard_map.84.one), channel_id=1, source_target_pairs={{0,4},{1,5},{2,6},{3,7},{4,0},{5,1},{6,2},{7,3},{8,12},{9,13},{10,... | collective-permute-start | bytes 331784 | tf_op jit(solution)/shard_map/ppermute | solution.py:401
  36.1 4.8 %collective-permute-start.12 = (bf16[16,3456]{1,0:T(8,128)(2,1)S(1)}, bf16[16,3456]{1,0:T(8,128)(2,1)S(1)}, u32[]{:S(2)}, u32[]{:S(2)}) collective-permute-start(bf16[16,3456]{1,0:T(8,128)(2,1)S(1)} %shard_map.85.one), channel_id=1, source_target_pairs={{0,2},{1,3},{2,0},{3,1},{4,6},{5,7},{6,4},{7,5},{8,10},{9,11},{10,... | collective-permute-start | bytes 331784 | tf_op jit(solution)/shard_map/ppermute | solution.py:401
  38.6 5.7 %collective-permute-start.19 = (bf16[16,3456]{1,0:T(8,128)(2,1)S(1)}, bf16[16,3456]{1,0:T(8,128)(2,1)S(1)}, u32[]{:S(2)}, u32[]{:S(2)}) collective-permute-start(bf16[16,3456]{1,0:T(8,128)(2,1)S(1)} %shard_map.90.one), channel_id=1, source_target_pairs={{0,8},{1,9},{2,10},{3,11},{4,12},{5,13},{6,14},{7,15},{8,0},{9,1},... | collective-permute-start | bytes 331784 | tf_op jit(solution)/shard_map/ppermute | solution.py:401
  41.0 6.9 %collective-permute-start.13 = (bf16[16,3456]{1,0:T(8,128)(2,1)S(1)}, bf16[16,3456]{1,0:T(8,128)(2,1)S(1)}, u32[]{:S(2)}, u32[]{:S(2)}) collective-permute-start(bf16[16,3456]{1,0:T(8,128)(2,1)S(1)} %shard_map.86.one), channel_id=1, source_target_pairs={{0,8},{1,9},{2,10},{3,11},{4,12},{5,13},{6,14},{7,15},{8,0},{9,1},... | collective-permute-start | bytes 331784 | tf_op jit(solution)/shard_map/ppermute | solution.py:401
  44.3 6.1 %collective-permute-start.20 = (bf16[432,128]{1,0:T(8,128)(2,1)S(1)}, bf16[432,128]{1,0:T(8,128)(2,1)S(1)}, u32[]{:S(2)}, u32[]{:S(2)}) collective-permute-start(bf16[432,128]{1,0:T(8,128)(2,1)S(1)} %shard_map.91.refs_0_), channel_id=1, source_target_pairs={{0,3},{1,2},{2,1},{3,0},{4,7},{5,6},{6,5},{7,4},{8,11},{9,10},{10,... | collective-permute-start | bytes 331784 | tf_op jit(solution)/shard_map/ppermute | solution.py:401
  45.8 5.7 %collective-permute-start.21 = (bf16[432,128]{1,0:T(8,128)(2,1)S(1)}, bf16[432,128]{1,0:T(8,128)(2,1)S(1)}, u32[]{:S(2)}, u32[]{:S(2)}) collective-permute-start(bf16[432,128]{1,0:T(8,128)(2,1)S(1)} %shard_map.91.refs_0_), channel_id=1, source_target_pairs={{0,1},{1,0},{2,3},{3,2},{4,5},{5,4},{6,7},{7,6},{8,9},{9,8},{10,11... | collective-permute-start | bytes 331784 | tf_op jit(solution)/shard_map/ppermute | solution.py:401
  46.8 5.9 %collective-permute-start.22 = (bf16[432,128]{1,0:T(8,128)(2,1)S(1)}, bf16[432,128]{1,0:T(8,128)(2,1)S(1)}, u32[]{:S(2)}, u32[]{:S(2)}) collective-permute-start(bf16[432,128]{1,0:T(8,128)(2,1)S(1)} %shard_map.91.refs_0_), channel_id=1, source_target_pairs={{0,2},{1,3},{2,0},{3,1},{4,6},{5,7},{6,4},{7,5},{8,10},{9,11},{10,... | collective-permute-start | bytes 331784 | tf_op jit(solution)/shard_map/ppermute | solution.py:401
  47.9 5.7 %collective-permute-start.14 = (bf16[432,128]{1,0:T(8,128)(2,1)S(1)}, bf16[432,128]{1,0:T(8,128)(2,1)S(1)}, u32[]{:S(2)}, u32[]{:S(2)}) collective-permute-start(bf16[432,128]{1,0:T(8,128)(2,1)S(1)} %shard_map.87.refs_0_), channel_id=1, source_target_pairs={{0,5},{1,4},{2,7},{3,6},{4,1},{5,0},{6,3},{7,2},{8,13},{9,12},{10,... | collective-permute-start | bytes 331784 | tf_op jit(solution)/shard_map/ppermute | solution.py:401
  50.4 4.7 %collective-permute-start.15 = (bf16[432,128]{1,0:T(8,128)(2,1)S(1)}, bf16[432,128]{1,0:T(8,128)(2,1)S(1)}, u32[]{:S(2)}, u32[]{:S(2)}) collective-permute-start(bf16[432,128]{1,0:T(8,128)(2,1)S(1)} %shard_map.87.refs_0_), channel_id=1, source_target_pairs={{0,4},{1,5},{2,6},{3,7},{4,0},{5,1},{6,2},{7,3},{8,12},{9,13},{10,... | collective-permute-start | bytes 331784 | tf_op jit(solution)/shard_map/ppermute | solution.py:401
  50.5 4.7 %collective-permute-start.16 = (bf16[432,128]{1,0:T(8,128)(2,1)S(1)}, bf16[432,128]{1,0:T(8,128)(2,1)S(1)}, u32[]{:S(2)}, u32[]{:S(2)}) collective-permute-start(bf16[432,128]{1,0:T(8,128)(2,1)S(1)} %shard_map.87.refs_0_), channel_id=1, source_target_pairs={{0,1},{1,0},{2,3},{3,2},{4,5},{5,4},{6,7},{7,6},{8,9},{9,8},{10,11... | collective-permute-start | bytes 331784 | tf_op jit(solution)/shard_map/ppermute | solution.py:401
  52.7 4.1 %collective-permute-start.23 = (bf16[1728,128]{1,0:T(8,128)(2,1)S(1)}, bf16[1728,128]{1,0:T(8,128)(2,1)S(1)}, u32[]{:S(2)}, u32[]{:S(2)}) collective-permute-start(bf16[1728,128]{1,0:T(8,128)(2,1)S(1)} %shard_map.92.own), channel_id=1, source_target_pairs={{0,16},{16,0},{1,17},{17,1},{2,18},{18,2},{3,19},{19,3},{4,20},{20... | collective-permute-start | bytes 1327112 | tf_op jit(solution)/shard_map/ppermute | solution.py:391
  55.3 2.9 %collective-permute-start.17 = (bf16[1728,128]{1,0:T(8,128)(2,1)S(1)}, bf16[1728,128]{1,0:T(8,128)(2,1)S(1)}, u32[]{:S(2)}, u32[]{:S(2)}) collective-permute-start(bf16[1728,128]{1,0:T(8,128)(2,1)S(1)} %shard_map.88.own), channel_id=1, source_target_pairs={{0,16},{16,0},{1,17},{17,1},{2,18},{18,2},{3,19},{19,3},{4,20},{20... | collective-permute-start | bytes 1327112 | tf_op jit(solution)/shard_map/ppermute | solution.py:391

commit v7 on v6

--- a/solution.py
+++ b/solution.py
@@ -579,7 +579,7 @@
     for n, (bits_one, bits_two) in enumerate(zip(*steps)):
         add = laid_pair if n == len(steps[0]) - 1 else pair_stage
         got_one, got_two = cross(one, bits_one), cross(two, bits_two)
-        one = add(after(one, two), got_one)
+        one = add(one, got_one)
         if other is None:
             other = beside(two)
         two = add(two, got_two)

time: 59.7 us -> 59.7 us (level)
  no operation moved by 1% of the time
where the time goes in v7:
time: 59.7 us; the launch traced here: 59.5 us
  starting transfers between devices  33.7 us (56%)
  Pallas kernels  11.1 us (19%)
  waiting for transfers between devices  10.7 us (18%)
  other arithmetic  2.59 us (4%)
  between operations  1.44 us (2%)
    ppermute x16, starting transfers between devices, cross(): return lax.ppermute(value, ('dp', 'blk'), pairs)  21.4 us
    pallas_call x19, Pallas kernels, call(): pl.pallas_call(body, out_shape=list(outs), in_specs=specs, out_specs=[VM]...  11.1 us
    ppermute x2, starting transfers between devices, beside(): lax.ppermute(one, 'blk', pairs[0])  10.2 us
    ppermute x16, waiting for transfers between devices, cross(): return lax.ppermute(value, ('dp', 'blk'), pairs)  8.85 us
    ppermute x2, waiting for transfers between devices, beside(): lax.ppermute(one, 'blk', pairs[0])  1.66 us
    another operation x1, other arithmetic, on_device(): jnp.stack([w_first, w_second])  1.6 us
    ppermute x2, starting transfers between devices, beside(): lax.ppermute(two, 'blk', pairs[1])  1.33 us
  transfers between devices with their start and end apart: 24, of which 15 were waited for; matrix products, arithmetic and copies ran while one was open for 3% of the time, Pallas kernels for 13%

profile of v7, /device:TPU:0, one launch (start us, length us, event | category | flops | bytes accessed | tf_op | source)
XLA Modules:
  0.0 59.5 jit_solution(7430665043805143512)
XLA Ops:
  1.3 1.0 %pad_maximum_fusion.1.both = bf16[2,512,128]{2,1,0:T(8,128)(2,1)S(1)} fusion(bf16[1,512,128]{2,1,0:T(8,128)(2,1)} %param.9, bf16[1,512,128]{2,1,0:T(8,128)(2,1)} %param.5), kind=kLoop, calls=%fused_computation.1 | loop fusion | flops 131072 | bytes 524288 | tf_op jit(solution)/shard_map/stack | solution.py:644
  2.3 0.1 shard_map.76
  2.4 0.7 %collective-permute-start = (bf16[272,128]{1,0:T(8,128)(2,1)S(1)}, bf16[272,128]{1,0:T(8,128)(2,1)S(1)}, u32[]{:S(2)}, u32[]{:S(2)}) collective-permute-start(bf16[272,128]{1,0:T(8,128)(2,1)S(1)} %get-tuple-element.43), channel_id=1, source_target_pairs={{1,2},{2,1},{5,6},{6,5},{9,10},{10,9},{13,14},{14,13},{17,18},{18,... | collective-permute-start | bytes 208904 | tf_op jit(solution)/shard_map/ppermute | solution.py:633
  3.1 5.7 %collective-permute-start.1 = (bf16[272,128]{1,0:T(8,128)(2,1)S(1)}, bf16[272,128]{1,0:T(8,128)(2,1)S(1)}, u32[]{:S(2)}, u32[]{:S(2)}) collective-permute-start(bf16[272,128]{1,0:T(8,128)(2,1)S(1)} %get-tuple-element.44), channel_id=1, source_target_pairs={{0,1},{1,0},{2,3},{3,2},{4,5},{5,4},{6,7},{7,6},{8,9},{9,8},{10,11... | collective-permute-start | bytes 208904 | tf_op jit(solution)/shard_map/ppermute | solution.py:633
  8.8 1.6 %pad_maximum_fusion.src = bf16[2,3456,128]{2,1,0:T(8,128)(2,1)S(1)} fusion(bf16[1,3456,128]{2,1,0:T(8,128)(2,1)} %bitcast.3, bf16[1,3456,128]{2,1,0:T(8,128)(2,1)} %bitcast.4), kind=kLoop, calls=%fused_computation | loop fusion | flops 884736 | bytes 3538944 | tf_op jit(solution)/shard_map/stack | solution.py:655
  10.4 0.6 %shard_map.77 = (bf16[384,1152]{1,0:T(8,128)(2,1)S(1)}, bf16[1152,384]{1,0:T(8,128)(2,1)S(1)}, bf16[384,1152]{1,0:T(8,128)(2,1)S(1)}) custom-call(bf16[2,3456,128]{2,1,0:T(8,128)(2,1)S(1)} %pad_maximum_fusion.src), custom_call_target="tpu_custom_call" | custom-call | bytes 4423680 | tf_op jit(solution)/shard_map/pallas_call | solution.py:35
  11.0 0.0 collective-permute-done.z_odd
  11.0 1.1 %collective-permute-done.1.z_even = bf16[272,128]{1,0:T(8,128)(2,1)S(1)} collective-permute-done((bf16[272,128]{1,0:T(8,128)(2,1)S(1)}, bf16[272,128]{1,0:T(8,128)(2,1)S(1)}, u32[]{:S(2)}, u32[]{:S(2)}) %collective-permute-start.1) | collective-permute-done | bytes 69664 | tf_op jit(solution)/shard_map/ppermute | solution.py:633
  12.1 0.1 shard_map.78
  12.2 0.7 %collective-permute-start.2 = (bf16[400,128]{1,0:T(8,128)(2,1)S(1)}, bf16[400,128]{1,0:T(8,128)(2,1)S(1)}, u32[]{:S(2)}, u32[]{:S(2)}) collective-permute-start(bf16[400,128]{1,0:T(8,128)(2,1)S(1)} %get-tuple-element.51), channel_id=1, source_target_pairs={{4,8},{8,4},{5,9},{9,5},{6,10},{10,6},{7,11},{11,7},{20,24},{24,20... | collective-permute-start | bytes 307208 | tf_op jit(solution)/shard_map/ppermute | solution.py:633
  12.9 4.5 %collective-permute-start.3 = (bf16[400,128]{1,0:T(8,128)(2,1)S(1)}, bf16[400,128]{1,0:T(8,128)(2,1)S(1)}, u32[]{:S(2)}, u32[]{:S(2)}) collective-permute-start(bf16[400,128]{1,0:T(8,128)(2,1)S(1)} %get-tuple-element.52), channel_id=1, source_target_pairs={{0,4},{4,0},{1,5},{5,1},{2,6},{6,2},{3,7},{7,3},{8,12},{12,8},{9,1... | collective-permute-start | bytes 307208 | tf_op jit(solution)/shard_map/ppermute | solution.py:633
  17.3 2.0 %shard_map.79 = (f32[640,128]{1,0:T(8,128)S(1)}, f32[640,128]{1,0:T(8,128)S(1)}, bf16[128,640]{1,0:T(8,128)(2,1)S(1)}) custom-call(f32[784,128]{1,0:T(8,128)S(1)} %get-tuple-element.45.deep_in, f32[784,128]{1,0:T(8,128)S(1)} %get-tuple-element.46.deep_g, bf16[512,128]{1,0:T(8,128)(2,1)S(1)} %get-tuple-element.40.inp, ...), custom_call_target="tpu_custom_call" | custom-call | flops 905969664 | bytes 3522560 | tf_op jit(solution)/shard_map/pallas_call | solution.py:35
  19.4 0.0 collective-permute-done.2.y_odd
  19.4 0.6 collective-permute-done.3.y_even
  20.0 1.9 %shard_map.80 = (f32[64,3456]{1,0:T(8,128)S(1)}, f32[64,3456]{1,0:T(8,128)S(1)}, f32[1024,128]{1,0:T(8,128)S(1)}, f32[1600,128]{1,0:T(8,128)S(1)}) custom-call(f32[784,128]{1,0:T(8,128)S(1)} %get-tuple-element.45.deep_in, f32[784,128]{1,0:T(8,128)S(1)} %get-tuple-element.46.deep_g, bf16[48,128]{1,0:T(8,128)(2,1)S(1)} %get-tuple-element.50.marks3, ...), custom_call_target="tpu_custom_call" | custom-call | flops 905969664 | bytes 5345280 | tf_op jit(solution)/shard_map/pallas_call | solution.py:35
  21.9 0.1 collective-permute-start.5
  22.0 1.7 %shard_map.81 = (f32[64,3456]{1,0:T(8,128)S(1)}, f32[64,3456]{1,0:T(8,128)S(1)}, bf16[512,1152]{1,0:T(8,128)(2,1)S(1)}) custom-call(f32[1600,128]{1,0:T(8,128)S(1)} %get-tuple-element.54.grid_g, f32[1024,128]{1,0:T(8,128)S(1)} %get-tuple-element.55.act, f32[640,128]{1,0:T(8,128)S(1)} %get-tuple-element.56.inner, ...), custom_call_target="tpu_custom_call" | custom-call | flops 905969664 | bytes 5885952 | tf_op jit(solution)/shard_map/pallas_call | solution.py:35
  23.7 0.6 collective-permute-start.4
  24.2 0.1 collective-permute-done.5.got
  24.4 0.1 shard_map.83
  24.5 1.5 %collective-permute-start.6 = (bf16[16,3456]{1,0:T(8,128)(2,1)S(1)}, bf16[16,3456]{1,0:T(8,128)(2,1)S(1)}, u32[]{:S(2)}, u32[]{:S(2)}) collective-permute-start(bf16[16,3456]{1,0:T(8,128)(2,1)S(1)} %get-tuple-element.63), channel_id=1, source_target_pairs={{0,3},{1,2},{2,1},{3,0},{4,7},{5,6},{6,5},{7,4},{8,11},{9,10},{10,... | collective-permute-start | bytes 331784 | tf_op jit(solution)/shard_map/ppermute | solution.py:401
  26.0 1.0 %collective-permute-start.7 = (bf16[16,3456]{1,0:T(8,128)(2,1)S(1)}, bf16[16,3456]{1,0:T(8,128)(2,1)S(1)}, u32[]{:S(2)}, u32[]{:S(2)}) collective-permute-start(bf16[16,3456]{1,0:T(8,128)(2,1)S(1)} %get-tuple-element.64), channel_id=1, source_target_pairs={{0,1},{1,0},{2,3},{3,2},{4,5},{5,4},{6,7},{7,6},{8,9},{9,8},{10,11... | collective-permute-start | bytes 331784 | tf_op jit(solution)/shard_map/ppermute | solution.py:401
  27.0 1.1 %collective-permute-start.8 = (bf16[16,3456]{1,0:T(8,128)(2,1)S(1)}, bf16[16,3456]{1,0:T(8,128)(2,1)S(1)}, u32[]{:S(2)}, u32[]{:S(2)}) collective-permute-start(bf16[16,3456]{1,0:T(8,128)(2,1)S(1)} %get-tuple-element.65), channel_id=1, source_target_pairs={{0,2},{1,3},{2,0},{3,1},{4,6},{5,7},{6,4},{7,5},{8,10},{9,11},{10,... | collective-permute-start | bytes 331784 | tf_op jit(solution)/shard_map/ppermute | solution.py:401
  28.0 0.0 collective-permute-done.4.got
  28.0 0.1 shard_map.82
  28.1 2.5 %collective-permute-start.10 = (bf16[16,3456]{1,0:T(8,128)(2,1)S(1)}, bf16[16,3456]{1,0:T(8,128)(2,1)S(1)}, u32[]{:S(2)}, u32[]{:S(2)}) collective-permute-start(bf16[16,3456]{1,0:T(8,128)(2,1)S(1)} %get-tuple-element.68), channel_id=1, source_target_pairs={{0,5},{1,4},{2,7},{3,6},{4,1},{5,0},{6,3},{7,2},{8,13},{9,12},{10,... | collective-permute-start | bytes 331784 | tf_op jit(solution)/shard_map/ppermute | solution.py:401
  30.6 0.0 collective-permute-start.11
  30.6 0.7 %collective-permute-done.6.refs_1_ = bf16[16,3456]{1,0:T(8,128)(2,1)S(1)} collective-permute-done((bf16[16,3456]{1,0:T(8,128)(2,1)S(1)}, bf16[16,3456]{1,0:T(8,128)(2,1)S(1)}, u32[]{:S(2)}, u32[]{:S(2)}) %collective-permute-start.6) | collective-permute-done | bytes 110624 | tf_op jit(solution)/shard_map/ppermute | solution.py:401
  31.3 1.0 %collective-permute-start.9 = (bf16[16,3456]{1,0:T(8,128)(2,1)S(1)}, bf16[16,3456]{1,0:T(8,128)(2,1)S(1)}, u32[]{:S(2)}, u32[]{:S(2)}) collective-permute-start(bf16[16,3456]{1,0:T(8,128)(2,1)S(1)} %get-tuple-element.67), channel_id=1, source_target_pairs={{0,1},{1,0},{2,3},{3,2},{4,5},{5,4},{6,7},{7,6},{8,9},{9,8},{10,11... | collective-permute-start | bytes 331784 | tf_op jit(solution)/shard_map/ppermute | solution.py:401
  32.3 0.1 collective-permute-done.7.refs_2_
  32.4 1.0 %collective-permute-done.8.refs_3_ = bf16[16,3456]{1,0:T(8,128)(2,1)S(1)} collective-permute-done((bf16[16,3456]{1,0:T(8,128)(2,1)S(1)}, bf16[16,3456]{1,0:T(8,128)(2,1)S(1)}, u32[]{:S(2)}, u32[]{:S(2)}) %collective-permute-start.8) | collective-permute-done | bytes 110624 | tf_op jit(solution)/shard_map/ppermute | solution.py:401
  33.4 0.1 shard_map.84.one
  33.4 2.1 %collective-permute-start.18 = (bf16[16,3456]{1,0:T(8,128)(2,1)S(1)}, bf16[16,3456]{1,0:T(8,128)(2,1)S(1)}, u32[]{:S(2)}, u32[]{:S(2)}) collective-permute-start(bf16[16,3456]{1,0:T(8,128)(2,1)S(1)} %shard_map.84.one), channel_id=1, source_target_pairs={{0,4},{1,5},{2,6},{3,7},{4,0},{5,1},{6,2},{7,3},{8,12},{9,13},{10,... | collective-permute-start | bytes 331784 | tf_op jit(solution)/shard_map/ppermute | solution.py:401
  35.5 0.0 collective-permute-done.10.refs_2_
  35.5 0.3 collective-permute-done.11.refs_3_
  35.8 0.2 collective-permute-done.9.refs_1_
  36.1 0.1 shard_map.85.one
  36.1 1.0 %collective-permute-start.12 = (bf16[16,3456]{1,0:T(8,128)(2,1)S(1)}, bf16[16,3456]{1,0:T(8,128)(2,1)S(1)}, u32[]{:S(2)}, u32[]{:S(2)}) collective-permute-start(bf16[16,3456]{1,0:T(8,128)(2,1)S(1)} %shard_map.85.one), channel_id=1, source_target_pairs={{0,2},{1,3},{2,0},{3,1},{4,6},{5,7},{6,4},{7,5},{8,10},{9,11},{10,... | collective-permute-start | bytes 331784 | tf_op jit(solution)/shard_map/ppermute | solution.py:401
  37.2 1.4 %collective-permute-done.18.two = bf16[16,3456]{1,0:T(8,128)(2,1)S(1)} collective-permute-done((bf16[16,3456]{1,0:T(8,128)(2,1)S(1)}, bf16[16,3456]{1,0:T(8,128)(2,1)S(1)}, u32[]{:S(2)}, u32[]{:S(2)}) %collective-permute-start.18) | collective-permute-done | bytes 110624 | tf_op jit(solution)/shard_map/ppermute | solution.py:401
  38.6 2.1 %collective-permute-start.19 = (bf16[16,3456]{1,0:T(8,128)(2,1)S(1)}, bf16[16,3456]{1,0:T(8,128)(2,1)S(1)}, u32[]{:S(2)}, u32[]{:S(2)}) collective-permute-start(bf16[16,3456]{1,0:T(8,128)(2,1)S(1)} %shard_map.90.one), channel_id=1, source_target_pairs={{0,8},{1,9},{2,10},{3,11},{4,12},{5,13},{6,14},{7,15},{8,0},{9,1},... | collective-permute-start | bytes 331784 | tf_op jit(solution)/shard_map/ppermute | solution.py:401
  40.6 0.3 collective-permute-done.12.two
  41.0 2.0 %collective-permute-start.13 = (bf16[16,3456]{1,0:T(8,128)(2,1)S(1)}, bf16[16,3456]{1,0:T(8,128)(2,1)S(1)}, u32[]{:S(2)}, u32[]{:S(2)}) collective-permute-start(bf16[16,3456]{1,0:T(8,128)(2,1)S(1)} %shard_map.86.one), channel_id=1, source_target_pairs={{0,8},{1,9},{2,10},{3,11},{4,12},{5,13},{6,14},{7,15},{8,0},{9,1},... | collective-permute-start | bytes 331784 | tf_op jit(solution)/shard_map/ppermute | solution.py:401
  42.9 1.3 %collective-permute-done.19.two = bf16[16,3456]{1,0:T(8,128)(2,1)S(1)} collective-permute-done((bf16[16,3456]{1,0:T(8,128)(2,1)S(1)}, bf16[16,3456]{1,0:T(8,128)(2,1)S(1)}, u32[]{:S(2)}, u32[]{:S(2)}) %collective-permute-start.19) | collective-permute-done | bytes 110624 | tf_op jit(solution)/shard_map/ppermute | solution.py:401
  44.3 1.5 %collective-permute-start.20 = (bf16[432,128]{1,0:T(8,128)(2,1)S(1)}, bf16[432,128]{1,0:T(8,128)(2,1)S(1)}, u32[]{:S(2)}, u32[]{:S(2)}) collective-permute-start(bf16[432,128]{1,0:T(8,128)(2,1)S(1)} %shard_map.91.refs_0_), channel_id=1, source_target_pairs={{0,3},{1,2},{2,1},{3,0},{4,7},{5,6},{6,5},{7,4},{8,11},{9,10},{10,... | collective-permute-start | bytes 331784 | tf_op jit(solution)/shard_map/ppermute | solution.py:401
  45.8 1.0 %collective-permute-start.21 = (bf16[432,128]{1,0:T(8,128)(2,1)S(1)}, bf16[432,128]{1,0:T(8,128)(2,1)S(1)}, u32[]{:S(2)}, u32[]{:S(2)}) collective-permute-start(bf16[432,128]{1,0:T(8,128)(2,1)S(1)} %shard_map.91.refs_0_), channel_id=1, source_target_pairs={{0,1},{1,0},{2,3},{3,2},{4,5},{5,4},{6,7},{7,6},{8,9},{9,8},{10,11... | collective-permute-start | bytes 331784 | tf_op jit(solution)/shard_map/ppermute | solution.py:401
  46.8 1.1 %collective-permute-start.22 = (bf16[432,128]{1,0:T(8,128)(2,1)S(1)}, bf16[432,128]{1,0:T(8,128)(2,1)S(1)}, u32[]{:S(2)}, u32[]{:S(2)}) collective-permute-start(bf16[432,128]{1,0:T(8,128)(2,1)S(1)} %shard_map.91.refs_0_), channel_id=1, source_target_pairs={{0,2},{1,3},{2,0},{3,1},{4,6},{5,7},{6,4},{7,5},{8,10},{9,11},{10,... | collective-permute-start | bytes 331784 | tf_op jit(solution)/shard_map/ppermute | solution.py:401
  47.9 0.0 collective-permute-done.13.two
  47.9 2.4 %collective-permute-start.14 = (bf16[432,128]{1,0:T(8,128)(2,1)S(1)}, bf16[432,128]{1,0:T(8,128)(2,1)S(1)}, u32[]{:S(2)}, u32[]{:S(2)}) collective-permute-start(bf16[432,128]{1,0:T(8,128)(2,1)S(1)} %shard_map.87.refs_0_), channel_id=1, source_target_pairs={{0,5},{1,4},{2,7},{3,6},{4,1},{5,0},{6,3},{7,2},{8,13},{9,12},{10,... | collective-permute-start | bytes 331784 | tf_op jit(solution)/shard_map/ppermute | solution.py:401
  50.4 0.1 collective-permute-start.15
  50.5 0.0 collective-permute-done.20.refs_1_
  50.5 1.0 %collective-permute-start.16 = (bf16[432,128]{1,0:T(8,128)(2,1)S(1)}, bf16[432,128]{1,0:T(8,128)(2,1)S(1)}, u32[]{:S(2)}, u32[]{:S(2)}) collective-permute-start(bf16[432,128]{1,0:T(8,128)(2,1)S(1)} %shard_map.87.refs_0_), channel_id=1, source_target_pairs={{0,1},{1,0},{2,3},{3,2},{4,5},{5,4},{6,7},{7,6},{8,9},{9,8},{10,11... | collective-permute-start | bytes 331784 | tf_op jit(solution)/shard_map/ppermute | solution.py:401
  51.5 0.0 collective-permute-done.21.refs_2_
  51.5 1.2 %collective-permute-done.22.refs_3_ = bf16[432,128]{1,0:T(8,128)(2,1)S(1)} collective-permute-done((bf16[432,128]{1,0:T(8,128)(2,1)S(1)}, bf16[432,128]{1,0:T(8,128)(2,1)S(1)}, u32[]{:S(2)}, u32[]{:S(2)}) %collective-permute-start.22) | collective-permute-done | bytes 110624 | tf_op jit(solution)/shard_map/ppermute | solution.py:401
  52.7 0.1 collective-permute-start.23
  52.8 0.8 %collective-permute-done.14.refs_1_ = bf16[432,128]{1,0:T(8,128)(2,1)S(1)} collective-permute-done((bf16[432,128]{1,0:T(8,128)(2,1)S(1)}, bf16[432,128]{1,0:T(8,128)(2,1)S(1)}, u32[]{:S(2)}, u32[]{:S(2)}) %collective-permute-start.14) | collective-permute-done | bytes 110624 | tf_op jit(solution)/shard_map/ppermute | solution.py:401
  53.6 1.5 %collective-permute-done.15.refs_2_ = bf16[432,128]{1,0:T(8,128)(2,1)S(1)} collective-permute-done((bf16[432,128]{1,0:T(8,128)(2,1)S(1)}, bf16[432,128]{1,0:T(8,128)(2,1)S(1)}, u32[]{:S(2)}, u32[]{:S(2)}) %collective-permute-start.15) | collective-permute-done | bytes 110624 | tf_op jit(solution)/shard_map/ppermute | solution.py:401
  55.1 0.1 collective-permute-done.16.refs_3_
  55.2 0.1 shard_map.88.own
  55.3 0.1 collective-permute-start.17
  55.3 1.5 %shard_map.94 = bf16[512,128]{1,0:T(8,128)(2,1)} custom-call(bf16[512,1152]{1,0:T(8,128)(2,1)S(1)} %get-tuple-element.71.st_own, bf16[512,128]{1,0:T(8,128)(2,1)S(1)} %get-tuple-element.41.grads, bf16[48,128]{1,0:T(8,128)(2,1)S(1)} %get-tuple-element.50.marks3, bf16[384,1152]{1,0:T(8,128)(2,1)S(1)} %get-tuple-element.72.w1_wide), custom_call_target="tpu_custom_call" | custom-call | flops 452984832 | bytes 2338816 | tf_op jit(solution)/shard_map/pallas_call | solution.py:35
  56.8 0.0 collective-permute-done.23.other
  56.8 1.3 %shard_map.93 = f32[3456,128]{1,0:T(8,128)} custom-call(bf16[1728,128]{1,0:T(8,128)(2,1)S(1)} %shard_map.92.own, bf16[1728,128]{1,0:T(8,128)(2,1)S(1)} %collective-permute-done.23.other), custom_call_target="tpu_custom_call" | custom-call | bytes 2654208 | tf_op jit(solution)/shard_map/pallas_call | solution.py:35
  58.2 0.0 collective-permute-done.17.other
  58.2 1.3 %shard_map.89 = f32[3456,128]{1,0:T(8,128)} custom-call(bf16[1728,128]{1,0:T(8,128)(2,1)S(1)} %shard_map.88.own, bf16[1728,128]{1,0:T(8,128)(2,1)S(1)} %collective-permute-done.17.other), custom_call_target="tpu_custom_call" | custom-call | bytes 2654208 | tf_op jit(solution)/shard_map/pallas_call | solution.py:35
  (5 shorter events, 0.2 us)
Async XLA Ops:
  2.4 8.6 %collective-permute-start = (bf16[272,128]{1,0:T(8,128)(2,1)S(1)}, bf16[272,128]{1,0:T(8,128)(2,1)S(1)}, u32[]{:S(2)}, u32[]{:S(2)}) collective-permute-start(bf16[272,128]{1,0:T(8,128)(2,1)S(1)} %get-tuple-element.43), channel_id=1, source_target_pairs={{1,2},{2,1},{5,6},{6,5},{9,10},{10,9},{13,14},{14,13},{17,18},{18,... | collective-permute-start | bytes 208904 | tf_op jit(solution)/shard_map/ppermute | solution.py:633
  3.1 9.0 %collective-permute-start.1 = (bf16[272,128]{1,0:T(8,128)(2,1)S(1)}, bf16[272,128]{1,0:T(8,128)(2,1)S(1)}, u32[]{:S(2)}, u32[]{:S(2)}) collective-permute-start(bf16[272,128]{1,0:T(8,128)(2,1)S(1)} %get-tuple-element.44), channel_id=1, source_target_pairs={{0,1},{1,0},{2,3},{3,2},{4,5},{5,4},{6,7},{7,6},{8,9},{9,8},{10,11... | collective-permute-start | bytes 208904 | tf_op jit(solution)/shard_map/ppermute | solution.py:633
  12.2 7.2 %collective-permute-start.2 = (bf16[400,128]{1,0:T(8,128)(2,1)S(1)}, bf16[400,128]{1,0:T(8,128)(2,1)S(1)}, u32[]{:S(2)}, u32[]{:S(2)}) collective-permute-start(bf16[400,128]{1,0:T(8,128)(2,1)S(1)} %get-tuple-element.51), channel_id=1, source_target_pairs={{4,8},{8,4},{5,9},{9,5},{6,10},{10,6},{7,11},{11,7},{20,24},{24,20... | collective-permute-start | bytes 307208 | tf_op jit(solution)/shard_map/ppermute | solution.py:633
  12.9 7.1 %collective-permute-start.3 = (bf16[400,128]{1,0:T(8,128)(2,1)S(1)}, bf16[400,128]{1,0:T(8,128)(2,1)S(1)}, u32[]{:S(2)}, u32[]{:S(2)}) collective-permute-start(bf16[400,128]{1,0:T(8,128)(2,1)S(1)} %get-tuple-element.52), channel_id=1, source_target_pairs={{0,4},{4,0},{1,5},{5,1},{2,6},{6,2},{3,7},{7,3},{8,12},{12,8},{9,1... | collective-permute-start | bytes 307208 | tf_op jit(solution)/shard_map/ppermute | solution.py:633
  21.9 2.5 %collective-permute-start.5 = (f32[64,3456]{1,0:T(8,128)S(1)}, f32[64,3456]{1,0:T(8,128)S(1)}, u32[]{:S(2)}, u32[]{:S(2)}) collective-permute-start(f32[64,3456]{1,0:T(8,128)S(1)} %get-tuple-element.61), channel_id=1, source_target_pairs={{0,16},{16,0},{1,17},{17,1},{2,18},{18,2},{3,19},{19,3},{4,20},{20... | collective-permute-start | bytes 2654216 | tf_op jit(solution)/shard_map/ppermute | solution.py:391
  23.7 4.3 %collective-permute-start.4 = (f32[64,3456]{1,0:T(8,128)S(1)}, f32[64,3456]{1,0:T(8,128)S(1)}, u32[]{:S(2)}, u32[]{:S(2)}) collective-permute-start(f32[64,3456]{1,0:T(8,128)S(1)} %get-tuple-element.58), channel_id=1, source_target_pairs={{0,16},{16,0},{1,17},{17,1},{2,18},{18,2},{3,19},{19,3},{4,20},{20... | collective-permute-start | bytes 2654216 | tf_op jit(solution)/shard_map/ppermute | solution.py:391
  24.5 6.9 %collective-permute-start.6 = (bf16[16,3456]{1,0:T(8,128)(2,1)S(1)}, bf16[16,3456]{1,0:T(8,128)(2,1)S(1)}, u32[]{:S(2)}, u32[]{:S(2)}) collective-permute-start(bf16[16,3456]{1,0:T(8,128)(2,1)S(1)} %get-tuple-element.63), channel_id=1, source_target_pairs={{0,3},{1,2},{2,1},{3,0},{4,7},{5,6},{6,5},{7,4},{8,11},{9,10},{10,... | collective-permute-start | bytes 331784 | tf_op jit(solution)/shard_map/ppermute | solution.py:401
  26.0 6.4 %collective-permute-start.7 = (bf16[16,3456]{1,0:T(8,128)(2,1)S(1)}, bf16[16,3456]{1,0:T(8,128)(2,1)S(1)}, u32[]{:S(2)}, u32[]{:S(2)}) collective-permute-start(bf16[16,3456]{1,0:T(8,128)(2,1)S(1)} %get-tuple-element.64), channel_id=1, source_target_pairs={{0,1},{1,0},{2,3},{3,2},{4,5},{5,4},{6,7},{7,6},{8,9},{9,8},{10,11... | collective-permute-start | bytes 331784 | tf_op jit(solution)/shard_map/ppermute | solution.py:401
  27.0 6.4 %collective-permute-start.8 = (bf16[16,3456]{1,0:T(8,128)(2,1)S(1)}, bf16[16,3456]{1,0:T(8,128)(2,1)S(1)}, u32[]{:S(2)}, u32[]{:S(2)}) collective-permute-start(bf16[16,3456]{1,0:T(8,128)(2,1)S(1)} %get-tuple-element.65), channel_id=1, source_target_pairs={{0,2},{1,3},{2,0},{3,1},{4,6},{5,7},{6,4},{7,5},{8,10},{9,11},{10,... | collective-permute-start | bytes 331784 | tf_op jit(solution)/shard_map/ppermute | solution.py:401
  28.1 7.4 %collective-permute-start.10 = (bf16[16,3456]{1,0:T(8,128)(2,1)S(1)}, bf16[16,3456]{1,0:T(8,128)(2,1)S(1)}, u32[]{:S(2)}, u32[]{:S(2)}) collective-permute-start(bf16[16,3456]{1,0:T(8,128)(2,1)S(1)} %get-tuple-element.68), channel_id=1, source_target_pairs={{0,5},{1,4},{2,7},{3,6},{4,1},{5,0},{6,3},{7,2},{8,13},{9,12},{10,... | collective-permute-start | bytes 331784 | tf_op jit(solution)/shard_map/ppermute | solution.py:401
  30.6 5.2 %collective-permute-start.11 = (bf16[16,3456]{1,0:T(8,128)(2,1)S(1)}, bf16[16,3456]{1,0:T(8,128)(2,1)S(1)}, u32[]{:S(2)}, u32[]{:S(2)}) collective-permute-start(bf16[16,3456]{1,0:T(8,128)(2,1)S(1)} %get-tuple-element.69), channel_id=1, source_target_pairs={{0,4},{1,5},{2,6},{3,7},{4,0},{5,1},{6,2},{7,3},{8,12},{9,13},{10,... | collective-permute-start | bytes 331784 | tf_op jit(solution)/shard_map/ppermute | solution.py:401
  31.3 4.7 %collective-permute-start.9 = (bf16[16,3456]{1,0:T(8,128)(2,1)S(1)}, bf16[16,3456]{1,0:T(8,128)(2,1)S(1)}, u32[]{:S(2)}, u32[]{:S(2)}) collective-permute-start(bf16[16,3456]{1,0:T(8,128)(2,1)S(1)} %get-tuple-element.67), channel_id=1, source_target_pairs={{0,1},{1,0},{2,3},{3,2},{4,5},{5,4},{6,7},{7,6},{8,9},{9,8},{10,11... | collective-permute-start | bytes 331784 | tf_op jit(solution)/shard_map/ppermute | solution.py:401
  33.4 5.1 %collective-permute-start.18 = (bf16[16,3456]{1,0:T(8,128)(2,1)S(1)}, bf16[16,3456]{1,0:T(8,128)(2,1)S(1)}, u32[]{:S(2)}, u32[]{:S(2)}) collective-permute-start(bf16[16,3456]{1,0:T(8,128)(2,1)S(1)} %shard_map.84.one), channel_id=1, source_target_pairs={{0,4},{1,5},{2,6},{3,7},{4,0},{5,1},{6,2},{7,3},{8,12},{9,13},{10,... | collective-permute-start | bytes 331784 | tf_op jit(solution)/shard_map/ppermute | solution.py:401
  36.1 4.8 %collective-permute-start.12 = (bf16[16,3456]{1,0:T(8,128)(2,1)S(1)}, bf16[16,3456]{1,0:T(8,128)(2,1)S(1)}, u32[]{:S(2)}, u32[]{:S(2)}) collective-permute-start(bf16[16,3456]{1,0:T(8,128)(2,1)S(1)} %shard_map.85.one), channel_id=1, source_target_pairs={{0,2},{1,3},{2,0},{3,1},{4,6},{5,7},{6,4},{7,5},{8,10},{9,11},{10,... | collective-permute-start | bytes 331784 | tf_op jit(solution)/shard_map/ppermute | solution.py:401
  38.6 5.7 %collective-permute-start.19 = (bf16[16,3456]{1,0:T(8,128)(2,1)S(1)}, bf16[16,3456]{1,0:T(8,128)(2,1)S(1)}, u32[]{:S(2)}, u32[]{:S(2)}) collective-permute-start(bf16[16,3456]{1,0:T(8,128)(2,1)S(1)} %shard_map.90.one), channel_id=1, source_target_pairs={{0,8},{1,9},{2,10},{3,11},{4,12},{5,13},{6,14},{7,15},{8,0},{9,1},... | collective-permute-start | bytes 331784 | tf_op jit(solution)/shard_map/ppermute | solution.py:401
  41.0 6.9 %collective-permute-start.13 = (bf16[16,3456]{1,0:T(8,128)(2,1)S(1)}, bf16[16,3456]{1,0:T(8,128)(2,1)S(1)}, u32[]{:S(2)}, u32[]{:S(2)}) collective-permute-start(bf16[16,3456]{1,0:T(8,128)(2,1)S(1)} %shard_map.86.one), channel_id=1, source_target_pairs={{0,8},{1,9},{2,10},{3,11},{4,12},{5,13},{6,14},{7,15},{8,0},{9,1},... | collective-permute-start | bytes 331784 | tf_op jit(solution)/shard_map/ppermute | solution.py:401
  44.3 6.1 %collective-permute-start.20 = (bf16[432,128]{1,0:T(8,128)(2,1)S(1)}, bf16[432,128]{1,0:T(8,128)(2,1)S(1)}, u32[]{:S(2)}, u32[]{:S(2)}) collective-permute-start(bf16[432,128]{1,0:T(8,128)(2,1)S(1)} %shard_map.91.refs_0_), channel_id=1, source_target_pairs={{0,3},{1,2},{2,1},{3,0},{4,7},{5,6},{6,5},{7,4},{8,11},{9,10},{10,... | collective-permute-start | bytes 331784 | tf_op jit(solution)/shard_map/ppermute | solution.py:401
  45.8 5.7 %collective-permute-start.21 = (bf16[432,128]{1,0:T(8,128)(2,1)S(1)}, bf16[432,128]{1,0:T(8,128)(2,1)S(1)}, u32[]{:S(2)}, u32[]{:S(2)}) collective-permute-start(bf16[432,128]{1,0:T(8,128)(2,1)S(1)} %shard_map.91.refs_0_), channel_id=1, source_target_pairs={{0,1},{1,0},{2,3},{3,2},{4,5},{5,4},{6,7},{7,6},{8,9},{9,8},{10,11... | collective-permute-start | bytes 331784 | tf_op jit(solution)/shard_map/ppermute | solution.py:401
  46.8 5.9 %collective-permute-start.22 = (bf16[432,128]{1,0:T(8,128)(2,1)S(1)}, bf16[432,128]{1,0:T(8,128)(2,1)S(1)}, u32[]{:S(2)}, u32[]{:S(2)}) collective-permute-start(bf16[432,128]{1,0:T(8,128)(2,1)S(1)} %shard_map.91.refs_0_), channel_id=1, source_target_pairs={{0,2},{1,3},{2,0},{3,1},{4,6},{5,7},{6,4},{7,5},{8,10},{9,11},{10,... | collective-permute-start | bytes 331784 | tf_op jit(solution)/shard_map/ppermute | solution.py:401
  47.9 5.7 %collective-permute-start.14 = (bf16[432,128]{1,0:T(8,128)(2,1)S(1)}, bf16[432,128]{1,0:T(8,128)(2,1)S(1)}, u32[]{:S(2)}, u32[]{:S(2)}) collective-permute-start(bf16[432,128]{1,0:T(8,128)(2,1)S(1)} %shard_map.87.refs_0_), channel_id=1, source_target_pairs={{0,5},{1,4},{2,7},{3,6},{4,1},{5,0},{6,3},{7,2},{8,13},{9,12},{10,... | collective-permute-start | bytes 331784 | tf_op jit(solution)/shard_map/ppermute | solution.py:401
  50.4 4.7 %collective-permute-start.15 = (bf16[432,128]{1,0:T(8,128)(2,1)S(1)}, bf16[432,128]{1,0:T(8,128)(2,1)S(1)}, u32[]{:S(2)}, u32[]{:S(2)}) collective-permute-start(bf16[432,128]{1,0:T(8,128)(2,1)S(1)} %shard_map.87.refs_0_), channel_id=1, source_target_pairs={{0,4},{1,5},{2,6},{3,7},{4,0},{5,1},{6,2},{7,3},{8,12},{9,13},{10,... | collective-permute-start | bytes 331784 | tf_op jit(solution)/shard_map/ppermute | solution.py:401
  50.5 4.7 %collective-permute-start.16 = (bf16[432,128]{1,0:T(8,128)(2,1)S(1)}, bf16[432,128]{1,0:T(8,128)(2,1)S(1)}, u32[]{:S(2)}, u32[]{:S(2)}) collective-permute-start(bf16[432,128]{1,0:T(8,128)(2,1)S(1)} %shard_map.87.refs_0_), channel_id=1, source_target_pairs={{0,1},{1,0},{2,3},{3,2},{4,5},{5,4},{6,7},{7,6},{8,9},{9,8},{10,11... | collective-permute-start | bytes 331784 | tf_op jit(solution)/shard_map/ppermute | solution.py:401
  52.7 4.1 %collective-permute-start.23 = (bf16[1728,128]{1,0:T(8,128)(2,1)S(1)}, bf16[1728,128]{1,0:T(8,128)(2,1)S(1)}, u32[]{:S(2)}, u32[]{:S(2)}) collective-permute-start(bf16[1728,128]{1,0:T(8,128)(2,1)S(1)} %shard_map.92.own), channel_id=1, source_target_pairs={{0,16},{16,0},{1,17},{17,1},{2,18},{18,2},{3,19},{19,3},{4,20},{20... | collective-permute-start | bytes 1327112 | tf_op jit(solution)/shard_map/ppermute | solution.py:391
  55.3 2.9 %collective-permute-start.17 = (bf16[1728,128]{1,0:T(8,128)(2,1)S(1)}, bf16[1728,128]{1,0:T(8,128)(2,1)S(1)}, u32[]{:S(2)}, u32[]{:S(2)}) collective-permute-start(bf16[1728,128]{1,0:T(8,128)(2,1)S(1)} %shard_map.88.own), channel_id=1, source_target_pairs={{0,16},{16,0},{1,17},{17,1},{2,18},{18,2},{3,19},{19,3},{4,20},{20... | collective-permute-start | bytes 1327112 | tf_op jit(solution)/shard_map/ppermute | solution.py:391
